TPU v7x, 32 devices: a whole 2x2x4 slice. The times are simulated.
32 devices in a mesh: feat: 16 (over z, y, core), width: 2 (over x).
Axes of the slice: x: 2, y: 2, z: 4, core: 2. Of those that a mesh axis runs over, the one named last changes fastest.
Arguments:
- residual: bfloat16 [2, 448, 3584], P(None, None, 'width'), may hold values from -6 to 6
- targets: bfloat16 [2, 448, 3584], P(None, None, 'width'), may hold values from -6 to 6
- encoder: bfloat16 [3584, 32768], P('width', 'feat'), may hold values from -0.09375 to 0.09375
- biases: bfloat16 [32768], P('feat'), may hold values from -3 to 3
- same_decoder: bfloat16 [32768, 3584], P('feat', 'width'), may hold values from -0.03125 to 0.03125
- next_decoder: bfloat16 [16384, 3584], P('feat', 'width'), may hold values from -0.03125 to 0.03125
- encoder_first: bfloat16 [3584, 32768], P('width', 'feat'), may hold values from -24 to 24
- encoder_second: bfloat16 [3584, 32768], P('width', 'feat'), may hold values from 4 to 64
- biases_first: bfloat16 [32768], P('feat'), may hold values from -24 to 24
- biases_second: bfloat16 [32768], P('feat'), may hold values from 4 to 64
- same_first: bfloat16 [32768, 3584], P('feat', 'width'), may hold values from -24 to 24
- same_second: bfloat16 [32768, 3584], P('feat', 'width'), may hold values from 4 to 64
- next_first: bfloat16 [16384, 3584], P('feat', 'width'), may hold values from -24 to 24
- next_second: bfloat16 [16384, 3584], P('feat', 'width'), may hold values from 4 to 64
Outputs:
- updated_encoder: bfloat16 [3584, 32768], P('width', 'feat')
- updated_biases: bfloat16 [32768], P('feat')
- updated_same: bfloat16 [32768, 3584], P('feat', 'width')
- updated_next: bfloat16 [16384, 3584], P('feat', 'width')
- encoder_moment: bfloat16 [3584, 32768], P('width', 'feat')
- encoder_square: bfloat16 [3584, 32768], P('width', 'feat')
- biases_moment: bfloat16 [32768], P('feat')
- biases_square: bfloat16 [32768], P('feat')
- same_moment: bfloat16 [32768, 3584], P('feat', 'width')
- same_square: bfloat16 [32768, 3584], P('feat', 'width')
- next_moment: bfloat16 [16384, 3584], P('feat', 'width')
- next_square: bfloat16 [16384, 3584], P('feat', 'width')
All inputs are finite; a program needn't handle non-finite values.
Results may differ from a plain program's by a relative error of at most 0.0055.
Values may be sent and summed in bfloat16 or wider, within the bound.
No kernel may reach another device: no remote copies, remote signals or barrier semaphores. Data moves between devices by JAX's collectives and lax.ppermute only.
A program may use at most 256 MiB of HBM per device.

v0:
```python
import functools
import math
import jax
import jax.numpy as jnp
from jax import lax
from jax.experimental import pallas as pl
from jax.experimental.pallas import tpu as pltpu
from jax.sharding import PartitionSpec as P

STEPS = 100


beta_one = 0.9
beta_two = 0.999
learn_rate = 0.002
adam_eps = 1e-08
weight_decay = 0.1


def adamw_update(parameter, first, second, gradient, decay_rate):
    first_new = beta_one * first.astype(jnp.float32) + (1.0 - beta_one) * gradient
    second_new = beta_two * second.astype(jnp.float32) + (1.0 - beta_two) * gradient * gradient
    first_hat = first_new / (1.0 - beta_one**STEPS)
    second_hat = second_new / (1.0 - beta_two**STEPS)
    weight = parameter.astype(jnp.float32)
    updated = weight - learn_rate * (
        first_hat / (jnp.sqrt(second_hat) + adam_eps) + decay_rate * weight
    )
    return (
        updated.astype(jnp.bfloat16),
        first_new.astype(jnp.bfloat16),
        second_new.astype(jnp.bfloat16),
    )


def adamw_kernel(decay_rate, tile, *refs):
    left_ref, right_ref, weight_ref, first_ref, second_ref = refs[:5]
    updated_ref, moment_ref, square_ref = refs[5:]
    first_scale, second_scale = 1.0 - beta_one**STEPS, 1.0 - beta_two**STEPS
    keep = 1.0 - learn_rate * decay_rate
    rate = learn_rate * math.sqrt(second_scale) / first_scale
    shift = adam_eps * math.sqrt(second_scale)
    left = left_ref[...]
    for start in range(0, weight_ref.shape[1], tile):
        columns = slice(start, start + tile)
        gradient = over_rows(left, right_ref[:, columns])
        scaled = (1.0 - beta_one) * gradient
        first_new = beta_one * first_ref[:, columns].astype(jnp.float32) + scaled
        second_new = (
            beta_two * second_ref[:, columns].astype(jnp.float32)
            + ((1.0 - beta_two) * gradient) * gradient
        )
        root = second_new * lax.rsqrt(second_new)
        step = (rate * first_new) * pl.reciprocal(root + shift, approx=True)
        updated = keep * weight_ref[:, columns].astype(jnp.float32) - step
        updated_ref[:, columns] = updated.astype(jnp.bfloat16)
        moment_ref[:, columns] = first_new.astype(jnp.bfloat16)
        square_ref[:, columns] = second_new.astype(jnp.bfloat16)


def adamw_matmul(left, right, weight, first, second, decay_rate):
    tokens = left.shape[0]
    rows, width = weight.shape
    block = math.gcd(rows, 256)
    tile = math.gcd(width, 256)
    whole = pl.BlockSpec((tokens, width), lambda place: (0, 0))
    strip = pl.BlockSpec((block, width), lambda place: (place, 0))
    return pl.pallas_call(
        functools.partial(adamw_kernel, decay_rate, tile),
        grid=(rows // block,),
        in_specs=[
            pl.BlockSpec((tokens, block), lambda place: (0, place)),
            whole,
            strip,
            strip,
            strip,
        ],
        out_specs=[strip] * 3,
        out_shape=[jax.ShapeDtypeStruct((rows, width), jnp.bfloat16)] * 3,
        compiler_params=pltpu.CompilerParams(vmem_limit_bytes=40 * 2**20),
        cost_estimate=pl.CostEstimate(
            flops=2 * tokens * rows * width,
            bytes_accessed=12 * rows * width,
            transcendentals=2 * rows * width,
        ),
    )(left, right, weight, first, second)


def matmul(left, right):
    return jnp.dot(left, right, preferred_element_type=jnp.float32)


def over_rows(left, right):
    return lax.dot_general(
        left, right, (((0,), (0,)), ((), ())), preferred_element_type=jnp.float32
    )


def over_cols(left, right):
    return lax.dot_general(
        left, right, (((1,), (1,)), ((), ())), preferred_element_type=jnp.float32
    )


def across(value):
    return lax.ppermute(value, "width", [(0, 1), (1, 0)])


def flipped(value, bit, members):
    step = 1 << bit
    return lax.ppermute(value, "feat", [(index, index ^ step) for index in range(members)])


def halves(value, axis):
    size = value.shape[axis] // 2
    return lax.slice_in_dim(value, 0, size, axis=axis), lax.slice_in_dim(
        value, size, 2 * size, axis=axis
    )


def scatter_step(total, bit, axis, members):
    upper = ((lax.axis_index("feat") >> bit) & 1) == 1
    low, high = halves(total, axis)
    leaving = jnp.where(upper, low, high).astype(jnp.bfloat16)
    keeping = jnp.where(upper, high, low)
    return keeping + flipped(leaving, bit, members).astype(jnp.float32)


def gather_step(value, bit, axis, members):
    upper = ((lax.axis_index("feat") >> bit) & 1) == 1
    other = flipped(value, bit, members)
    return jnp.concatenate(
        [jnp.where(upper, other, value), jnp.where(upper, value, other)], axis=axis
    )


def shard_of(target, plan, width_index):
    index = lax.axis_index("feat")
    starts, sizes = [0, 0], list(target.shape)
    for bit, axis in plan:
        sizes[axis] //= 2
        starts[axis] = starts[axis] + ((index >> bit) & 1) * sizes[axis]
    tokens = target.shape[0]
    starts[0] = lax.rem(starts[0] + width_index * (tokens // 2), tokens)
    return lax.dynamic_slice(target, starts, sizes)


def local(
    residual,
    targets,
    encoder,
    biases,
    same_decoder,
    next_decoder,
    encoder_first,
    encoder_second,
    biases_first,
    biases_second,
    same_first,
    same_second,
    next_first,
    next_second,
):
    feat_count = lax.axis_size("feat")
    feat_index = lax.axis_index("feat")
    width_index = lax.axis_index("width")
    half_count = feat_count // 2
    source_layer = feat_index // half_count
    leading = source_layer == 0
    tokens, width = residual.shape[1:]
    part = tokens // 2
    half = encoder.shape[1] // 2

    mine = lax.dynamic_slice(
        residual, (source_layer, width_index * part, 0), (1, part, width)
    )[0]
    theirs = lax.dynamic_slice(
        residual, (source_layer, (1 - width_index) * part, 0), (1, part, width)
    )[0]
    bias = biases.astype(jnp.float32)

    def preact_of(block, bias_block):
        leaving = matmul(theirs, block).astype(jnp.float16)
        arriving = across(leaving)
        return matmul(mine, block) + arriving.astype(jnp.float32) + bias_block

    pre_b = preact_of(encoder[:, half:], bias[half:])
    pre_a = preact_of(encoder[:, :half], bias[:half])
    act_b = jnp.maximum(pre_b, 0.0).astype(jnp.bfloat16)
    act_a = jnp.maximum(pre_a, 0.0).astype(jnp.bfloat16)
    sent = lax.ppermute(
        act_b, "feat", [(index, index + half_count) for index in range(half_count)]
    )
    trailing_pairs = [
        (2 * index + side, 2 * index + 1 - side)
        for index in range(half_count, feat_count)
        for side in range(2)
    ]
    full_b = jnp.concatenate([act_b, across(act_b)], axis=0)
    full_a = jnp.concatenate([act_a, across(act_a)], axis=0)
    sent_full = jnp.concatenate(
        [sent, lax.ppermute(sent, ("feat", "width"), trailing_pairs)], axis=0
    )
    active = jnp.concatenate([full_a, full_b], axis=1)
    cross_input = jnp.where(leading, full_a, sent_full)

    own_term = matmul(active, same_decoder)
    cross_term = matmul(cross_input, next_decoder)
    second_part = jnp.where(leading, cross_term, own_term + cross_term)

    bits = feat_count.bit_length() - 1
    second_plan = [(bit, 1 if bit == 2 else 0) for bit in range(bits)]
    first_order = [0, 2, 1] + list(range(3, bits - 1))
    first_plan = [(bit, 1 if place == 2 else 0) for place, bit in enumerate(first_order)]
    first_sum, second_sum = own_term, second_part
    for bit, axis in second_plan:
        second_sum = scatter_step(second_sum, bit, axis, feat_count)
    for bit, axis in first_plan:
        first_sum = scatter_step(first_sum, bit, axis, half_count)
    delta_first = (
        first_sum - shard_of(targets[0], first_plan, width_index).astype(jnp.float32)
    ).astype(jnp.bfloat16)
    delta_next = (
        second_sum - shard_of(targets[1], second_plan, width_index).astype(jnp.float32)
    ).astype(jnp.bfloat16)
    for bit, axis in reversed(second_plan):
        delta_next = gather_step(delta_next, bit, axis, feat_count)
    for bit, axis in reversed(first_plan):
        delta_first = gather_step(delta_first, bit, axis, half_count)
    delta_own = jnp.where(leading, delta_first, delta_next)

    cross_back = over_cols(delta_next, next_decoder)
    cross_arriving = lax.ppermute(
        cross_back[part:].astype(jnp.bfloat16), ("feat", "width"), trailing_pairs
    )
    cross_sum = (cross_back[:part] + cross_arriving.astype(jnp.float32)).astype(jnp.bfloat16)
    returned = lax.ppermute(
        cross_sum, "feat", [(index + half_count, index) for index in range(half_count)]
    ).astype(jnp.float32)
    back_a = over_cols(delta_own, same_decoder[:half]) + jnp.where(leading, cross_back, 0.0)
    back_b = over_cols(delta_own, same_decoder[half:])

    def preact_grad_of(back, pre, extra):
        arriving = across(back[part:].astype(jnp.bfloat16)).astype(jnp.float32)
        total = back[:part] + arriving
        if extra is not None:
            total = total + extra
        return jnp.where(pre > 0.0, total, 0.0).astype(jnp.bfloat16)

    grad_a = preact_grad_of(back_a, pre_a, None)
    grad_b = preact_grad_of(back_b, pre_b, returned)
    grad_mine = jnp.concatenate([grad_a, grad_b], axis=1)
    grad_theirs = jnp.concatenate([across(grad_a), across(grad_b)], axis=1)
    grad_sum = jnp.sum(grad_mine.astype(jnp.float32), axis=0)
    grad_biases = grad_sum + across(grad_sum)

    updated_same, same_moment, same_square = adamw_matmul(
        active, delta_own, same_decoder, same_first, same_second, weight_decay
    )
    updated_next, next_moment, next_square = adamw_matmul(
        cross_input, delta_next, next_decoder, next_first, next_second, weight_decay
    )
    updated_encoder, encoder_moment, encoder_square = adamw_matmul(
        jnp.concatenate([mine, theirs], axis=0),
        jnp.concatenate([grad_mine, grad_theirs], axis=0),
        encoder,
        encoder_first,
        encoder_second,
        weight_decay,
    )
    updated_biases, biases_moment, biases_square = adamw_update(
        biases, biases_first, biases_second, grad_biases, 0.0
    )
    return (
        updated_encoder,
        updated_biases,
        updated_same,
        updated_next,
        encoder_moment,
        encoder_square,
        biases_moment,
        biases_square,
        same_moment,
        same_square,
        next_moment,
        next_square,
    )


def solution(mesh):
    in_specs = (
        P(None, None, "width"),
        P(None, None, "width"),
        P("width", "feat"),
        P("feat"),
        P("feat", "width"),
        P("feat", "width"),
        P("width", "feat"),
        P("width", "feat"),
        P("feat"),
        P("feat"),
        P("feat", "width"),
        P("feat", "width"),
        P("feat", "width"),
        P("feat", "width"),
    )
    out_specs = (
        P("width", "feat"),
        P("feat"),
        P("feat", "width"),
        P("feat", "width"),
        P("width", "feat"),
        P("width", "feat"),
        P("feat"),
        P("feat"),
        P("feat", "width"),
        P("feat", "width"),
        P("feat", "width"),
        P("feat", "width"),
    )
    return jax.shard_map(local, mesh=mesh, in_specs=in_specs, out_specs=out_specs, check_vma=False)
```

profile of v0, /device:TPU:0, one launch (start us, length us, event | category | flops | bytes accessed | tf_op | source)
XLA Modules:
  0.0 218.5 jit_solution(7304336433865763099)
XLA Ops:
  0.7 1.6 dynamic-slice_bitcast_fusion.1
  2.4 3.9 %fusion.17 = f16[224,1024]{1,0:T(8,128)(2,1)S(1)} fusion(bf16[224,1792]{1,0:T(8,128)(2,1)S(1)} %get-tuple-element.33, bf16[1792,2048]{1,0:T(8,128)(2,1)} %refs_2_.3), kind=kOutput, calls=%fused_computation.25 | convolution fusion | flops 822312960 | bytes 4931584 | tf_op jit(solution)/shard_map/dot_general | solution.py:90
  6.3 3.0 %collective-permute-start.2 = (f16[224,1024]{1,0:T(8,128)(2,1)S(1)}, f16[224,1024]{1,0:T(8,128)(2,1)S(1)}, u32[]{:S(2)}, u32[]{:S(2)}) collective-permute-start(f16[224,1024]{1,0:T(8,128)(2,1)S(1)} %fusion.17), channel_id=1, source_target_pairs={{0,1},{1,0},{2,3},{3,2},{4,5},{5,4},{6,7},{7,6},{8,9},{9,8},{10,11... | collective-permute-start | bytes 1376264 | tf_op jit(solution)/shard_map/ppermute | solution.py:106
  9.3 1.0 fusion.14
  10.5 10.2 %collective-permute-done.2 = f16[224,1024]{1,0:T(8,128)(2,1)S(1)} collective-permute-done((f16[224,1024]{1,0:T(8,128)(2,1)S(1)}, f16[224,1024]{1,0:T(8,128)(2,1)S(1)}, u32[]{:S(2)}, u32[]{:S(2)}) %collective-permute-start.2) | collective-permute-done | bytes 458784 | tf_op jit(solution)/shard_map/ppermute | solution.py:106
  20.7 3.3 %maximum_convert_fusion = (bf16[224,1024]{1,0:T(8,128)(2,1)S(1)}, f32[224,1024]{1,0:T(8,128)S(1)}) fusion(f16[224,1024]{1,0:T(8,128)(2,1)S(1)} %collective-permute-done.2, f32[1024]{0:T(1024)S(1)} %get-tuple-element.54, bf16[224,1792]{1,0:T(8,128)(2,1)S(1)} %get-tuple-element.32, bf16[1792,2048]{1,0:T(8,128)(2,1)} %refs_2_.3), kind=kOutput, calls=%fused_computation.39 | convolution fusion | flops 823230464 | bytes 6311936 | tf_op jit(solution)/shard_map/dot_general | solution.py:90
  24.0 2.1 collective-permute-start.3
  26.1 4.5 %collective-permute-start.10 = (bf16[224,1024]{1,0:T(8,128)(2,1)S(1)}, bf16[224,1024]{1,0:T(8,128)(2,1)S(1)}, u32[]{:S(2)}, u32[]{:S(2)}) collective-permute-start(bf16[224,1024]{1,0:T(8,128)(2,1)S(1)} %get-tuple-element.57), channel_id=1, source_target_pairs={{0,16},{2,18},{4,20},{6,22},{8,24},{10,26},{12,28},{14,30},{1,17},... | collective-permute-start | bytes 1376264 | tf_op jit(solution)/shard_map/ppermute | solution.py:191
  30.7 3.3 %maximum_convert_fusion.1 = (bf16[224,1024]{1,0:T(8,128)(2,1)S(1)}, f32[224,1024]{1,0:T(8,128)S(1)}) fusion(f16[224,1024]{1,0:T(8,128)(2,1)S(1)} %collective-permute-done, f32[1024]{0:T(1024)S(1)} %get-tuple-element.53, bf16[224,1792]{1,0:T(8,128)(2,1)S(1)} %get-tuple-element.32, bf16[1792,2048]{1,0:T(8,128)(2,1)} %refs_2_.3), kind=kOutput, calls=%fused_computation.41 | convolution fusion | flops 823230464 | bytes 6311936 | tf_op jit(solution)/shard_map/dot_general | solution.py:90
  34.0 2.0 collective-permute-start.1
  36.2 1.9 collective-permute-done.10
  38.1 0.7 collective-permute-start.11
  38.8 10.5 %collective-permute-done.1 = bf16[224,1024]{1,0:T(8,128)(2,1)S(1)} collective-permute-done((bf16[224,1024]{1,0:T(8,128)(2,1)S(1)}, bf16[224,1024]{1,0:T(8,128)(2,1)S(1)}, u32[]{:S(2)}, u32[]{:S(2)}) %collective-permute-start.1) | collective-permute-done | bytes 458784 | tf_op jit(solution)/shard_map/ppermute | solution.py:106
  49.4 3.5 %fusion.32 = f32[448,1792]{1,0:T(8,128)S(1)} fusion(bf16[2048,1792]{1,0:T(8,128)(2,1)S(1)} %bitcast.21, bf16[224,1024]{1,0:T(8,128)(2,1)S(1)} %collective-permute-done.3, bf16[224,1024]{1,0:T(8,128)(2,1)S(1)} %get-tuple-element.57, bf16[224,1024]{1,0:T(8,128)(2,1)S(1)} %collective-permute-done.1, bf16[224,1024]{1,0:T(8,128)(2,1)S(1)} %get-tuple-element.55), kind=kOutput, calls=%fused_computation.83 | convolution fusion | flops 3295674368 | bytes 12386304 | tf_op jit(solution)/shard_map/dot_general | solution.py:90
  53.0 2.2 collective-permute-start.4
  55.2 0.4 maximum_select_fusion.1.refs_0_
  55.6 1.8 add_select_fusion
  57.6 0.6 collective-permute-start.12
  58.4 3.7 %collective-permute-start.5 = (bf16[112,1792]{1,0:T(8,128)(2,1)S(1)}, bf16[112,1792]{1,0:T(8,128)(2,1)S(1)}, u32[]{:S(2)}, u32[]{:S(2)}) collective-permute-start(bf16[112,1792]{1,0:T(8,128)(2,1)S(1)} %select_convert_fusion.3), channel_id=1, source_target_pairs={{0,8},{2,10},{4,12},{6,14},{8,0},{10,2},{12,4},{14,6},{1,9},{3,11}... | collective-permute-start | bytes 1204232 | tf_op jit(solution)/shard_map/ppermute | solution.py:111
  62.5 1.6 collective-permute-start.13
  64.1 7.6 %collective-permute-done.5 = bf16[112,1792]{1,0:T(8,128)(2,1)S(1)} collective-permute-done((bf16[112,1792]{1,0:T(8,128)(2,1)S(1)}, bf16[112,1792]{1,0:T(8,128)(2,1)S(1)}, u32[]{:S(2)}, u32[]{:S(2)}) %collective-permute-start.5) | collective-permute-done | bytes 401440 | tf_op jit(solution)/shard_map/ppermute | solution.py:111
  71.8 1.7 collective-permute-done.13
  73.6 0.4 collective-permute-start.14
  74.1 3.6 %collective-permute-start.6 = (bf16[112,896]{1,0:T(8,128)(2,1)S(1)}, bf16[112,896]{1,0:T(8,128)(2,1)S(1)}, u32[]{:S(2)}, u32[]{:S(2)}) collective-permute-start(bf16[112,896]{1,0:T(8,128)(2,1)S(1)} %select_convert_fusion.5), channel_id=1, source_target_pairs={{0,4},{2,6},{4,0},{6,2},{8,12},{10,14},{12,8},{14,10},{1,5},{3,7},... | collective-permute-start | bytes 602120 | tf_op jit(solution)/shard_map/ppermute | solution.py:111
  77.6 1.8 collective-permute-done.14
  79.6 8.8 %collective-permute-start.15 = (bf16[56,896]{1,0:T(8,128)(2,1)S(1)}, bf16[56,896]{1,0:T(8,128)(2,1)S(1)}, u32[]{:S(2)}, u32[]{:S(2)}) collective-permute-start(bf16[56,896]{1,0:T(8,128)(2,1)S(1)} %select_convert_fusion.6), channel_id=1, source_target_pairs={{0,16},{2,18},{4,20},{6,22},{8,24},{10,26},{12,28},{14,30},{16,0},... | collective-permute-start | bytes 301064 | tf_op jit(solution)/shard_map/ppermute | solution.py:111
  88.5 3.4 %collective-permute-start.7 = (bf16[112,896]{1,0:T(8,128)(2,1)S(1)}, bf16[112,896]{1,0:T(8,128)(2,1)S(1)}, u32[]{:S(2)}, u32[]{:S(2)}) collective-permute-start(bf16[112,896]{1,0:T(8,128)(2,1)S(1)} %fusion.26), channel_id=1, source_target_pairs={{0,4},{2,6},{4,0},{6,2},{8,12},{10,14},{12,8},{14,10},{1,5},{3,7},... | collective-permute-start | bytes 602120 | tf_op jit(solution)/shard_map/ppermute | solution.py:111
  92.1 2.1 collective-permute-start.16
  94.1 2.0 collective-permute-done.7
  96.1 1.5 collective-permute-done.16
  97.7 1.8 collective-permute-start.17
  99.6 2.2 %collective-permute-start.8 = (bf16[112,1792]{1,0:T(8,128)(2,1)S(1)}, bf16[112,1792]{1,0:T(8,128)(2,1)S(1)}, u32[]{:S(2)}, u32[]{:S(2)}) collective-permute-start(bf16[112,1792]{1,0:T(8,128)(2,1)S(1)} %pad_maximum_fusion.4), channel_id=1, source_target_pairs={{0,8},{2,10},{4,12},{6,14},{8,0},{10,2},{12,4},{14,6},{1,9},{3,11}... | collective-permute-start | bytes 1204232 | tf_op jit(solution)/shard_map/ppermute | solution.py:111
  101.8 4.0 %collective-permute-done.17 = bf16[112,896]{1,0:T(8,128)(2,1)S(1)} collective-permute-done((bf16[112,896]{1,0:T(8,128)(2,1)S(1)}, bf16[112,896]{1,0:T(8,128)(2,1)S(1)}, u32[]{:S(2)}, u32[]{:S(2)}) %collective-permute-start.17) | collective-permute-done | bytes 200736 | tf_op jit(solution)/shard_map/ppermute | solution.py:111
  105.9 1.1 collective-permute-start.18
  107.0 4.5 %collective-permute-done.8 = bf16[112,1792]{1,0:T(8,128)(2,1)S(1)} collective-permute-done((bf16[112,1792]{1,0:T(8,128)(2,1)S(1)}, bf16[112,1792]{1,0:T(8,128)(2,1)S(1)}, u32[]{:S(2)}, u32[]{:S(2)}) %collective-permute-start.8) | collective-permute-done | bytes 401440 | tf_op jit(solution)/shard_map/ppermute | solution.py:111
  111.6 2.1 collective-permute-start.9
  114.0 0.5 collective-permute-start.19
  114.6 1.2 collective-permute-done.9
  115.8 0.3 broadcast_select_fusion.3
  116.1 0.9 collective-permute-done.19
  117.0 0.3 broadcast_select_fusion.1
  117.3 1.8 fusion.31
  119.2 0.4 pad_maximum_fusion.1
  119.6 1.9 select_add_fusion
  121.6 0.6 collective-permute-start.20
  122.2 0.7 collective-permute-start.22
  122.8 1.8 fusion
  124.8 1.6 collective-permute-start.21
  126.5 1.4 collective-permute-start.23
  128.1 6.9 %collective-permute-done.20 = bf16[224,1024]{1,0:T(8,128)(2,1)S(1)} collective-permute-done((bf16[224,1024]{1,0:T(8,128)(2,1)S(1)}, bf16[224,1024]{1,0:T(8,128)(2,1)S(1)}, u32[]{:S(2)}, u32[]{:S(2)}) %collective-permute-start.20) | collective-permute-done | bytes 458784 | tf_op jit(solution)/shard_map/ppermute | solution.py:106
  135.0 1.0 fusion.25
  136.0 0.5 collective-permute-start.24
  136.6 8.2 %collective-permute-done.21 = bf16[224,1024]{1,0:T(8,128)(2,1)S(1)} collective-permute-done((bf16[224,1024]{1,0:T(8,128)(2,1)S(1)}, bf16[224,1024]{1,0:T(8,128)(2,1)S(1)}, u32[]{:S(2)}, u32[]{:S(2)}) %collective-permute-start.21) | collective-permute-done | bytes 458784 | tf_op jit(solution)/shard_map/ppermute | solution.py:106
  144.8 20.3 %collective-permute-done.23 = bf16[224,1024]{1,0:T(8,128)(2,1)S(1)} collective-permute-done((bf16[224,1024]{1,0:T(8,128)(2,1)S(1)}, bf16[224,1024]{1,0:T(8,128)(2,1)S(1)}, u32[]{:S(2)}, u32[]{:S(2)}) %collective-permute-start.23) | collective-permute-done | bytes 458784 | tf_op jit(solution)/shard_map/ppermute | solution.py:237
  165.1 1.1 fusion.23
  166.3 0.6 collective-permute-start.25
  166.8 18.7 %shard_map.230 = (bf16[2048,1792]{1,0:T(8,128)(2,1)}, bf16[2048,1792]{1,0:T(8,128)(2,1)}, bf16[2048,1792]{1,0:T(8,128)(2,1)}) custom-call(bf16[448,2048]{1,0:T(8,128)(2,1)S(1)} %maximum_maximum_fusion.refs_0_, bf16[448,1792]{1,0:T(8,128)(2,1)S(1)} %get-tuple-element.35.refs_1_, bf16[2048,1792]{1,0:T(8,128)(2,1)S(1)} %bitcast.21, bf16[2048,1792]{1,0:T(8,128)(2,1)} %refs_3_.4, ...), custom_call_target="tpu_custom_call" | custom-call | flops 3288334336 | bytes 44040192 | tf_op jit(solution)/shard_map/pallas_call | solution.py:68
  185.5 1.3 convert_reduce_fusion
  186.8 1.5 collective-permute-start.26
  188.4 2.2 copy-done.4
  190.6 7.4 %shard_map.231 = (bf16[1024,1792]{1,0:T(8,128)(2,1)}, bf16[1024,1792]{1,0:T(8,128)(2,1)}, bf16[1024,1792]{1,0:T(8,128)(2,1)}) custom-call(bf16[448,1024]{1,0:T(8,128)(2,1)S(1)} %maximum_select_fusion.1.refs_0_, bf16[448,1792]{1,0:T(8,128)(2,1)S(1)} %get-tuple-element.34.refs_1_, bf16[1024,1792]{1,0:T(8,128)(2,1)S(1)} %copy-done.2, ...), custom_call_target="tpu_custom_call" | custom-call | flops 1644167168 | bytes 22020096 | tf_op jit(solution)/shard_map/pallas_call | solution.py:68
  198.0 0.6 fusion.30
  198.7 1.6 maximum_maximum_fusion.1.refs_1_
  200.3 18.2 %shard_map.229 = (bf16[1792,2048]{1,0:T(8,128)(2,1)}, bf16[1792,2048]{1,0:T(8,128)(2,1)}, bf16[1792,2048]{1,0:T(8,128)(2,1)}) custom-call(bf16[448,1792]{1,0:T(8,128)(2,1)S(1)} %pad_maximum_fusion.refs_0_, bf16[448,2048]{1,0:T(8,128)(2,1)S(1)} %maximum_maximum_fusion.1.refs_1_, bf16[1792,2048]{1,0:T(8,128)(2,1)S(1)} %bitcast.23, bf16[1792,2048]{1,0:T(8,128)(2,1)} %refs_3_.3, ...), custom_call_target="tpu_custom_call" | custom-call | flops 3288334336 | bytes 44040192 | tf_op jit(solution)/shard_map/pallas_call | solution.py:68
  (88 shorter events, 3.2 us)
Async XLA Ops:
  0.7 8.7 %copy-start = (bf16[1792,2048]{1,0:T(8,128)(2,1)S(1)}, bf16[1792,2048]{1,0:T(8,128)(2,1)}, u32[]{:S(2)}) copy-start(bf16[1792,2048]{1,0:T(8,128)(2,1)} %refs_2_.3) | copy-start | bytes 22020100
  2.3 7.0 %copy-start.8 = (bf16[224,1792]{1,0:T(8,128)(2,1)}, bf16[224,1792]{1,0:T(8,128)(2,1)S(1)}, u32[]{:S(2)}) copy-start(bf16[224,1792]{1,0:T(8,128)(2,1)S(1)} %get-tuple-element.33) | copy-start | bytes 2408452
  2.3 28.3 %copy-start.6 = (bf16[224,1792]{1,0:T(8,128)(2,1)}, bf16[224,1792]{1,0:T(8,128)(2,1)S(1)}, u32[]{:S(2)}) copy-start(bf16[224,1792]{1,0:T(8,128)(2,1)S(1)} %get-tuple-element.32) | copy-start | bytes 2408452
  6.3 4.1 %copy-start.14 = (bf16[2048]{0:T(1024)(128)(2,1)S(1)}, bf16[2048]{0:T(1024)(128)(2,1)}, u32[]{:S(2)}) copy-start(bf16[2048]{0:T(1024)(128)(2,1)} %param.17) | copy-start | bytes 12292
  6.3 14.4 %collective-permute-start.2 = (f16[224,1024]{1,0:T(8,128)(2,1)S(1)}, f16[224,1024]{1,0:T(8,128)(2,1)S(1)}, u32[]{:S(2)}, u32[]{:S(2)}) collective-permute-start(f16[224,1024]{1,0:T(8,128)(2,1)S(1)} %fusion.17), channel_id=1, source_target_pairs={{0,1},{1,0},{2,3},{3,2},{4,5},{5,4},{6,7},{7,6},{8,9},{9,8},{10,11... | collective-permute-start | bytes 1376264 | tf_op jit(solution)/shard_map/ppermute | solution.py:106
  10.3 20.3 %collective-permute-start = (f16[224,1024]{1,0:T(8,128)(2,1)S(1)}, f16[224,1024]{1,0:T(8,128)(2,1)S(1)}, u32[]{:S(2)}, u32[]{:S(2)}) collective-permute-start(f16[224,1024]{1,0:T(8,128)(2,1)S(1)} %fusion.14), channel_id=1, source_target_pairs={{0,1},{1,0},{2,3},{3,2},{4,5},{5,4},{6,7},{7,6},{8,9},{9,8},{10,11... | collective-permute-start | bytes 1376264 | tf_op jit(solution)/shard_map/ppermute | solution.py:106
  20.7 3.3 %copy-start.12 = (f16[224,1024]{1,0:T(8,128)(2,1)}, f16[224,1024]{1,0:T(8,128)(2,1)S(1)}, u32[]{:S(2)}) copy-start(f16[224,1024]{1,0:T(8,128)(2,1)S(1)} %collective-permute-done.2) | copy-start | bytes 1376260
  20.7 28.7 %slice-start = ((s8[7340032]{0:T(1024)(128)(4,1)}), s8[4194304]{0:T(1024)(128)(4,1)S(1)}, s32[]{:S(2)}) async-start(s8[7340032]{0:T(1024)(128)(4,1)} %bitcast.20), calls=%async_computation | async-start | bytes 8388608
  24.0 25.3 %collective-permute-start.3 = (bf16[224,1024]{1,0:T(8,128)(2,1)S(1)}, bf16[224,1024]{1,0:T(8,128)(2,1)S(1)}, u32[]{:S(2)}, u32[]{:S(2)}) collective-permute-start(bf16[224,1024]{1,0:T(8,128)(2,1)S(1)} %get-tuple-element.57), channel_id=1, source_target_pairs={{0,1},{1,0},{2,3},{3,2},{4,5},{5,4},{6,7},{7,6},{8,9},{9,8},{10,11... | collective-permute-start | bytes 1376264 | tf_op jit(solution)/shard_map/ppermute | solution.py:106
  26.1 12.0 %collective-permute-start.10 = (bf16[224,1024]{1,0:T(8,128)(2,1)S(1)}, bf16[224,1024]{1,0:T(8,128)(2,1)S(1)}, u32[]{:S(2)}, u32[]{:S(2)}) collective-permute-start(bf16[224,1024]{1,0:T(8,128)(2,1)S(1)} %get-tuple-element.57), channel_id=1, source_target_pairs={{0,16},{2,18},{4,20},{6,22},{8,24},{10,26},{12,28},{14,30},{1,17},... | collective-permute-start | bytes 1376264 | tf_op jit(solution)/shard_map/ppermute | solution.py:191
  30.6 3.3 %copy-start.10 = (f16[224,1024]{1,0:T(8,128)(2,1)}, f16[224,1024]{1,0:T(8,128)(2,1)S(1)}, u32[]{:S(2)}) copy-start(f16[224,1024]{1,0:T(8,128)(2,1)S(1)} %collective-permute-done) | copy-start | bytes 1376260
  30.7 5.3 %copy-start.5 = (bf16[2,448,1792]{2,1,0:T(8,128)(2,1)S(1)}, bf16[2,448,1792]{2,1,0:T(8,128)(2,1)}, u32[]{:S(2)}) copy-start(bf16[2,448,1792]{2,1,0:T(8,128)(2,1)} %param.15) | copy-start | bytes 9633796
  30.7 18.7 %slice-start.1 = ((s8[7340032]{0:T(1024)(128)(4,1)}), s8[3145728]{0:T(1024)(128)(4,1)S(1)}, s32[]{:S(2)}) async-start(s8[7340032]{0:T(1024)(128)(4,1)} %bitcast.20), calls=%async_computation.1 | async-start | bytes 6291456
  34.0 15.4 %collective-permute-start.1 = (bf16[224,1024]{1,0:T(8,128)(2,1)S(1)}, bf16[224,1024]{1,0:T(8,128)(2,1)S(1)}, u32[]{:S(2)}, u32[]{:S(2)}) collective-permute-start(bf16[224,1024]{1,0:T(8,128)(2,1)S(1)} %get-tuple-element.55), channel_id=1, source_target_pairs={{0,1},{1,0},{2,3},{3,2},{4,5},{5,4},{6,7},{7,6},{8,9},{9,8},{10,11... | collective-permute-start | bytes 1376264 | tf_op jit(solution)/shard_map/ppermute | solution.py:106
  38.1 17.1 %collective-permute-start.11 = (bf16[224,1024]{1,0:T(8,128)(2,1)S(1)}, bf16[224,1024]{1,0:T(8,128)(2,1)S(1)}, u32[]{:S(2)}, u32[]{:S(2)}) collective-permute-start(bf16[224,1024]{1,0:T(8,128)(2,1)S(1)} %collective-permute-done.10), channel_id=1, source_target_pairs={{16,17},{17,16},{18,19},{19,18},{20,21},{21,20},{22,23},{23,22},{2... | collective-permute-start | bytes 1376264 | tf_op jit(solution)/shard_map/ppermute | solution.py:202
  52.8 2.7 %copy-start.1 = (bf16[1024,1792]{1,0:T(8,128)(2,1)S(1)}, bf16[1024,1792]{1,0:T(8,128)(2,1)}, u32[]{:S(2)}) copy-start(bf16[1024,1792]{1,0:T(8,128)(2,1)} %refs_2_.5) | copy-start | bytes 11010052
  53.0 5.1 %collective-permute-start.4 = (bf16[224,1792]{1,0:T(8,128)(2,1)S(1)}, bf16[224,1792]{1,0:T(8,128)(2,1)S(1)}, u32[]{:S(2)}, u32[]{:S(2)}) collective-permute-start(bf16[224,1792]{1,0:T(8,128)(2,1)S(1)} %select_convert_fusion.1), channel_id=1, source_target_pairs={{0,2},{2,0},{4,6},{6,4},{8,10},{10,8},{12,14},{14,12},{1,3},{3,1},... | collective-permute-start | bytes 2408456 | tf_op jit(solution)/shard_map/ppermute | solution.py:111
  57.6 4.6 %collective-permute-start.12 = (bf16[224,1792]{1,0:T(8,128)(2,1)S(1)}, bf16[224,1792]{1,0:T(8,128)(2,1)S(1)}, u32[]{:S(2)}, u32[]{:S(2)}) collective-permute-start(bf16[224,1792]{1,0:T(8,128)(2,1)S(1)} %select_convert_fusion), channel_id=1, source_target_pairs={{0,2},{2,0},{4,6},{6,4},{8,10},{10,8},{12,14},{14,12},{16,18},{18,... | collective-permute-start | bytes 2408456 | tf_op jit(solution)/shard_map/ppermute | solution.py:111
  58.4 13.2 %collective-permute-start.5 = (bf16[112,1792]{1,0:T(8,128)(2,1)S(1)}, bf16[112,1792]{1,0:T(8,128)(2,1)S(1)}, u32[]{:S(2)}, u32[]{:S(2)}) collective-permute-start(bf16[112,1792]{1,0:T(8,128)(2,1)S(1)} %select_convert_fusion.3), channel_id=1, source_target_pairs={{0,8},{2,10},{4,12},{6,14},{8,0},{10,2},{12,4},{14,6},{1,9},{3,11}... | collective-permute-start | bytes 1204232 | tf_op jit(solution)/shard_map/ppermute | solution.py:111
  62.5 11.0 %collective-permute-start.13 = (bf16[112,1792]{1,0:T(8,128)(2,1)S(1)}, bf16[112,1792]{1,0:T(8,128)(2,1)S(1)}, u32[]{:S(2)}, u32[]{:S(2)}) collective-permute-start(bf16[112,1792]{1,0:T(8,128)(2,1)S(1)} %select_convert_fusion.2), channel_id=1, source_target_pairs={{0,4},{2,6},{4,0},{6,2},{8,12},{10,14},{12,8},{14,10},{16,20},{18,... | collective-permute-start | bytes 1204232 | tf_op jit(solution)/shard_map/ppermute | solution.py:111
  73.6 5.8 %collective-permute-start.14 = (bf16[112,896]{1,0:T(8,128)(2,1)S(1)}, bf16[112,896]{1,0:T(8,128)(2,1)S(1)}, u32[]{:S(2)}, u32[]{:S(2)}) collective-permute-start(bf16[112,896]{1,0:T(8,128)(2,1)S(1)} %select_convert_fusion.4), channel_id=1, source_target_pairs={{0,8},{2,10},{4,12},{6,14},{8,0},{10,2},{12,4},{14,6},{16,24},{18,... | collective-permute-start | bytes 602120 | tf_op jit(solution)/shard_map/ppermute | solution.py:111
  74.1 14.3 %collective-permute-start.6 = (bf16[112,896]{1,0:T(8,128)(2,1)S(1)}, bf16[112,896]{1,0:T(8,128)(2,1)S(1)}, u32[]{:S(2)}, u32[]{:S(2)}) collective-permute-start(bf16[112,896]{1,0:T(8,128)(2,1)S(1)} %select_convert_fusion.5), channel_id=1, source_target_pairs={{0,4},{2,6},{4,0},{6,2},{8,12},{10,14},{12,8},{14,10},{1,5},{3,7},... | collective-permute-start | bytes 602120 | tf_op jit(solution)/shard_map/ppermute | solution.py:111
  79.6 12.4 %collective-permute-start.15 = (bf16[56,896]{1,0:T(8,128)(2,1)S(1)}, bf16[56,896]{1,0:T(8,128)(2,1)S(1)}, u32[]{:S(2)}, u32[]{:S(2)}) collective-permute-start(bf16[56,896]{1,0:T(8,128)(2,1)S(1)} %select_convert_fusion.6), channel_id=1, source_target_pairs={{0,16},{2,18},{4,20},{6,22},{8,24},{10,26},{12,28},{14,30},{16,0},... | collective-permute-start | bytes 301064 | tf_op jit(solution)/shard_map/ppermute | solution.py:111
  88.5 7.6 %collective-permute-start.7 = (bf16[112,896]{1,0:T(8,128)(2,1)S(1)}, bf16[112,896]{1,0:T(8,128)(2,1)S(1)}, u32[]{:S(2)}, u32[]{:S(2)}) collective-permute-start(bf16[112,896]{1,0:T(8,128)(2,1)S(1)} %fusion.26), channel_id=1, source_target_pairs={{0,4},{2,6},{4,0},{6,2},{8,12},{10,14},{12,8},{14,10},{1,5},{3,7},... | collective-permute-start | bytes 602120 | tf_op jit(solution)/shard_map/ppermute | solution.py:111
  92.1 5.6 %collective-permute-start.16 = (bf16[56,896]{1,0:T(8,128)(2,1)S(1)}, bf16[56,896]{1,0:T(8,128)(2,1)S(1)}, u32[]{:S(2)}, u32[]{:S(2)}) collective-permute-start(bf16[56,896]{1,0:T(8,128)(2,1)S(1)} %fusion.27), channel_id=1, source_target_pairs={{0,16},{2,18},{4,20},{6,22},{8,24},{10,26},{12,28},{14,30},{16,0},... | collective-permute-start | bytes 301064 | tf_op jit(solution)/shard_map/ppermute | solution.py:111
  97.7 8.0 %collective-permute-start.17 = (bf16[112,896]{1,0:T(8,128)(2,1)S(1)}, bf16[112,896]{1,0:T(8,128)(2,1)S(1)}, u32[]{:S(2)}, u32[]{:S(2)}) collective-permute-start(bf16[112,896]{1,0:T(8,128)(2,1)S(1)} %pad_maximum_fusion.6), channel_id=1, source_target_pairs={{0,8},{2,10},{4,12},{6,14},{8,0},{10,2},{12,4},{14,6},{16,24},{18,... | collective-permute-start | bytes 602120 | tf_op jit(solution)/shard_map/ppermute | solution.py:111
  99.6 11.9 %collective-permute-start.8 = (bf16[112,1792]{1,0:T(8,128)(2,1)S(1)}, bf16[112,1792]{1,0:T(8,128)(2,1)S(1)}, u32[]{:S(2)}, u32[]{:S(2)}) collective-permute-start(bf16[112,1792]{1,0:T(8,128)(2,1)S(1)} %pad_maximum_fusion.4), channel_id=1, source_target_pairs={{0,8},{2,10},{4,12},{6,14},{8,0},{10,2},{12,4},{14,6},{1,9},{3,11}... | collective-permute-start | bytes 1204232 | tf_op jit(solution)/shard_map/ppermute | solution.py:111
  105.8 8.7 %copy-start.7 = (bf16[224,1792]{1,0:T(8,128)(2,1)S(1)}, bf16[224,1792]{1,0:T(8,128)(2,1)}, u32[]{:S(2)}) copy-start(bf16[224,1792]{1,0:T(8,128)(2,1)} %copy-done.6) | copy-start | bytes 2408452
  105.8 8.7 %copy-start.9 = (bf16[224,1792]{1,0:T(8,128)(2,1)S(1)}, bf16[224,1792]{1,0:T(8,128)(2,1)}, u32[]{:S(2)}) copy-start(bf16[224,1792]{1,0:T(8,128)(2,1)} %copy-done.8) | copy-start | bytes 2408452
  105.9 7.9 %collective-permute-start.18 = (bf16[112,1792]{1,0:T(8,128)(2,1)S(1)}, bf16[112,1792]{1,0:T(8,128)(2,1)S(1)}, u32[]{:S(2)}, u32[]{:S(2)}) collective-permute-start(bf16[112,1792]{1,0:T(8,128)(2,1)S(1)} %pad_maximum_fusion.5), channel_id=1, source_target_pairs={{0,4},{2,6},{4,0},{6,2},{8,12},{10,14},{12,8},{14,10},{16,20},{18,... | collective-permute-start | bytes 1204232 | tf_op jit(solution)/shard_map/ppermute | solution.py:111
  111.6 4.2 %collective-permute-start.9 = (bf16[224,1792]{1,0:T(8,128)(2,1)S(1)}, bf16[224,1792]{1,0:T(8,128)(2,1)S(1)}, u32[]{:S(2)}, u32[]{:S(2)}) collective-permute-start(bf16[224,1792]{1,0:T(8,128)(2,1)S(1)} %pad_maximum_fusion.2), channel_id=1, source_target_pairs={{0,2},{2,0},{4,6},{6,4},{8,10},{10,8},{12,14},{14,12},{1,3},{3,1},... | collective-permute-start | bytes 2408456 | tf_op jit(solution)/shard_map/ppermute | solution.py:111
  114.0 3.0 %collective-permute-start.19 = (bf16[224,1792]{1,0:T(8,128)(2,1)S(1)}, bf16[224,1792]{1,0:T(8,128)(2,1)S(1)}, u32[]{:S(2)}, u32[]{:S(2)}) collective-permute-start(bf16[224,1792]{1,0:T(8,128)(2,1)S(1)} %pad_maximum_fusion.3), channel_id=1, source_target_pairs={{0,2},{2,0},{4,6},{6,4},{8,10},{10,8},{12,14},{14,12},{16,18},{18,... | collective-permute-start | bytes 2408456 | tf_op jit(solution)/shard_map/ppermute | solution.py:111
  121.6 13.4 %collective-permute-start.20 = (bf16[224,1024]{1,0:T(8,128)(2,1)S(1)}, bf16[224,1024]{1,0:T(8,128)(2,1)S(1)}, u32[]{:S(2)}, u32[]{:S(2)}) collective-permute-start(bf16[224,1024]{1,0:T(8,128)(2,1)S(1)} %slice.203), channel_id=1, source_target_pairs={{0,1},{1,0},{2,3},{3,2},{4,5},{5,4},{6,7},{7,6},{8,9},{9,8},{10,11... | collective-permute-start | bytes 1376264 | tf_op jit(solution)/shard_map/ppermute | solution.py:106
  122.2 4.2 %collective-permute-start.22 = (bf16[224,1024]{1,0:T(8,128)(2,1)S(1)}, bf16[224,1024]{1,0:T(8,128)(2,1)S(1)}, u32[]{:S(2)}, u32[]{:S(2)}) collective-permute-start(bf16[224,1024]{1,0:T(8,128)(2,1)S(1)} %slice.201), channel_id=1, source_target_pairs={{16,17},{17,16},{18,19},{19,18},{20,21},{21,20},{22,23},{23,22},{2... | collective-permute-start | bytes 1376264 | tf_op jit(solution)/shard_map/ppermute | solution.py:233
  124.7 10.3 %copy-start.11 = (f16[224,1024]{1,0:T(8,128)(2,1)S(1)}, f16[224,1024]{1,0:T(8,128)(2,1)}, u32[]{:S(2)}) copy-start(f16[224,1024]{1,0:T(8,128)(2,1)} %copy-done.10) | copy-start | bytes 1376260
  124.8 20.0 %collective-permute-start.21 = (bf16[224,1024]{1,0:T(8,128)(2,1)S(1)}, bf16[224,1024]{1,0:T(8,128)(2,1)S(1)}, u32[]{:S(2)}, u32[]{:S(2)}) collective-permute-start(bf16[224,1024]{1,0:T(8,128)(2,1)S(1)} %slice.202), channel_id=1, source_target_pairs={{0,1},{1,0},{2,3},{3,2},{4,5},{5,4},{6,7},{7,6},{8,9},{9,8},{10,11... | collective-permute-start | bytes 1376264 | tf_op jit(solution)/shard_map/ppermute | solution.py:106
  126.5 38.7 %copy-start.13 = (f16[224,1024]{1,0:T(8,128)(2,1)S(1)}, f16[224,1024]{1,0:T(8,128)(2,1)}, u32[]{:S(2)}) copy-start(f16[224,1024]{1,0:T(8,128)(2,1)} %copy-done.12) | copy-start | bytes 1376260
  126.5 38.7 %collective-permute-start.23 = (bf16[224,1024]{1,0:T(8,128)(2,1)S(1)}, bf16[224,1024]{1,0:T(8,128)(2,1)S(1)}, u32[]{:S(2)}, u32[]{:S(2)}) collective-permute-start(bf16[224,1024]{1,0:T(8,128)(2,1)S(1)} %fusion.20), channel_id=1, source_target_pairs={{16,0},{18,2},{20,4},{22,6},{24,8},{26,10},{28,12},{30,14},{17,1},... | collective-permute-start | bytes 1376264 | tf_op jit(solution)/shard_map/ppermute | solution.py:237
  136.0 62.6 %collective-permute-start.24 = (bf16[224,1024]{1,0:T(8,128)(2,1)}, bf16[224,1024]{1,0:T(8,128)(2,1)}, u32[]{:S(2)}, u32[]{:S(2)}) collective-permute-start(bf16[224,1024]{1,0:T(8,128)(2,1)} %fusion.25), channel_id=1, source_target_pairs={{0,1},{1,0},{2,3},{3,2},{4,5},{5,4},{6,7},{7,6},{8,9},{9,8},{10,11... | collective-permute-start | bytes 1376264 | tf_op jit(solution)/shard_map/ppermute | solution.py:106
  166.3 32.4 %collective-permute-start.25 = (bf16[224,1024]{1,0:T(8,128)(2,1)}, bf16[224,1024]{1,0:T(8,128)(2,1)}, u32[]{:S(2)}, u32[]{:S(2)}) collective-permute-start(bf16[224,1024]{1,0:T(8,128)(2,1)} %fusion.23), channel_id=1, source_target_pairs={{0,1},{1,0},{2,3},{3,2},{4,5},{5,4},{6,7},{7,6},{8,9},{9,8},{10,11... | collective-permute-start | bytes 1376264 | tf_op jit(solution)/shard_map/ppermute | solution.py:106
  166.8 21.6 %copy-start.2 = (bf16[1024,1792]{1,0:T(8,128)(2,1)S(1)}, bf16[1024,1792]{1,0:T(8,128)(2,1)}, u32[]{:S(2)}) copy-start(bf16[1024,1792]{1,0:T(8,128)(2,1)} %refs_2_.5) | copy-start | bytes 11010052
  166.8 21.6 %copy-start.3 = (bf16[1024,1792]{1,0:T(8,128)(2,1)S(1)}, bf16[1024,1792]{1,0:T(8,128)(2,1)}, u32[]{:S(2)}) copy-start(bf16[1024,1792]{1,0:T(8,128)(2,1)} %refs_3_.5) | copy-start | bytes 11010052
  186.8 11.2 %collective-permute-start.26 = (f32[2048]{0:T(1024)S(1)}, f32[2048]{0:T(1024)S(1)}, u32[]{:S(2)}, u32[]{:S(2)}) collective-permute-start(f32[2048]{0:T(1024)S(1)} %convert_reduce_fusion), channel_id=1, source_target_pairs={{0,1},{1,0},{2,3},{3,2},{4,5},{5,4},{6,7},{7,6},{8,9},{9,8},{10,11... | collective-permute-start | bytes 24584 | tf_op jit(solution)/shard_map/ppermute | solution.py:106
  188.4 11.9 %slice-start.2 = ((s8[7340032]{0:T(1024)(128)(4,1)}), s8[4194304]{0:T(1024)(128)(4,1)S(1)}, s32[]{:S(2)}) async-start(s8[7340032]{0:T(1024)(128)(4,1)} %bitcast.22), calls=%async_computation.2 | async-start | bytes 8388608
  188.4 2.2 %copy-start.4 = (bf16[1024,1792]{1,0:T(8,128)(2,1)S(1)}, bf16[1024,1792]{1,0:T(8,128)(2,1)}, u32[]{:S(2)}) copy-start(bf16[1024,1792]{1,0:T(8,128)(2,1)} %refs_4_.5) | copy-start | bytes 11010052
  190.6 7.4 %copy-start.15 = (bf16[2048]{0:T(1024)(128)(2,1)S(1)}, bf16[2048]{0:T(1024)(128)(2,1)}, u32[]{:S(2)}) copy-start(bf16[2048]{0:T(1024)(128)(2,1)} %param.23) | copy-start | bytes 12292
  190.6 7.4 %copy-start.16 = (bf16[2048]{0:T(1024)(128)(2,1)S(1)}, bf16[2048]{0:T(1024)(128)(2,1)}, u32[]{:S(2)}) copy-start(bf16[2048]{0:T(1024)(128)(2,1)} %param.22) | copy-start | bytes 12292
  190.6 9.7 %slice-start.3 = ((s8[7340032]{0:T(1024)(128)(4,1)}), s8[3145728]{0:T(1024)(128)(4,1)S(1)}, s32[]{:S(2)}) async-start(s8[7340032]{0:T(1024)(128)(4,1)} %bitcast.22), calls=%async_computation.3 | async-start | bytes 6291456
where the time goes:
time: 219 us; the launch traced here: 218 us
  waiting for transfers between devices  83.3 us (38%)
  starting transfers between devices  53.3 us (24%)
  Pallas kernels  44.3 us (20%)
  matrix products  22.4 us (10%)
  other arithmetic  9.59 us (4%)
  local copies, waits for them, and re-layouts  4.33 us (2%)
    pallas_call x3, Pallas kernels, adamw_matmul(): pl.pallas_call(functools.partial(adamw_kernel, decay_rate, tile), grid=(r...  44.3 us
    ppermute x9, waiting for transfers between devices, across(): return lax.ppermute(value, 'width', [(0, 1), (1, 0)])  35.9 us
    ppermute x14, starting transfers between devices, flipped(): lax.ppermute(value, 'feat', [(index, index ^ step) for index in range(mem...  34 us
    ppermute x14, waiting for transfers between devices, flipped(): lax.ppermute(value, 'feat', [(index, index ^ step) for index in range(mem...  25.1 us
    ppermute x1, waiting for transfers between devices, local(): lax.ppermute(cross_sum, 'feat', [(index + half_count, index) for index in...  20.3 us
    dot_general x6, matrix products, matmul(): return jnp.dot(left, right, preferred_element_type=jnp.float32)  16.8 us
    ppermute x9, starting transfers between devices, across(): return lax.ppermute(value, 'width', [(0, 1), (1, 0)])  12 us
    dot_general x3, matrix products, over_cols(): lax.dot_general(left, right, (((1,), (1,)), ((), ())), preferred_element_...  5.55 us
  transfers between devices with their start and end apart: 27, of which 15 were waited for; matrix products, arithmetic and copies ran while one was open for 10% of the time, Pallas kernels for 12%

commit v1 on v0

v1 whole, which is shorter than its diff:
```python
import functools
import math
import jax
import jax.numpy as jnp
from jax import lax
from jax.experimental import pallas as pl
from jax.experimental.pallas import tpu as pltpu
from jax.sharding import PartitionSpec as P

STEPS = 100


beta_one = 0.9
beta_two = 0.999
learn_rate = 0.002
adam_eps = 1e-08
weight_decay = 0.1


def adamw_update(parameter, first, second, gradient, decay_rate):
    first_new = beta_one * first.astype(jnp.float32) + (1.0 - beta_one) * gradient
    second_new = beta_two * second.astype(jnp.float32) + (1.0 - beta_two) * gradient * gradient
    first_hat = first_new / (1.0 - beta_one**STEPS)
    second_hat = second_new / (1.0 - beta_two**STEPS)
    weight = parameter.astype(jnp.float32)
    updated = weight - learn_rate * (
        first_hat / (jnp.sqrt(second_hat) + adam_eps) + decay_rate * weight
    )
    return (
        updated.astype(jnp.bfloat16),
        first_new.astype(jnp.bfloat16),
        second_new.astype(jnp.bfloat16),
    )


def adamw_kernel(decay_rate, tile, *refs):
    left_ref, right_ref, weight_ref, first_ref, second_ref = refs[:5]
    updated_ref, moment_ref, square_ref = refs[-3:]
    first_scale, second_scale = 1.0 - beta_one**STEPS, 1.0 - beta_two**STEPS
    keep = 1.0 - learn_rate * decay_rate
    rate = learn_rate * math.sqrt(second_scale) / first_scale
    shift = adam_eps * math.sqrt(second_scale)
    for start in range(0, weight_ref.shape[1], tile):
        columns = slice(start, start + tile)
        gradient = over_rows(left_ref[...], right_ref[:, columns])
        scaled = (1.0 - beta_one) * gradient
        first_new = beta_one * first_ref[:, columns].astype(jnp.float32) + scaled
        second_new = (
            beta_two * second_ref[:, columns].astype(jnp.float32)
            + ((1.0 - beta_two) * gradient) * gradient
        )
        root = second_new * lax.rsqrt(second_new)
        step = (rate * first_new) * pl.reciprocal(root + shift, approx=True)
        updated = keep * weight_ref[:, columns].astype(jnp.float32) - step
        updated_ref[:, columns] = updated.astype(jnp.bfloat16)
        moment_ref[:, columns] = first_new.astype(jnp.bfloat16)
        square_ref[:, columns] = second_new.astype(jnp.bfloat16)


def adamw_matmul(left, right, weight, first, second, decay_rate, share=(0, 1), partly_done=()):
    tokens = left.shape[0]
    rows, width = weight.shape
    block = math.gcd(rows, 256)
    span = width // share[1]
    tile = math.gcd(span, 256)
    strip = pl.BlockSpec((block, span), lambda place: (place, share[0]))
    return pl.pallas_call(
        functools.partial(adamw_kernel, decay_rate, tile),
        grid=(rows // block,),
        in_specs=[
            pl.BlockSpec((tokens, block), lambda place: (0, place)),
            pl.BlockSpec((tokens, span), lambda place: (0, 0)),
            strip,
            strip,
            strip,
        ]
        + [pl.BlockSpec(memory_space=pl.ANY)] * len(partly_done),
        out_specs=[strip] * 3,
        out_shape=[jax.ShapeDtypeStruct((rows, width), jnp.bfloat16)] * 3,
        input_output_aliases={5 + at: at for at in range(len(partly_done))},
        compiler_params=pltpu.CompilerParams(vmem_limit_bytes=40 * 2**20),
        cost_estimate=pl.CostEstimate(
            flops=2 * tokens * rows * span,
            bytes_accessed=12 * rows * span,
            transcendentals=2 * rows * span,
        ),
    )(left, right, weight, first, second, *partly_done)


def matmul(left, right):
    return jnp.dot(left, right, preferred_element_type=jnp.float32)


def over_rows(left, right):
    return lax.dot_general(
        left, right, (((0,), (0,)), ((), ())), preferred_element_type=jnp.float32
    )


def over_cols(left, right):
    return lax.dot_general(
        left, right, (((1,), (1,)), ((), ())), preferred_element_type=jnp.float32
    )


def across(value):
    return lax.ppermute(value, "width", [(0, 1), (1, 0)])


def flipped(value, bit, members):
    step = 1 << bit
    return lax.ppermute(value, "feat", [(index, index ^ step) for index in range(members)])


def halves(value, axis):
    size = value.shape[axis] // 2
    return lax.slice_in_dim(value, 0, size, axis=axis), lax.slice_in_dim(
        value, size, 2 * size, axis=axis
    )


def is_upper(bit):
    return ((lax.axis_index("feat") >> bit) & 1) == 1


def split_for(total, bit, axis):
    low, high = halves(total, axis)
    upper = is_upper(bit)
    return jnp.where(upper, high, low), jnp.where(upper, low, high).astype(jnp.bfloat16)


def joined(own, other, bit, axis):
    upper = is_upper(bit)
    return jnp.concatenate(
        [jnp.where(upper, other, own), jnp.where(upper, own, other)], axis=axis
    )


def plan_of(order):
    last = len(order) - 1
    return [
        (bit, None if place == last else 1 if place == 2 else 0)
        for place, bit in enumerate(order)
    ]


def add(total, arrived):
    return total + arrived.astype(jnp.float32)


def summed_steps(total, plan, members, wanted):
    for bit, axis in plan:
        if axis is None:
            keeping, leaving = total, total.astype(jnp.bfloat16)
        else:
            keeping, leaving = split_for(total, bit, axis)
        keeping, arrived = yield (leaving,), (keeping, flipped(leaving, bit, members))
        total = add(keeping, arrived)
    value = (total - wanted).astype(jnp.bfloat16)
    for bit, axis in reversed(plan):
        if axis is not None:
            value, other = yield (value,), (value, flipped(value, bit, members))
            value = joined(value, other, bit, axis)
    yield (value,), value


class Order:
    def __init__(self):
        self.last = ()
        self.waiting = {}

    def after(self, values):
        return lax.optimization_barrier((values, self.last))[0]

    def mark(self, *values):
        self.last = values

    def start(self, name, thread):
        self.last, pending = next(thread)
        self.waiting[name] = (thread, pending)

    def advance(self, name):
        thread, pending = self.waiting[name]
        self.last, pending = thread.send(self.after(pending))
        self.waiting[name] = (thread, pending)

    def result(self, name):
        return self.waiting[name][1]


def local(
    residual,
    targets,
    encoder,
    biases,
    same_decoder,
    next_decoder,
    encoder_first,
    encoder_second,
    biases_first,
    biases_second,
    same_first,
    same_second,
    next_first,
    next_second,
):
    feat_count = lax.axis_size("feat")
    feat_index = lax.axis_index("feat")
    width_index = lax.axis_index("width")
    half_count = feat_count // 2
    source_layer = feat_index // half_count
    leading = source_layer == 0
    tokens, width = residual.shape[1:]
    part = tokens // 2
    half = encoder.shape[1] // 2
    bias = biases.astype(jnp.float32)
    downward = [(index, index + half_count) for index in range(half_count)]
    upward = [(index + half_count, index) for index in range(half_count)]
    trailing_pairs = [
        (2 * index + side, 2 * index + 1 - side)
        for index in range(half_count, feat_count)
        for side in range(2)
    ]

    def wanted_block(layer, plan):
        starts, sizes = [0, 0], [tokens, width]
        for bit, axis in plan:
            if axis is not None:
                sizes[axis] //= 2
                starts[axis] = starts[axis] + is_upper(bit).astype(jnp.int32) * sizes[axis]
        row = lax.rem(starts[0] + width_index * part, tokens)
        block = lax.dynamic_slice(targets, (layer, row, starts[1]), (1, *sizes))
        return block[0].astype(jnp.float32)

    bits = feat_count.bit_length() - 1
    second_plan = plan_of(list(range(bits)))
    first_plan = plan_of(list(range(bits - 1)))
    order = Order()

    inputs = jnp.concatenate(
        [
            lax.dynamic_slice(residual, (source_layer, side * part, 0), (1, part, width))[0]
            for side in (width_index, 1 - width_index)
        ],
        axis=0,
    )
    partial_b = matmul(inputs, encoder[:, half:])
    leaving_b = partial_b[part:].astype(jnp.float16)
    arriving_b = across(leaving_b)
    leaving_a = matmul(inputs[part:], encoder[:, :half]).astype(jnp.float16)
    arriving_a = across(leaving_a)
    pre_b = add(partial_b[:part], arriving_b) + bias[half:]
    act_b = jnp.maximum(pre_b, 0.0).astype(jnp.bfloat16)
    sent = lax.ppermute(act_b, "feat", downward)
    sent_other = lax.ppermute(sent, ("feat", "width"), trailing_pairs)
    other_b = across(act_b)
    pre_a = add(matmul(inputs[:part], encoder[:, :half]), arriving_a) + bias[:half]
    act_a = jnp.maximum(pre_a, 0.0).astype(jnp.bfloat16)
    other_a = across(act_a)
    _, act_a, other_a = lax.optimization_barrier((sent, act_a, other_a))
    active = jnp.concatenate(
        [jnp.concatenate([act_a, act_b], axis=1), jnp.concatenate([other_a, other_b], axis=1)],
        axis=0,
    )
    own_term = matmul(active, same_decoder)
    order.start(
        0, summed_steps(own_term, first_plan, half_count, wanted_block(0, first_plan))
    )
    sent_other, own_term, sent = order.after((sent_other, own_term, sent))
    cross_input = jnp.where(leading, active[:, :half], jnp.concatenate([sent, sent_other], axis=0))
    cross_term = matmul(cross_input, next_decoder)
    second_part = jnp.where(leading, cross_term, own_term + cross_term)
    order.start(
        1, summed_steps(second_part, second_plan, feat_count, wanted_block(1, second_plan))
    )
    left = [len(plan) + len(plan) - 1 for plan in (first_plan, second_plan)]
    while left[1] > 0:
        for layer in (0, 1):
            if left[layer] > 0:
                order.advance(layer)
                left[layer] -= 1
    delta_first, delta_next = order.result(0), order.result(1)
    delta_own = jnp.where(leading, delta_first, delta_next)

    cross_back = over_cols(delta_next, next_decoder)
    cross_leaving = cross_back[part:].astype(jnp.bfloat16)
    cross_arriving = lax.ppermute(cross_leaving, ("feat", "width"), trailing_pairs)
    order.mark(cross_leaving)
    delta_own, cross_back = order.after((delta_own, cross_back))
    back_a = over_cols(delta_own, same_decoder[:half]) + jnp.where(leading, cross_back, 0.0)
    back_leaving = back_a[part:].astype(jnp.bfloat16)
    arriving_a = across(back_leaving)
    order.mark(back_leaving)
    delta_own, back_a = order.after((delta_own, back_a))
    back_b = over_cols(delta_own, same_decoder[half:])
    back_leaving = back_b[part:].astype(jnp.bfloat16)
    arriving_b = across(back_leaving)
    order.mark(back_leaving)
    next_done = adamw_matmul(
        order.after(cross_input), delta_next, next_decoder, next_first, next_second, weight_decay
    )
    order.mark(*next_done)
    kept_cross, cross_arriving = order.after((cross_back[:part], cross_arriving))
    cross_sum = add(kept_cross, cross_arriving).astype(jnp.bfloat16)
    returned = lax.ppermute(cross_sum, "feat", upward)
    order.mark(cross_sum)
    kept_a, arriving_a, pre_a = order.after((back_a[:part], arriving_a, pre_a))
    grad_a = jnp.where(pre_a > 0.0, add(kept_a, arriving_a), 0.0).astype(jnp.bfloat16)
    grad_other_a = across(grad_a)
    order.mark(grad_a)
    same_done = adamw_matmul(
        order.after(active), delta_own, same_decoder, same_first, same_second, weight_decay
    )
    order.mark(*same_done)
    kept_b, arriving_b, returned, pre_b = order.after((back_b[:part], arriving_b, returned, pre_b))
    total_b = add(add(kept_b, arriving_b), returned)
    grad_b = jnp.where(pre_b > 0.0, total_b, 0.0).astype(jnp.bfloat16)
    grad_other_b = across(grad_b)
    grad_sum = jnp.concatenate(
        [jnp.sum(grad.astype(jnp.float32), axis=0) for grad in (grad_a, grad_b)]
    )
    sum_other = across(grad_sum)
    order.mark(grad_b, grad_sum)
    grad_a, grad_other_a = order.after((grad_a, grad_other_a))
    encoder_done = adamw_matmul(
        inputs,
        jnp.concatenate([grad_a, grad_other_a], axis=0),
        encoder,
        encoder_first,
        encoder_second,
        weight_decay,
        (0, 2),
    )
    order.mark(*encoder_done)
    grad_b, grad_other_b, sum_other = order.after((grad_b, grad_other_b, sum_other))
    encoder_done = adamw_matmul(
        inputs,
        jnp.concatenate([grad_b, grad_other_b], axis=0),
        encoder,
        encoder_first,
        encoder_second,
        weight_decay,
        (1, 2),
        encoder_done,
    )
    grad_biases = grad_sum + sum_other
    updated_same, same_moment, same_square = same_done
    updated_next, next_moment, next_square = next_done
    updated_encoder, encoder_moment, encoder_square = encoder_done
    updated_biases, biases_moment, biases_square = adamw_update(
        biases, biases_first, biases_second, grad_biases, 0.0
    )
    return (
        updated_encoder,
        updated_biases,
        updated_same,
        updated_next,
        encoder_moment,
        encoder_square,
        biases_moment,
        biases_square,
        same_moment,
        same_square,
        next_moment,
        next_square,
    )


def solution(mesh):
    in_specs = (
        P(None, None, "width"),
        P(None, None, "width"),
        P("width", "feat"),
        P("feat"),
        P("feat", "width"),
        P("feat", "width"),
        P("width", "feat"),
        P("width", "feat"),
        P("feat"),
        P("feat"),
        P("feat", "width"),
        P("feat", "width"),
        P("feat", "width"),
        P("feat", "width"),
    )
    out_specs = (
        P("width", "feat"),
        P("feat"),
        P("feat", "width"),
        P("feat", "width"),
        P("width", "feat"),
        P("width", "feat"),
        P("feat"),
        P("feat"),
        P("feat", "width"),
        P("feat", "width"),
        P("feat", "width"),
        P("feat", "width"),
    )
    return jax.shard_map(local, mesh=mesh, in_specs=in_specs, out_specs=out_specs, check_vma=False)
```

time: 219 us -> 206 us (0.941)
  the two profiles are of different devices: /device:TPU:0 before, /device:TPU:20 now
where the time goes in v1:
time: 206 us; the launch traced here: 205 us
  waiting for transfers between devices  83 us (40%)
  Pallas kernels  49.3 us (24%)
  starting transfers between devices  31.6 us (15%)
  matrix products  21.4 us (10%)
  other arithmetic  9.86 us (5%)
  local copies, waits for them, and re-layouts  8.28 us (4%)
    pallas_call x4, Pallas kernels, adamw_matmul(): pl.pallas_call(functools.partial(adamw_kernel, decay_rate, tile), grid=(r...  49.3 us
    ppermute x9, waiting for transfers between devices, across(): return lax.ppermute(value, 'width', [(0, 1), (1, 0)])  38.8 us
    ppermute x12, waiting for transfers between devices, flipped(): lax.ppermute(value, 'feat', [(index, index ^ step) for index in range(mem...  35 us
    dot_general x5, matrix products, matmul(): return jnp.dot(left, right, preferred_element_type=jnp.float32)  15.9 us
    ppermute x12, starting transfers between devices, flipped(): lax.ppermute(value, 'feat', [(index, index ^ step) for index in range(mem...  12.2 us
    ppermute x9, starting transfers between devices, across(): return lax.ppermute(value, 'width', [(0, 1), (1, 0)])  9.7 us
    ppermute x1, waiting for transfers between devices, local(): sent_other = lax.ppermute(sent, ('feat', 'width'), trailing_pairs)  8.59 us
    dot_general x3, matrix products, over_cols(): lax.dot_general(left, right, (((1,), (1,)), ((), ())), preferred_element_...  5.56 us
  transfers between devices with their start and end apart: 25, of which 14 were waited for; matrix products, arithmetic and copies ran while one was open for 9% of the time, Pallas kernels for 18%

profile of v1, /device:TPU:20, one launch (start us, length us, event | category | flops | bytes accessed | tf_op | source)
XLA Modules:
  0.0 204.8 jit_solution(7705087234649237364)
XLA Ops:
  0.7 1.6 dynamic-slice_bitcast_fusion.1
  2.4 4.5 %fusion.4 = f32[448,1024]{1,0:T(8,128)S(1)} fusion(bf16[1792,2048]{1,0:T(8,128)(2,1)} %refs_2_.7, bf16[224,1792]{1,0:T(8,128)(2,1)S(1)} %get-tuple-element.147, bf16[224,1792]{1,0:T(8,128)(2,1)S(1)} %get-tuple-element.146), kind=kOutput, calls=%fused_computation.5 | convolution fusion | flops 1647378432 | bytes 7110656 | tf_op jit(solution)/shard_map/dot_general | solution.py:91
  7.0 1.6 collective-permute-start
  8.5 1.0 fusion.12
  9.5 0.6 collective-permute-start.2
  10.1 10.3 %collective-permute-done = f16[224,1024]{1,0:T(8,128)(2,1)S(1)} collective-permute-done((f16[224,1024]{1,0:T(8,128)(2,1)S(1)}, f16[224,1024]{1,0:T(8,128)(2,1)S(1)}, u32[]{:S(2)}, u32[]{:S(2)}) %collective-permute-start) | collective-permute-done | bytes 458784 | tf_op jit(solution)/shard_map/ppermute | solution.py:107
  20.6 1.3 collective-permute-start.1
  21.9 7.2 %collective-permute-done.2 = f16[224,1024]{1,0:T(8,128)(2,1)S(1)} collective-permute-done((f16[224,1024]{1,0:T(8,128)(2,1)S(1)}, f16[224,1024]{1,0:T(8,128)(2,1)S(1)}, u32[]{:S(2)}, u32[]{:S(2)}) %collective-permute-start.2) | collective-permute-done | bytes 458784 | tf_op jit(solution)/shard_map/ppermute | solution.py:107
  29.1 2.0 maximum_convert_fusion
  31.1 1.5 collective-permute-start.3
  32.6 0.5 collective-permute-start.4
  33.1 0.7 collective-permute-done.1
  33.8 10.8 %collective-permute-done.3 = bf16[224,1024]{1,0:T(8,128)(2,1)S(1)} collective-permute-done((bf16[224,1024]{1,0:T(8,128)(2,1)S(1)}, bf16[224,1024]{1,0:T(8,128)(2,1)S(1)}, u32[]{:S(2)}, u32[]{:S(2)}) %collective-permute-start.3) | collective-permute-done | bytes 458784 | tf_op jit(solution)/shard_map/ppermute | solution.py:107
  44.6 7.8 %collective-permute-done.4 = bf16[224,1024]{1,0:T(8,128)(2,1)S(1)} collective-permute-done((bf16[224,1024]{1,0:T(8,128)(2,1)S(1)}, bf16[224,1024]{1,0:T(8,128)(2,1)S(1)}, u32[]{:S(2)}, u32[]{:S(2)}) %collective-permute-start.4) | collective-permute-done | bytes 458784 | tf_op jit(solution)/shard_map/ppermute | solution.py:107
  52.3 6.6 %fusion.22 = f32[448,1792]{1,0:T(8,128)S(1)} fusion(bf16[2048,1792]{1,0:T(8,128)(2,1)} %refs_2_.5, bf16[224,1024]{1,0:T(8,128)(2,1)S(1)} %collective-permute-done.4, bf16[224,1024]{1,0:T(8,128)(2,1)S(1)} %collective-permute-done.3, bf16[224,1024]{1,0:T(8,128)(2,1)S(1)} %get-tuple-element.144, bf16[224,1024]{1,0:T(8,128)(2,1)S(1)} %get-tuple-element.73), kind=kOutput, calls=%fused_computation.77 | convolution fusion | flops 3295674368 | bytes 12386304 | tf_op jit(solution)/shard_map/dot_general | solution.py:91
  59.0 0.7 collective-permute-start.5
  59.7 3.4 %collective-permute-start.6 = (bf16[224,1024]{1,0:T(8,128)(2,1)S(1)}, bf16[224,1024]{1,0:T(8,128)(2,1)S(1)}, u32[]{:S(2)}, u32[]{:S(2)}) collective-permute-start(bf16[224,1024]{1,0:T(8,128)(2,1)S(1)} %collective-permute-done.1), channel_id=1, source_target_pairs={{16,17},{17,16},{18,19},{19,18},{20,21},{21,20},{22,23},{23,22},{2... | collective-permute-start | bytes 1376264 | tf_op jit(solution)/shard_map/ppermute | solution.py:255
  63.5 8.6 %collective-permute-done.6 = bf16[224,1024]{1,0:T(8,128)(2,1)S(1)} collective-permute-done((bf16[224,1024]{1,0:T(8,128)(2,1)S(1)}, bf16[224,1024]{1,0:T(8,128)(2,1)S(1)}, u32[]{:S(2)}, u32[]{:S(2)}) %collective-permute-start.6) | collective-permute-done | bytes 458784 | tf_op jit(solution)/shard_map/ppermute | solution.py:255
  72.1 0.3 slice_select_fusion.2.refs_0_
  72.5 1.8 fusion.27
  74.3 0.4 add_select_fusion
  75.4 0.7 collective-permute-start.7
  76.2 1.1 collective-permute-done.8
  77.5 0.6 collective-permute-start.10
  78.2 0.7 collective-permute-start.9
  79.0 9.9 %collective-permute-done.10 = bf16[112,1792]{1,0:T(8,128)(2,1)S(1)} collective-permute-done((bf16[112,1792]{1,0:T(8,128)(2,1)S(1)}, bf16[112,1792]{1,0:T(8,128)(2,1)S(1)}, u32[]{:S(2)}, u32[]{:S(2)}) %collective-permute-start.10) | collective-permute-done | bytes 401440 | tf_op jit(solution)/shard_map/ppermute | solution.py:112
  89.0 1.7 collective-permute-start.12
  90.7 1.2 fusion.16
  91.9 0.7 collective-permute-start.11
  92.6 2.7 %collective-permute-done.12 = bf16[112,896]{1,0:T(8,128)(2,1)S(1)} collective-permute-done((bf16[112,896]{1,0:T(8,128)(2,1)S(1)}, bf16[112,896]{1,0:T(8,128)(2,1)S(1)}, u32[]{:S(2)}, u32[]{:S(2)}) %collective-permute-start.12) | collective-permute-done | bytes 200736 | tf_op jit(solution)/shard_map/ppermute | solution.py:112
  95.4 3.3 %collective-permute-start.14 = (bf16[112,896]{1,0:T(8,128)(2,1)S(1)}, bf16[112,896]{1,0:T(8,128)(2,1)S(1)}, u32[]{:S(2)}, u32[]{:S(2)}) collective-permute-start(bf16[112,896]{1,0:T(8,128)(2,1)S(1)} %get-tuple-element.138), channel_id=1, source_target_pairs={{0,16},{2,18},{4,20},{6,22},{8,24},{10,26},{12,28},{14,30},{16,0},... | collective-permute-start | bytes 602120 | tf_op jit(solution)/shard_map/ppermute | solution.py:112
  98.8 5.8 %collective-permute-done.14 = bf16[112,896]{1,0:T(8,128)(2,1)S(1)} collective-permute-done((bf16[112,896]{1,0:T(8,128)(2,1)S(1)}, bf16[112,896]{1,0:T(8,128)(2,1)S(1)}, u32[]{:S(2)}, u32[]{:S(2)}) %collective-permute-start.14) | collective-permute-done | bytes 200736 | tf_op jit(solution)/shard_map/ppermute | solution.py:112
  104.6 1.1 fusion.17
  105.6 2.9 %collective-permute-start.15 = (bf16[112,896]{1,0:T(8,128)(2,1)S(1)}, bf16[112,896]{1,0:T(8,128)(2,1)S(1)}, u32[]{:S(2)}, u32[]{:S(2)}) collective-permute-start(bf16[112,896]{1,0:T(8,128)(2,1)S(1)} %fusion.17), channel_id=1, source_target_pairs={{0,8},{2,10},{4,12},{6,14},{8,0},{10,2},{12,4},{14,6},{16,24},{18,... | collective-permute-start | bytes 602120 | tf_op jit(solution)/shard_map/ppermute | solution.py:112
  108.5 4.4 %collective-permute-done.15 = bf16[112,896]{1,0:T(8,128)(2,1)S(1)} collective-permute-done((bf16[112,896]{1,0:T(8,128)(2,1)S(1)}, bf16[112,896]{1,0:T(8,128)(2,1)S(1)}, u32[]{:S(2)}, u32[]{:S(2)}) %collective-permute-start.15) | collective-permute-done | bytes 200736 | tf_op jit(solution)/shard_map/ppermute | solution.py:112
  113.1 0.9 collective-permute-start.13
  114.0 8.9 %collective-permute-done.16 = bf16[112,1792]{1,0:T(8,128)(2,1)S(1)} collective-permute-done((bf16[112,1792]{1,0:T(8,128)(2,1)S(1)}, bf16[112,1792]{1,0:T(8,128)(2,1)S(1)}, u32[]{:S(2)}, u32[]{:S(2)}) %collective-permute-start.16) | collective-permute-done | bytes 401440 | tf_op jit(solution)/shard_map/ppermute | solution.py:112
  123.4 2.1 %collective-permute-done.17 = bf16[224,1792]{1,0:T(8,128)(2,1)S(1)} collective-permute-done((bf16[224,1792]{1,0:T(8,128)(2,1)S(1)}, bf16[224,1792]{1,0:T(8,128)(2,1)S(1)}, u32[]{:S(2)}, u32[]{:S(2)}) %collective-permute-start.17) | collective-permute-done | bytes 802848 | tf_op jit(solution)/shard_map/ppermute | solution.py:112
  125.6 1.9 fusion.21
  127.5 0.9 slice.168
  128.3 3.4 %collective-permute-start.19 = (bf16[224,1024]{1,0:T(8,128)(2,1)}, bf16[224,1024]{1,0:T(8,128)(2,1)}, u32[]{:S(2)}, u32[]{:S(2)}) collective-permute-start(bf16[224,1024]{1,0:T(8,128)(2,1)} %slice.168), channel_id=1, source_target_pairs={{16,17},{17,16},{18,19},{19,18},{20,21},{21,20},{22,23},{23,22},{2... | collective-permute-start | bytes 1376264 | tf_op jit(solution)/shard_map/ppermute | solution.py:287
  131.8 0.5 pad_maximum_fusion.2
  132.4 1.9 select_add_fusion
  134.2 0.9 slice.167
  135.2 0.5 collective-permute-start.21
  135.7 1.8 fusion
  137.5 0.8 slice.166
  138.4 1.5 collective-permute-start.18
  139.9 0.5 copy-done.2
  140.5 7.9 %shard_map.229 = (bf16[1024,1792]{1,0:T(8,128)(2,1)}, bf16[1024,1792]{1,0:T(8,128)(2,1)}, bf16[1024,1792]{1,0:T(8,128)(2,1)}) custom-call(bf16[448,1024]{1,0:T(8,128)(2,1)S(1)} %slice_select_fusion.2.refs_0_, bf16[448,1792]{1,0:T(8,128)(2,1)S(1)} %get-tuple-element.148.refs_1_, bf16[1024,1792]{1,0:T(8,128)(2,1)S(1)} %copy-done.1, ...), custom_call_target="tpu_custom_call" | custom-call | flops 1644167168 | bytes 22020096 | tf_op jit(solution)/shard_map/pallas_call | solution.py:67
  148.3 1.1 add_convert_fusion
  149.5 1.5 collective-permute-start.20
  151.0 2.8 %collective-permute-done.21 = bf16[224,1024]{1,0:T(8,128)(2,1)} collective-permute-done((bf16[224,1024]{1,0:T(8,128)(2,1)}, bf16[224,1024]{1,0:T(8,128)(2,1)}, u32[]{:S(2)}, u32[]{:S(2)}) %collective-permute-start.21) | collective-permute-done | bytes 458784 | tf_op jit(solution)/shard_map/ppermute | solution.py:107
  153.7 1.4 convert_reduce_fusion.1
  155.2 1.6 collective-permute-start.24
  156.8 3.1 %copy-done = bf16[2048,1792]{1,0:T(8,128)(2,1)S(1)} copy-done((bf16[2048,1792]{1,0:T(8,128)(2,1)S(1)}, bf16[2048,1792]{1,0:T(8,128)(2,1)}, u32[]{:S(2)}) %copy-start) | copy-done | bytes 7340056
  159.9 18.5 %shard_map.230 = (bf16[2048,1792]{1,0:T(8,128)(2,1)}, bf16[2048,1792]{1,0:T(8,128)(2,1)}, bf16[2048,1792]{1,0:T(8,128)(2,1)}) custom-call(bf16[448,2048]{1,0:T(8,128)(2,1)S(1)} %maximum_maximum_fusion.refs_0_, bf16[448,1792]{1,0:T(8,128)(2,1)S(1)} %get-tuple-element.104.refs_1_, bf16[2048,1792]{1,0:T(8,128)(2,1)S(1)} %copy-done, bf16[2048,1792]{1,0:T(8,128)(2,1)} %refs_3_.5, ...), custom_call_target="tpu_custom_call" | custom-call | flops 3288334336 | bytes 44040192 | tf_op jit(solution)/shard_map/pallas_call | solution.py:67
  178.4 0.3 convert_reduce_fusion
  178.7 0.8 collective-permute-start.22
  179.5 0.2 copy-done.10
  179.9 1.1 collective-permute-start.23
  181.1 11.5 %shard_map.231 = (bf16[1792,2048]{1,0:T(8,128)(2,1)}, bf16[1792,2048]{1,0:T(8,128)(2,1)}, bf16[1792,2048]{1,0:T(8,128)(2,1)}) custom-call(bf16[448,1792]{1,0:T(8,128)(2,1)S(1)} %pad_maximum_fusion.refs_0_, bf16[448,1024]{1,0:T(8,128)(2,1)S(1)} %pad_maximum_fusion.3.refs_1_, bf16[1792,2048]{1,0:T(8,128)(2,1)S(1)} %bitcast.21, bf16[1792,2048]{1,0:T(8,128)(2,1)} %refs_3_.7, ...), custom_call_target="tpu_custom_call" | custom-call | flops 1644167168 | bytes 22020096 | tf_op jit(solution)/shard_map/pallas_call | solution.py:67
  192.7 11.5 %shard_map.232 = (bf16[1792,2048]{1,0:T(8,128)(2,1)}, bf16[1792,2048]{1,0:T(8,128)(2,1)}, bf16[1792,2048]{1,0:T(8,128)(2,1)}) custom-call(bf16[448,1792]{1,0:T(8,128)(2,1)S(1)} %pad_maximum_fusion.refs_0_, bf16[448,1024]{1,0:T(8,128)(2,1)S(1)} %pad_maximum_fusion.4.refs_1_, ...), custom_call_target="tpu_custom_call", output_to_operand_aliasing={{0}: (5, {}), {1}: (6, {}), {2}: (7, {})} | custom-call | flops 1644167168 | bytes 22020096 | tf_op jit(solution)/shard_map/pallas_call | solution.py:67
  204.2 0.6 fusion.20
  (93 shorter events, 3.3 us)
Async XLA Ops:
  0.7 7.9 %slice-start = ((s8[7340032]{0:T(1024)(128)(4,1)}), s8[4194304]{0:T(1024)(128)(4,1)S(1)}, s32[]{:S(2)}) async-start(s8[7340032]{0:T(1024)(128)(4,1)} %bitcast.18), calls=%async_computation | async-start | bytes 8388608
  2.3 6.2 %copy-start.9 = (bf16[224,1792]{1,0:T(8,128)(2,1)}, bf16[224,1792]{1,0:T(8,128)(2,1)S(1)}, u32[]{:S(2)}) copy-start(bf16[224,1792]{1,0:T(8,128)(2,1)S(1)} %get-tuple-element.147) | copy-start | bytes 2408452
  2.3 26.8 %copy-start.7 = (bf16[224,1792]{1,0:T(8,128)(2,1)}, bf16[224,1792]{1,0:T(8,128)(2,1)S(1)}, u32[]{:S(2)}) copy-start(bf16[224,1792]{1,0:T(8,128)(2,1)S(1)} %get-tuple-element.146) | copy-start | bytes 2408452
  2.3 6.2 %slice-start.1 = ((s8[7340032]{0:T(1024)(128)(4,1)}), s8[3145728]{0:T(1024)(128)(4,1)S(1)}, s32[]{:S(2)}) async-start(s8[7340032]{0:T(1024)(128)(4,1)} %bitcast.18), calls=%async_computation.1 | async-start | bytes 6291456
  7.0 3.2 %copy-start.12 = (bf16[2048]{0:T(1024)(128)(2,1)S(1)}, bf16[2048]{0:T(1024)(128)(2,1)}, u32[]{:S(2)}) copy-start(bf16[2048]{0:T(1024)(128)(2,1)} %param.17) | copy-start | bytes 12292
  7.0 13.5 %collective-permute-start = (f16[224,1024]{1,0:T(8,128)(2,1)S(1)}, f16[224,1024]{1,0:T(8,128)(2,1)S(1)}, u32[]{:S(2)}, u32[]{:S(2)}) collective-permute-start(f16[224,1024]{1,0:T(8,128)(2,1)S(1)} %slice_convert_fusion.3), channel_id=1, source_target_pairs={{0,1},{1,0},{2,3},{3,2},{4,5},{5,4},{6,7},{7,6},{8,9},{9,8},{10,11... | collective-permute-start | bytes 1376264 | tf_op jit(solution)/shard_map/ppermute | solution.py:107
  9.5 19.6 %collective-permute-start.2 = (f16[224,1024]{1,0:T(8,128)(2,1)S(1)}, f16[224,1024]{1,0:T(8,128)(2,1)S(1)}, u32[]{:S(2)}, u32[]{:S(2)}) collective-permute-start(f16[224,1024]{1,0:T(8,128)(2,1)S(1)} %fusion.12), channel_id=1, source_target_pairs={{0,1},{1,0},{2,3},{3,2},{4,5},{5,4},{6,7},{7,6},{8,9},{9,8},{10,11... | collective-permute-start | bytes 1376264 | tf_op jit(solution)/shard_map/ppermute | solution.py:107
  20.6 13.1 %collective-permute-start.1 = (bf16[224,1024]{1,0:T(8,128)(2,1)S(1)}, bf16[224,1024]{1,0:T(8,128)(2,1)S(1)}, u32[]{:S(2)}, u32[]{:S(2)}) collective-permute-start(bf16[224,1024]{1,0:T(8,128)(2,1)S(1)} %get-tuple-element.144), channel_id=1, source_target_pairs={{0,16},{2,18},{4,20},{6,22},{8,24},{10,26},{12,28},{14,30},{1,17},... | collective-permute-start | bytes 1376264 | tf_op jit(solution)/shard_map/ppermute | solution.py:254
  31.1 13.5 %collective-permute-start.3 = (bf16[224,1024]{1,0:T(8,128)(2,1)S(1)}, bf16[224,1024]{1,0:T(8,128)(2,1)S(1)}, u32[]{:S(2)}, u32[]{:S(2)}) collective-permute-start(bf16[224,1024]{1,0:T(8,128)(2,1)S(1)} %get-tuple-element.73), channel_id=1, source_target_pairs={{0,1},{1,0},{2,3},{3,2},{4,5},{5,4},{6,7},{7,6},{8,9},{9,8},{10,11... | collective-permute-start | bytes 1376264 | tf_op jit(solution)/shard_map/ppermute | solution.py:107
  32.6 19.7 %collective-permute-start.4 = (bf16[224,1024]{1,0:T(8,128)(2,1)S(1)}, bf16[224,1024]{1,0:T(8,128)(2,1)S(1)}, u32[]{:S(2)}, u32[]{:S(2)}) collective-permute-start(bf16[224,1024]{1,0:T(8,128)(2,1)S(1)} %get-tuple-element.144), channel_id=1, source_target_pairs={{0,1},{1,0},{2,3},{3,2},{4,5},{5,4},{6,7},{7,6},{8,9},{9,8},{10,11... | collective-permute-start | bytes 1376264 | tf_op jit(solution)/shard_map/ppermute | solution.py:107
  59.0 16.1 %collective-permute-start.5 = (bf16[224,1792]{1,0:T(8,128)(2,1)S(1)}, bf16[224,1792]{1,0:T(8,128)(2,1)S(1)}, u32[]{:S(2)}, u32[]{:S(2)}) collective-permute-start(bf16[224,1792]{1,0:T(8,128)(2,1)S(1)} %select_convert_fusion.1), channel_id=1, source_target_pairs={{0,2},{2,0},{4,6},{6,4},{8,10},{10,8},{12,14},{14,12},{1,3},{3,1},... | collective-permute-start | bytes 2408456 | tf_op jit(solution)/shard_map/ppermute | solution.py:112
  59.7 12.4 %collective-permute-start.6 = (bf16[224,1024]{1,0:T(8,128)(2,1)S(1)}, bf16[224,1024]{1,0:T(8,128)(2,1)S(1)}, u32[]{:S(2)}, u32[]{:S(2)}) collective-permute-start(bf16[224,1024]{1,0:T(8,128)(2,1)S(1)} %collective-permute-done.1), channel_id=1, source_target_pairs={{16,17},{17,16},{18,19},{19,18},{20,21},{21,20},{22,23},{23,22},{2... | collective-permute-start | bytes 1376264 | tf_op jit(solution)/shard_map/ppermute | solution.py:255
  63.3 9.1 %copy-start.1 = (bf16[1024,1792]{1,0:T(8,128)(2,1)S(1)}, bf16[1024,1792]{1,0:T(8,128)(2,1)}, u32[]{:S(2)}) copy-start(bf16[1024,1792]{1,0:T(8,128)(2,1)} %refs_2_.4) | copy-start | bytes 11010052
  74.9 2.4 %collective-permute-start.8 = (bf16[224,1792]{1,0:T(8,128)(2,1)S(1)}, bf16[224,1792]{1,0:T(8,128)(2,1)S(1)}, u32[]{:S(2)}, u32[]{:S(2)}) collective-permute-start(bf16[224,1792]{1,0:T(8,128)(2,1)S(1)} %select_convert_fusion), channel_id=1, source_target_pairs={{0,2},{2,0},{4,6},{6,4},{8,10},{10,8},{12,14},{14,12},{16,18},{18,... | collective-permute-start | bytes 2408456 | tf_op jit(solution)/shard_map/ppermute | solution.py:112
  75.4 2.7 %collective-permute-start.7 = (bf16[112,1792]{1,0:T(8,128)(2,1)S(1)}, bf16[112,1792]{1,0:T(8,128)(2,1)S(1)}, u32[]{:S(2)}, u32[]{:S(2)}) collective-permute-start(bf16[112,1792]{1,0:T(8,128)(2,1)S(1)} %select_convert_fusion.5), channel_id=1, source_target_pairs={{0,4},{2,6},{4,0},{6,2},{8,12},{10,14},{12,8},{14,10},{1,5},{3,7},... | collective-permute-start | bytes 1204232 | tf_op jit(solution)/shard_map/ppermute | solution.py:112
  77.5 11.4 %collective-permute-start.10 = (bf16[112,1792]{1,0:T(8,128)(2,1)S(1)}, bf16[112,1792]{1,0:T(8,128)(2,1)S(1)}, u32[]{:S(2)}, u32[]{:S(2)}) collective-permute-start(bf16[112,1792]{1,0:T(8,128)(2,1)S(1)} %select_convert_fusion.4), channel_id=1, source_target_pairs={{0,4},{2,6},{4,0},{6,2},{8,12},{10,14},{12,8},{14,10},{16,20},{18,... | collective-permute-start | bytes 1204232 | tf_op jit(solution)/shard_map/ppermute | solution.py:112
  78.2 12.5 %collective-permute-start.9 = (bf16[112,1792]{1,0:T(8,128)(2,1)S(1)}, bf16[112,1792]{1,0:T(8,128)(2,1)S(1)}, u32[]{:S(2)}, u32[]{:S(2)}) collective-permute-start(bf16[112,1792]{1,0:T(8,128)(2,1)S(1)} %get-tuple-element.140), channel_id=1, source_target_pairs={{0,8},{2,10},{4,12},{6,14},{8,0},{10,2},{12,4},{14,6},{1,9},{3,11}... | collective-permute-start | bytes 1204232 | tf_op jit(solution)/shard_map/ppermute | solution.py:112
  89.0 6.3 %collective-permute-start.12 = (bf16[112,896]{1,0:T(8,128)(2,1)S(1)}, bf16[112,896]{1,0:T(8,128)(2,1)S(1)}, u32[]{:S(2)}, u32[]{:S(2)}) collective-permute-start(bf16[112,896]{1,0:T(8,128)(2,1)S(1)} %select_convert_fusion.6), channel_id=1, source_target_pairs={{0,8},{2,10},{4,12},{6,14},{8,0},{10,2},{12,4},{14,6},{16,24},{18,... | collective-permute-start | bytes 602120 | tf_op jit(solution)/shard_map/ppermute | solution.py:112
  91.9 6.8 %collective-permute-start.11 = (bf16[112,1792]{1,0:T(8,128)(2,1)S(1)}, bf16[112,1792]{1,0:T(8,128)(2,1)S(1)}, u32[]{:S(2)}, u32[]{:S(2)}) collective-permute-start(bf16[112,1792]{1,0:T(8,128)(2,1)S(1)} %fusion.16), channel_id=1, source_target_pairs={{0,4},{2,6},{4,0},{6,2},{8,12},{10,14},{12,8},{14,10},{1,5},{3,7},... | collective-permute-start | bytes 1204232 | tf_op jit(solution)/shard_map/ppermute | solution.py:112
  95.4 9.2 %collective-permute-start.14 = (bf16[112,896]{1,0:T(8,128)(2,1)S(1)}, bf16[112,896]{1,0:T(8,128)(2,1)S(1)}, u32[]{:S(2)}, u32[]{:S(2)}) collective-permute-start(bf16[112,896]{1,0:T(8,128)(2,1)S(1)} %get-tuple-element.138), channel_id=1, source_target_pairs={{0,16},{2,18},{4,20},{6,22},{8,24},{10,26},{12,28},{14,30},{16,0},... | collective-permute-start | bytes 602120 | tf_op jit(solution)/shard_map/ppermute | solution.py:112
  105.6 7.3 %collective-permute-start.15 = (bf16[112,896]{1,0:T(8,128)(2,1)S(1)}, bf16[112,896]{1,0:T(8,128)(2,1)S(1)}, u32[]{:S(2)}, u32[]{:S(2)}) collective-permute-start(bf16[112,896]{1,0:T(8,128)(2,1)S(1)} %fusion.17), channel_id=1, source_target_pairs={{0,8},{2,10},{4,12},{6,14},{8,0},{10,2},{12,4},{14,6},{16,24},{18,... | collective-permute-start | bytes 602120 | tf_op jit(solution)/shard_map/ppermute | solution.py:112
  113.0 9.9 %collective-permute-start.16 = (bf16[112,1792]{1,0:T(8,128)(2,1)S(1)}, bf16[112,1792]{1,0:T(8,128)(2,1)S(1)}, u32[]{:S(2)}, u32[]{:S(2)}) collective-permute-start(bf16[112,1792]{1,0:T(8,128)(2,1)S(1)} %pad_maximum_fusion.7), channel_id=1, source_target_pairs={{0,4},{2,6},{4,0},{6,2},{8,12},{10,14},{12,8},{14,10},{16,20},{18,... | collective-permute-start | bytes 1204232 | tf_op jit(solution)/shard_map/ppermute | solution.py:112
  113.1 10.1 %collective-permute-start.13 = (bf16[224,1792]{1,0:T(8,128)(2,1)S(1)}, bf16[224,1792]{1,0:T(8,128)(2,1)S(1)}, u32[]{:S(2)}, u32[]{:S(2)}) collective-permute-start(bf16[224,1792]{1,0:T(8,128)(2,1)S(1)} %pad_maximum_fusion.5), channel_id=1, source_target_pairs={{0,2},{2,0},{4,6},{6,4},{8,10},{10,8},{12,14},{14,12},{1,3},{3,1},... | collective-permute-start | bytes 2408456 | tf_op jit(solution)/shard_map/ppermute | solution.py:112
  123.1 2.4 %collective-permute-start.17 = (bf16[224,1792]{1,0:T(8,128)(2,1)S(1)}, bf16[224,1792]{1,0:T(8,128)(2,1)S(1)}, u32[]{:S(2)}, u32[]{:S(2)}) collective-permute-start(bf16[224,1792]{1,0:T(8,128)(2,1)S(1)} %pad_maximum_fusion.6), channel_id=1, source_target_pairs={{0,2},{2,0},{4,6},{6,4},{8,10},{10,8},{12,14},{14,12},{16,18},{18,... | collective-permute-start | bytes 2408456 | tf_op jit(solution)/shard_map/ppermute | solution.py:112
  125.5 6.8 %slice-start.4 = ((s8[7340032]{0:T(1024)(128)(4,1)}), s8[4194304]{0:T(1024)(128)(4,1)S(1)}, s32[]{:S(2)}) async-start(s8[7340032]{0:T(1024)(128)(4,1)} %bitcast.22), calls=%async_computation.4 | async-start | bytes 8388608
  125.6 6.7 %slice-start.5 = ((s8[7340032]{0:T(1024)(128)(4,1)}), s8[3145728]{0:T(1024)(128)(4,1)S(1)}, s32[]{:S(2)}) async-start(s8[7340032]{0:T(1024)(128)(4,1)} %bitcast.22), calls=%async_computation.5 | async-start | bytes 6291456
  127.5 10.1 %copy-start.4 = (f32[448,1024]{1,0:T(8,128)}, f32[448,1024]{1,0:T(8,128)S(1)}, u32[]{:S(2)}) copy-start(f32[448,1024]{1,0:T(8,128)S(1)} %fusion.21) | copy-start | bytes 5505028
  128.3 20.0 %collective-permute-start.19 = (bf16[224,1024]{1,0:T(8,128)(2,1)}, bf16[224,1024]{1,0:T(8,128)(2,1)}, u32[]{:S(2)}, u32[]{:S(2)}) collective-permute-start(bf16[224,1024]{1,0:T(8,128)(2,1)} %slice.168), channel_id=1, source_target_pairs={{16,17},{17,16},{18,19},{19,18},{20,21},{21,20},{22,23},{23,22},{2... | collective-permute-start | bytes 1376264 | tf_op jit(solution)/shard_map/ppermute | solution.py:287
  134.2 5.7 %copy-start.6 = (f32[448,1024]{1,0:T(8,128)}, f32[448,1024]{1,0:T(8,128)S(1)}, u32[]{:S(2)}) copy-start(f32[448,1024]{1,0:T(8,128)S(1)} %select_add_fusion) | copy-start | bytes 5505028
  135.2 18.5 %collective-permute-start.21 = (bf16[224,1024]{1,0:T(8,128)(2,1)}, bf16[224,1024]{1,0:T(8,128)(2,1)}, u32[]{:S(2)}, u32[]{:S(2)}) collective-permute-start(bf16[224,1024]{1,0:T(8,128)(2,1)} %slice.167), channel_id=1, source_target_pairs={{0,1},{1,0},{2,3},{3,2},{4,5},{5,4},{6,7},{7,6},{8,9},{9,8},{10,11... | collective-permute-start | bytes 1376264 | tf_op jit(solution)/shard_map/ppermute | solution.py:107
  135.7 4.3 %copy-start.3 = (bf16[1024,1792]{1,0:T(8,128)(2,1)S(1)}, bf16[1024,1792]{1,0:T(8,128)(2,1)}, u32[]{:S(2)}) copy-start(bf16[1024,1792]{1,0:T(8,128)(2,1)} %refs_4_.4) | copy-start | bytes 11010052
  137.5 2.4 %copy-start.5 = (f32[448,1024]{1,0:T(8,128)}, f32[448,1024]{1,0:T(8,128)S(1)}, u32[]{:S(2)}) copy-start(f32[448,1024]{1,0:T(8,128)S(1)} %fusion) | copy-start | bytes 5505028
  137.5 2.9 %copy-start.2 = (bf16[1024,1792]{1,0:T(8,128)(2,1)S(1)}, bf16[1024,1792]{1,0:T(8,128)(2,1)}, u32[]{:S(2)}) copy-start(bf16[1024,1792]{1,0:T(8,128)(2,1)} %refs_3_.4) | copy-start | bytes 11010052
  138.4 40.0 %collective-permute-start.18 = (bf16[224,1024]{1,0:T(8,128)(2,1)}, bf16[224,1024]{1,0:T(8,128)(2,1)S(1)}, u32[]{:S(2)}, u32[]{:S(2)}) collective-permute-start(bf16[224,1024]{1,0:T(8,128)(2,1)} %slice.166), channel_id=1, source_target_pairs={{0,1},{1,0},{2,3},{3,2},{4,5},{5,4},{6,7},{7,6},{8,9},{9,8},{10,11... | collective-permute-start | bytes 1376264 | tf_op jit(solution)/shard_map/ppermute | solution.py:107
  140.4 7.9 %slice-start.6 = ((f32[448,1024]{1,0:T(8,128)}), f32[224,1024]{1,0:T(8,128)S(1)}, s32[]{:S(2)}) async-start(f32[448,1024]{1,0:T(8,128)} %copy-done.4), calls=%async_computation.6 | async-start | bytes 1835008 | tf_op jit(solution)/shard_map/slice | solution.py:303
  140.4 13.3 %slice-start.8 = ((f32[448,1024]{1,0:T(8,128)}), f32[224,1024]{1,0:T(8,128)S(1)}, s32[]{:S(2)}) async-start(f32[448,1024]{1,0:T(8,128)} %copy-done.6), calls=%async_computation.8 | async-start | bytes 1835008 | tf_op jit(solution)/shard_map/slice | solution.py:307
  140.4 13.3 %copy-start.11 = (f32[224,1024]{1,0:T(8,128)S(1)}, f32[224,1024]{1,0:T(8,128)}, u32[]{:S(2)}) copy-start(f32[224,1024]{1,0:T(8,128)} %get-tuple-element.112) | copy-start | bytes 2752516
  149.5 28.9 %collective-permute-start.20 = (bf16[224,1024]{1,0:T(8,128)(2,1)S(1)}, bf16[224,1024]{1,0:T(8,128)(2,1)S(1)}, u32[]{:S(2)}, u32[]{:S(2)}) collective-permute-start(bf16[224,1024]{1,0:T(8,128)(2,1)S(1)} %add_convert_fusion), channel_id=1, source_target_pairs={{16,0},{18,2},{20,4},{22,6},{24,8},{26,10},{28,12},{30,14},{17,1},... | collective-permute-start | bytes 1376264 | tf_op jit(solution)/shard_map/ppermute | solution.py:305
  153.7 27.3 %slice-start.2 = ((s8[7340032]{0:T(1024)(128)(4,1)}), s8[4194304]{0:T(1024)(128)(4,1)S(1)}, s32[]{:S(2)}) async-start(s8[7340032]{0:T(1024)(128)(4,1)} %bitcast.20), calls=%async_computation.2 | async-start | bytes 8388608
  155.1 25.9 %slice-start.3 = ((s8[7340032]{0:T(1024)(128)(4,1)}), s8[3145728]{0:T(1024)(128)(4,1)S(1)}, s32[]{:S(2)}) async-start(s8[7340032]{0:T(1024)(128)(4,1)} %bitcast.20), calls=%async_computation.3 | async-start | bytes 6291456
  155.2 25.8 %collective-permute-start.24 = (bf16[224,1024]{1,0:T(8,128)(2,1)S(1)}, bf16[224,1024]{1,0:T(8,128)(2,1)S(1)}, u32[]{:S(2)}, u32[]{:S(2)}) collective-permute-start(bf16[224,1024]{1,0:T(8,128)(2,1)S(1)} %get-tuple-element.123), channel_id=1, source_target_pairs={{0,1},{1,0},{2,3},{3,2},{4,5},{5,4},{6,7},{7,6},{8,9},{9,8},{10,11... | collective-permute-start | bytes 1376264 | tf_op jit(solution)/shard_map/ppermute | solution.py:107
  156.8 3.1 %copy-start = (bf16[2048,1792]{1,0:T(8,128)(2,1)S(1)}, bf16[2048,1792]{1,0:T(8,128)(2,1)}, u32[]{:S(2)}) copy-start(bf16[2048,1792]{1,0:T(8,128)(2,1)} %refs_2_.5) | copy-start | bytes 22020100
  159.9 18.5 %slice-start.7 = ((f32[448,1024]{1,0:T(8,128)}), f32[224,1024]{1,0:T(8,128)S(1)}, s32[]{:S(2)}) async-start(f32[448,1024]{1,0:T(8,128)} %copy-done.5), calls=%async_computation.7 | async-start | bytes 1835008 | tf_op jit(solution)/shard_map/slice | solution.py:315
  178.4 1.1 copy-start.8
  178.4 1.4 copy-start.10
  178.7 13.9 %collective-permute-start.22 = (bf16[224,1024]{1,0:T(8,128)(2,1)S(1)}, bf16[224,1024]{1,0:T(8,128)(2,1)S(1)}, u32[]{:S(2)}, u32[]{:S(2)}) collective-permute-start(bf16[224,1024]{1,0:T(8,128)(2,1)S(1)} %get-tuple-element.128), channel_id=1, source_target_pairs={{0,1},{1,0},{2,3},{3,2},{4,5},{5,4},{6,7},{7,6},{8,9},{9,8},{10,11... | collective-permute-start | bytes 1376264 | tf_op jit(solution)/shard_map/ppermute | solution.py:107
  179.9 12.7 %collective-permute-start.23 = (f32[2048]{0:T(1024)S(1)}, f32[2048]{0:T(1024)S(1)}, u32[]{:S(2)}, u32[]{:S(2)}) collective-permute-start(f32[2048]{0:T(1024)S(1)} %pad_maximum_fusion.8), channel_id=1, source_target_pairs={{0,1},{1,0},{2,3},{3,2},{4,5},{5,4},{6,7},{7,6},{8,9},{9,8},{10,11... | collective-permute-start | bytes 24584 | tf_op jit(solution)/shard_map/ppermute | solution.py:107
  192.6 11.5 %copy-start.13 = (bf16[2048]{0:T(1024)(128)(2,1)S(1)}, bf16[2048]{0:T(1024)(128)(2,1)}, u32[]{:S(2)}) copy-start(bf16[2048]{0:T(1024)(128)(2,1)} %param.23) | copy-start | bytes 12292
  192.7 11.5 %copy-start.14 = (bf16[2048]{0:T(1024)(128)(2,1)S(1)}, bf16[2048]{0:T(1024)(128)(2,1)}, u32[]{:S(2)}) copy-start(bf16[2048]{0:T(1024)(128)(2,1)} %param.22) | copy-start | bytes 12292

commit v2 on v1

--- a/solution.py
+++ b/solution.py
@@ -60,8 +60,8 @@
 def adamw_matmul(left, right, weight, first, second, decay_rate, share=(0, 1), partly_done=()):
     tokens = left.shape[0]
     rows, width = weight.shape
-    block = math.gcd(rows, 256)
     span = width // share[1]
+    block = math.gcd(rows, 256 if span <= 1024 else 128)
     tile = math.gcd(span, 256)
     strip = pl.BlockSpec((block, span), lambda place: (place, share[0]))
     return pl.pallas_call(
@@ -69,7 +69,7 @@
         grid=(rows // block,),
         in_specs=[
             pl.BlockSpec((tokens, block), lambda place: (0, place)),
-            pl.BlockSpec((tokens, span), lambda place: (0, 0)),
+            pl.BlockSpec((tokens, span), lambda place: (0, 0), pipeline_mode=pl.Buffered(1)),
             strip,
             strip,
             strip,
@@ -78,7 +78,7 @@
         out_specs=[strip] * 3,
         out_shape=[jax.ShapeDtypeStruct((rows, width), jnp.bfloat16)] * 3,
         input_output_aliases={5 + at: at for at in range(len(partly_done))},
-        compiler_params=pltpu.CompilerParams(vmem_limit_bytes=40 * 2**20),
+        compiler_params=pltpu.CompilerParams(vmem_limit_bytes=14 * 2**20),
         cost_estimate=pl.CostEstimate(
             flops=2 * tokens * rows * span,
             bytes_accessed=12 * rows * span,
@@ -262,11 +262,12 @@
         [jnp.concatenate([act_a, act_b], axis=1), jnp.concatenate([other_a, other_b], axis=1)],
         axis=0,
     )
+    active = lax.optimization_barrier(active)
     own_term = matmul(active, same_decoder)
+    sent_other, own_term, sent = lax.optimization_barrier((sent_other, own_term, sent))
     order.start(
         0, summed_steps(own_term, first_plan, half_count, wanted_block(0, first_plan))
     )
-    sent_other, own_term, sent = order.after((sent_other, own_term, sent))
     cross_input = jnp.where(leading, active[:, :half], jnp.concatenate([sent, sent_other], axis=0))
     cross_term = matmul(cross_input, next_decoder)
     second_part = jnp.where(leading, cross_term, own_term + cross_term)
@@ -282,29 +283,29 @@
     delta_first, delta_next = order.result(0), order.result(1)
     delta_own = jnp.where(leading, delta_first, delta_next)
 
-    cross_back = over_cols(delta_next, next_decoder)
-    cross_leaving = cross_back[part:].astype(jnp.bfloat16)
-    cross_arriving = lax.ppermute(cross_leaving, ("feat", "width"), trailing_pairs)
-    order.mark(cross_leaving)
-    delta_own, cross_back = order.after((delta_own, cross_back))
-    back_a = over_cols(delta_own, same_decoder[:half]) + jnp.where(leading, cross_back, 0.0)
-    back_leaving = back_a[part:].astype(jnp.bfloat16)
-    arriving_a = across(back_leaving)
-    order.mark(back_leaving)
-    delta_own, back_a = order.after((delta_own, back_a))
-    back_b = over_cols(delta_own, same_decoder[half:])
-    back_leaving = back_b[part:].astype(jnp.bfloat16)
-    arriving_b = across(back_leaving)
-    order.mark(back_leaving)
-    next_done = adamw_matmul(
-        order.after(cross_input), delta_next, next_decoder, next_first, next_second, weight_decay
-    )
-    order.mark(*next_done)
-    kept_cross, cross_arriving = order.after((cross_back[:part], cross_arriving))
+    def back_parts(rows, delta_own, delta_next):
+        cross = over_cols(delta_next[rows], next_decoder)
+        back = over_cols(delta_own[rows], same_decoder[:half]) + jnp.where(leading, cross, 0.0)
+        return cross, back, over_cols(delta_own[rows], same_decoder[half:])
+
+    leaving = [
+        block.astype(jnp.bfloat16) for block in back_parts(slice(part, None), delta_own, delta_next)
+    ]
+    cross_arriving = lax.ppermute(leaving[0], ("feat", "width"), trailing_pairs)
+    arriving_a, arriving_b = across(leaving[1]), across(leaving[2])
+    order.mark(*leaving)
+    delta_own, delta_next = order.after((delta_own, delta_next))
+    kept_cross, kept_a, kept_b = back_parts(slice(0, part), delta_own, delta_next)
+    order.mark(kept_cross, kept_a, kept_b)
+    kept_cross, cross_arriving = order.after((kept_cross, cross_arriving))
     cross_sum = add(kept_cross, cross_arriving).astype(jnp.bfloat16)
     returned = lax.ppermute(cross_sum, "feat", upward)
     order.mark(cross_sum)
-    kept_a, arriving_a, pre_a = order.after((back_a[:part], arriving_a, pre_a))
+    next_done = adamw_matmul(
+        order.after(cross_input), delta_next, next_decoder, next_first, next_second, weight_decay
+    )
+    order.mark(*next_done)
+    kept_a, arriving_a, pre_a = order.after((kept_a, arriving_a, pre_a))
     grad_a = jnp.where(pre_a > 0.0, add(kept_a, arriving_a), 0.0).astype(jnp.bfloat16)
     grad_other_a = across(grad_a)
     order.mark(grad_a)
@@ -312,7 +313,7 @@
         order.after(active), delta_own, same_decoder, same_first, same_second, weight_decay
     )
     order.mark(*same_done)
-    kept_b, arriving_b, returned, pre_b = order.after((back_b[:part], arriving_b, returned, pre_b))
+    kept_b, arriving_b, returned, pre_b = order.after((kept_b, arriving_b, returned, pre_b))
     total_b = add(add(kept_b, arriving_b), returned)
     grad_b = jnp.where(pre_b > 0.0, total_b, 0.0).astype(jnp.bfloat16)
     grad_other_b = across(grad_b)

time: 206 us -> 205 us (level)
  Pallas kernels: 49.3 us -> 42.2 us
  waiting for transfers between devices: 83 us -> 78.7 us
  matrix products: 21.4 us -> 25.6 us
  starting transfers between devices: 31.6 us -> 35.5 us
    pallas_call x4, Pallas kernels: 49.3 us -> 42.2 us  [adamw_matmul(): pl.pallas_call(functools.partial(adamw_kernel, decay_rate, tile), grid=(r...]
    ppermute x1, waiting for transfers between devices: 8.59 us -> 2.69 us  [local(): sent_other = lax.ppermute(sent, ('feat', 'width'), trailing_pairs)]
    ppermute x1, waiting for transfers between devices: 0.01 us -> 5.11 us  [local(): cross_arriving = lax.ppermute(leaving[0], ('feat', 'width'), trailing_pairs)]
    unnamed x42 -> x50, local copies, waits for them, and re-layouts: 3.98 us -> 8.62 us
    dot_general x3 -> x6, matrix products: 5.56 us -> 9.86 us  [over_cols(): lax.dot_general(left, right, (((1,), (1,)), ((), ())), preferred_element_...]
    ppermute x12, starting transfers between devices: 12.2 us -> 16.4 us  [flipped(): lax.ppermute(value, 'feat', [(index, index ^ step) for index in range(mem...]
    slice x9 -> x0, local copies, waits for them, and re-layouts: 2.65 us -> none  [the longest x1 0.95 us: local(): back_leaving = back_a[part:].astype(jnp.bfloat16)]
    ppermute x9, waiting for transfers between devices: 38.8 us -> 36.2 us  [across(): return lax.ppermute(value, 'width', [(0, 1), (1, 0)])]
  transfers between devices with their start and end apart: 25 -> 25, of which waited for: 14 -> 14; matrix products, arithmetic and copies ran while one was open for 9% -> 11% of each run, Pallas kernels for 18% -> 16%
where the time goes in v2:
time: 205 us
  waiting for transfers between devices  78.7 us (38%)
  Pallas kernels  42.2 us (21%)
  starting transfers between devices  35.5 us (17%)
  matrix products  25.6 us (12%)
  other arithmetic  10.9 us (5%)
  local copies, waits for them, and re-layouts  10.3 us (5%)
    pallas_call x4, Pallas kernels, adamw_matmul(): pl.pallas_call(functools.partial(adamw_kernel, decay_rate, tile), grid=(r...  42.2 us
    ppermute x9, waiting for transfers between devices, across(): return lax.ppermute(value, 'width', [(0, 1), (1, 0)])  36.2 us
    ppermute x12, waiting for transfers between devices, flipped(): lax.ppermute(value, 'feat', [(index, index ^ step) for index in range(mem...  34 us
    ppermute x12, starting transfers between devices, flipped(): lax.ppermute(value, 'feat', [(index, index ^ step) for index in range(mem...  16.4 us
    dot_general x5, matrix products, matmul(): return jnp.dot(left, right, preferred_element_type=jnp.float32)  15.7 us
    dot_general x6, matrix products, over_cols(): lax.dot_general(left, right, (((1,), (1,)), ((), ())), preferred_element_...  9.86 us
    ppermute x9, starting transfers between devices, across(): return lax.ppermute(value, 'width', [(0, 1), (1, 0)])  9.47 us
    unnamed x50, local copies, waits for them, and re-layouts  8.62 us
  transfers between devices with their start and end apart: 25, of which 14 were waited for; matrix products, arithmetic and copies ran while one was open for 11% of the time, Pallas kernels for 16%

profile of v2, /device:TPU:20, one launch (start us, length us, event | category | flops | bytes accessed | tf_op | source)
XLA Modules:
  0.0 204.6 jit_solution(1383572043567984329)
XLA Ops:
  0.7 1.6 dynamic-slice_bitcast_fusion.1
  2.4 4.3 %fusion = f32[448,1024]{1,0:T(8,128)S(1)} fusion(bf16[1792,2048]{1,0:T(8,128)(2,1)} %refs_2_.7, bf16[224,1792]{1,0:T(8,128)(2,1)S(1)} %get-tuple-element.143, bf16[224,1792]{1,0:T(8,128)(2,1)S(1)} %get-tuple-element.142), kind=kOutput, calls=%fused_computation.1 | convolution fusion | flops 1647378432 | bytes 7110656 | tf_op jit(solution)/shard_map/dot_general | solution.py:91
  6.7 1.6 collective-permute-start
  8.3 1.0 fusion.23
  9.3 0.6 collective-permute-start.3
  9.9 10.3 %collective-permute-done = f16[224,1024]{1,0:T(8,128)(2,1)S(1)} collective-permute-done((f16[224,1024]{1,0:T(8,128)(2,1)S(1)}, f16[224,1024]{1,0:T(8,128)(2,1)S(1)}, u32[]{:S(2)}, u32[]{:S(2)}) %collective-permute-start) | collective-permute-done | bytes 458784 | tf_op jit(solution)/shard_map/ppermute | solution.py:107
  20.4 1.3 collective-permute-start.1
  21.7 7.2 %collective-permute-done.3 = f16[224,1024]{1,0:T(8,128)(2,1)S(1)} collective-permute-done((f16[224,1024]{1,0:T(8,128)(2,1)S(1)}, f16[224,1024]{1,0:T(8,128)(2,1)S(1)}, u32[]{:S(2)}, u32[]{:S(2)}) %collective-permute-start.3) | collective-permute-done | bytes 458784 | tf_op jit(solution)/shard_map/ppermute | solution.py:107
  28.8 2.0 maximum_convert_fusion
  30.9 1.5 collective-permute-start.4
  32.4 0.5 collective-permute-start.5
  32.9 0.7 collective-permute-done.1
  33.6 10.7 %collective-permute-done.4 = bf16[224,1024]{1,0:T(8,128)(2,1)S(1)} collective-permute-done((bf16[224,1024]{1,0:T(8,128)(2,1)S(1)}, bf16[224,1024]{1,0:T(8,128)(2,1)S(1)}, u32[]{:S(2)}, u32[]{:S(2)}) %collective-permute-start.4) | collective-permute-done | bytes 458784 | tf_op jit(solution)/shard_map/ppermute | solution.py:107
  44.3 8.0 %collective-permute-done.5 = bf16[224,1024]{1,0:T(8,128)(2,1)} collective-permute-done((bf16[224,1024]{1,0:T(8,128)(2,1)S(1)}, bf16[224,1024]{1,0:T(8,128)(2,1)}, u32[]{:S(2)}, u32[]{:S(2)}) %collective-permute-start.5) | collective-permute-done | bytes 458784 | tf_op jit(solution)/shard_map/ppermute | solution.py:107
  52.3 1.2 maximum_maximum_fusion.refs_0_
  53.5 3.4 %collective-permute-start.2 = (bf16[224,1024]{1,0:T(8,128)(2,1)}, bf16[224,1024]{1,0:T(8,128)(2,1)S(1)}, u32[]{:S(2)}, u32[]{:S(2)}) collective-permute-start(bf16[224,1024]{1,0:T(8,128)(2,1)} %collective-permute-done.1), channel_id=1, source_target_pairs={{16,17},{17,16},{18,19},{19,18},{20,21},{21,20},{22,23},{23,22},{2... | collective-permute-start | bytes 1376264 | tf_op jit(solution)/shard_map/ppermute | solution.py:255
  56.9 6.6 %fusion.46 = f32[448,1792]{1,0:T(8,128)S(1)} fusion(bf16[448,2048]{1,0:T(8,128)(2,1)S(1)} %maximum_maximum_fusion.refs_0_, bf16[2048,1792]{1,0:T(8,128)(2,1)} %refs_2_.5), kind=kOutput, calls=%fused_computation.90 | convolution fusion | flops 3288334336 | bytes 12386304 | tf_op jit(solution)/shard_map/dot_general | solution.py:91
  63.5 2.7 %collective-permute-done.2 = bf16[224,1024]{1,0:T(8,128)(2,1)S(1)} collective-permute-done((bf16[224,1024]{1,0:T(8,128)(2,1)}, bf16[224,1024]{1,0:T(8,128)(2,1)S(1)}, u32[]{:S(2)}, u32[]{:S(2)}) %collective-permute-start.2) | collective-permute-done | bytes 458784 | tf_op jit(solution)/shard_map/ppermute | solution.py:255
  66.5 0.8 collective-permute-start.6
  67.3 1.4 slice_select_fusion.2.refs_0_
  68.8 1.9 add_select_fusion
  71.3 0.7 collective-permute-start.7
  72.1 1.1 collective-permute-done.8
  73.4 0.6 collective-permute-start.10
  74.2 0.7 collective-permute-start.9
  74.9 9.9 %collective-permute-done.10 = bf16[112,1792]{1,0:T(8,128)(2,1)S(1)} collective-permute-done((bf16[112,1792]{1,0:T(8,128)(2,1)S(1)}, bf16[112,1792]{1,0:T(8,128)(2,1)S(1)}, u32[]{:S(2)}, u32[]{:S(2)}) %collective-permute-start.10) | collective-permute-done | bytes 401440 | tf_op jit(solution)/shard_map/ppermute | solution.py:112
  84.9 1.4 collective-permute-start.12
  86.4 1.2 fusion.30
  87.6 0.7 collective-permute-start.11
  88.3 2.9 %collective-permute-done.12 = bf16[112,896]{1,0:T(8,128)(2,1)S(1)} collective-permute-done((bf16[112,896]{1,0:T(8,128)(2,1)S(1)}, bf16[112,896]{1,0:T(8,128)(2,1)S(1)}, u32[]{:S(2)}, u32[]{:S(2)}) %collective-permute-start.12) | collective-permute-done | bytes 200736 | tf_op jit(solution)/shard_map/ppermute | solution.py:112
  91.3 7.7 %collective-permute-start.14 = (bf16[112,896]{1,0:T(8,128)(2,1)S(1)}, bf16[112,896]{1,0:T(8,128)(2,1)S(1)}, u32[]{:S(2)}, u32[]{:S(2)}) collective-permute-start(bf16[112,896]{1,0:T(8,128)(2,1)S(1)} %get-tuple-element.134), channel_id=1, source_target_pairs={{0,16},{2,18},{4,20},{6,22},{8,24},{10,26},{12,28},{14,30},{16,0},... | collective-permute-start | bytes 602120 | tf_op jit(solution)/shard_map/ppermute | solution.py:112
  99.1 5.8 %collective-permute-done.14 = bf16[112,896]{1,0:T(8,128)(2,1)S(1)} collective-permute-done((bf16[112,896]{1,0:T(8,128)(2,1)S(1)}, bf16[112,896]{1,0:T(8,128)(2,1)S(1)}, u32[]{:S(2)}, u32[]{:S(2)}) %collective-permute-start.14) | collective-permute-done | bytes 200736 | tf_op jit(solution)/shard_map/ppermute | solution.py:112
  104.9 1.1 fusion.37
  106.0 2.4 %collective-permute-start.15 = (bf16[112,896]{1,0:T(8,128)(2,1)S(1)}, bf16[112,896]{1,0:T(8,128)(2,1)S(1)}, u32[]{:S(2)}, u32[]{:S(2)}) collective-permute-start(bf16[112,896]{1,0:T(8,128)(2,1)S(1)} %fusion.37), channel_id=1, source_target_pairs={{0,8},{2,10},{4,12},{6,14},{8,0},{10,2},{12,4},{14,6},{16,24},{18,... | collective-permute-start | bytes 602120 | tf_op jit(solution)/shard_map/ppermute | solution.py:112
  108.3 4.0 %collective-permute-done.15 = bf16[112,896]{1,0:T(8,128)(2,1)S(1)} collective-permute-done((bf16[112,896]{1,0:T(8,128)(2,1)S(1)}, bf16[112,896]{1,0:T(8,128)(2,1)S(1)}, u32[]{:S(2)}, u32[]{:S(2)}) %collective-permute-start.15) | collective-permute-done | bytes 200736 | tf_op jit(solution)/shard_map/ppermute | solution.py:112
  112.4 0.4 collective-permute-start.16
  112.8 0.9 collective-permute-start.13
  113.7 8.1 %collective-permute-done.16 = bf16[112,1792]{1,0:T(8,128)(2,1)S(1)} collective-permute-done((bf16[112,1792]{1,0:T(8,128)(2,1)S(1)}, bf16[112,1792]{1,0:T(8,128)(2,1)S(1)}, u32[]{:S(2)}, u32[]{:S(2)}) %collective-permute-start.16) | collective-permute-done | bytes 401440 | tf_op jit(solution)/shard_map/ppermute | solution.py:112
  122.2 2.2 %collective-permute-done.17 = bf16[224,1792]{1,0:T(8,128)(2,1)S(1)} collective-permute-done((bf16[224,1792]{1,0:T(8,128)(2,1)S(1)}, bf16[224,1792]{1,0:T(8,128)(2,1)S(1)}, u32[]{:S(2)}, u32[]{:S(2)}) %collective-permute-start.17) | collective-permute-done | bytes 802848 | tf_op jit(solution)/shard_map/ppermute | solution.py:112
  124.5 1.2 fusion.45
  125.7 0.5 pad_maximum_fusion.2
  126.5 1.0 slice-done.9
  127.5 2.0 fusion.26
  129.6 2.0 fusion.20
  131.6 3.4 %collective-permute-start.19 = (bf16[224,1024]{1,0:T(8,128)(2,1)S(1)}, bf16[224,1024]{1,0:T(8,128)(2,1)S(1)}, u32[]{:S(2)}, u32[]{:S(2)}) collective-permute-start(bf16[224,1024]{1,0:T(8,128)(2,1)S(1)} %get-tuple-element.161), channel_id=1, source_target_pairs={{16,17},{17,16},{18,19},{19,18},{20,21},{21,20},{22,23},{23,22},{2... | collective-permute-start | bytes 1376264 | tf_op jit(solution)/shard_map/ppermute | solution.py:294
  134.9 0.6 collective-permute-start.21
  135.6 1.5 collective-permute-start.18
  137.0 1.2 fusion.31
  138.3 1.2 fusion.17
  139.5 2.2 %fusion.2 = f32[224,1024]{1,0:T(8,128)} fusion(bf16[2048,1792]{1,0:T(8,128)(2,1)S(1)} %bitcast.28, bf16[448,1792]{1,0:T(8,128)(2,1)S(1)} %get-tuple-element.100.refs_1_), kind=kOutput, calls=%fused_computation.3 | convolution fusion | flops 822083584 | bytes 5390336 | tf_op jit(solution)/shard_map/dot_general | solution.py:101
  141.7 5.1 %collective-permute-done.19 = bf16[224,1024]{1,0:T(8,128)(2,1)S(1)} collective-permute-done((bf16[224,1024]{1,0:T(8,128)(2,1)S(1)}, bf16[224,1024]{1,0:T(8,128)(2,1)S(1)}, u32[]{:S(2)}, u32[]{:S(2)}) %collective-permute-start.19) | collective-permute-done | bytes 458784 | tf_op jit(solution)/shard_map/ppermute | solution.py:294
  146.8 0.9 add_convert_fusion
  147.7 1.6 collective-permute-start.20
  149.3 2.8 %copy-done.3 = bf16[1024,1792]{1,0:T(8,128)(2,1)S(1)} copy-done((bf16[1024,1792]{1,0:T(8,128)(2,1)S(1)}, bf16[1024,1792]{1,0:T(8,128)(2,1)}, u32[]{:S(2)}) %copy-start.3) | copy-done | bytes 3670040
  152.1 8.5 %shard_map.229 = (bf16[1024,1792]{1,0:T(8,128)(2,1)}, bf16[1024,1792]{1,0:T(8,128)(2,1)}, bf16[1024,1792]{1,0:T(8,128)(2,1)}) custom-call(bf16[448,1024]{1,0:T(8,128)(2,1)S(1)} %slice_select_fusion.2.refs_0_, bf16[448,1792]{1,0:T(8,128)(2,1)S(1)} %get-tuple-element.101.refs_1_, bf16[1024,1792]{1,0:T(8,128)(2,1)S(1)} %copy-done.1, ...), custom_call_target="tpu_custom_call" | custom-call | flops 1644167168 | bytes 22020096 | tf_op jit(solution)/shard_map/pallas_call | solution.py:67
  160.9 1.6 collective-permute-start.24
  162.5 3.8 %copy-done = bf16[2048,1792]{1,0:T(8,128)(2,1)S(1)} copy-done((bf16[2048,1792]{1,0:T(8,128)(2,1)S(1)}, bf16[2048,1792]{1,0:T(8,128)(2,1)}, u32[]{:S(2)}) %copy-start) | copy-done | bytes 7340056
  166.4 16.1 %shard_map.230 = (bf16[2048,1792]{1,0:T(8,128)(2,1)}, bf16[2048,1792]{1,0:T(8,128)(2,1)}, bf16[2048,1792]{1,0:T(8,128)(2,1)}) custom-call(bf16[448,2048]{1,0:T(8,128)(2,1)S(1)} %maximum_maximum_fusion.refs_0_, bf16[448,1792]{1,0:T(8,128)(2,1)S(1)} %get-tuple-element.100.refs_1_, bf16[2048,1792]{1,0:T(8,128)(2,1)S(1)} %bitcast.30, ...), custom_call_target="tpu_custom_call" | custom-call | flops 3288334336 | bytes 44040192 | tf_op jit(solution)/shard_map/pallas_call | solution.py:67
  183.1 0.5 copy-done.5
  183.7 1.4 collective-permute-start.23
  185.1 1.1 pad_maximum_fusion.3.refs_1_
  186.3 8.8 %shard_map.231 = (bf16[1792,2048]{1,0:T(8,128)(2,1)}, bf16[1792,2048]{1,0:T(8,128)(2,1)}, bf16[1792,2048]{1,0:T(8,128)(2,1)}) custom-call(bf16[448,1792]{1,0:T(8,128)(2,1)S(1)} %pad_maximum_fusion.refs_0_, bf16[448,1024]{1,0:T(8,128)(2,1)S(1)} %pad_maximum_fusion.3.refs_1_, bf16[1792,2048]{1,0:T(8,128)(2,1)S(1)} %bitcast.22, ...), custom_call_target="tpu_custom_call" | custom-call | flops 1644167168 | bytes 22020096 | tf_op jit(solution)/shard_map/pallas_call | solution.py:67
  195.2 8.8 %shard_map.232 = (bf16[1792,2048]{1,0:T(8,128)(2,1)}, bf16[1792,2048]{1,0:T(8,128)(2,1)}, bf16[1792,2048]{1,0:T(8,128)(2,1)}) custom-call(bf16[448,1792]{1,0:T(8,128)(2,1)S(1)} %pad_maximum_fusion.refs_0_, bf16[448,1024]{1,0:T(8,128)(2,1)S(1)} %pad_maximum_fusion.4.refs_1_, ...), custom_call_target="tpu_custom_call", output_to_operand_aliasing={{0}: (5, {}), {1}: (6, {}), {2}: (7, {})} | custom-call | flops 1644167168 | bytes 22020096 | tf_op jit(solution)/shard_map/pallas_call | solution.py:67
  203.9 0.6 fusion.40
  (98 shorter events, 4.0 us)
Async XLA Ops:
  0.7 7.6 %slice-start = ((s8[7340032]{0:T(1024)(128)(4,1)}), s8[4194304]{0:T(1024)(128)(4,1)S(1)}, s32[]{:S(2)}) async-start(s8[7340032]{0:T(1024)(128)(4,1)} %bitcast.19), calls=%async_computation | async-start | bytes 8388608
  2.3 5.9 %copy-start.4 = (bf16[224,1792]{1,0:T(8,128)(2,1)}, bf16[224,1792]{1,0:T(8,128)(2,1)S(1)}, u32[]{:S(2)}) copy-start(bf16[224,1792]{1,0:T(8,128)(2,1)S(1)} %get-tuple-element.143) | copy-start | bytes 2408452
  2.3 5.9 %slice-start.1 = ((s8[7340032]{0:T(1024)(128)(4,1)}), s8[3145728]{0:T(1024)(128)(4,1)S(1)}, s32[]{:S(2)}) async-start(s8[7340032]{0:T(1024)(128)(4,1)} %bitcast.19), calls=%async_computation.1 | async-start | bytes 6291456
  6.7 3.2 %copy-start.8 = (bf16[2048]{0:T(1024)(128)(2,1)S(1)}, bf16[2048]{0:T(1024)(128)(2,1)}, u32[]{:S(2)}) copy-start(bf16[2048]{0:T(1024)(128)(2,1)} %param.17) | copy-start | bytes 12292
  6.7 13.5 %collective-permute-start = (f16[224,1024]{1,0:T(8,128)(2,1)S(1)}, f16[224,1024]{1,0:T(8,128)(2,1)S(1)}, u32[]{:S(2)}, u32[]{:S(2)}) collective-permute-start(f16[224,1024]{1,0:T(8,128)(2,1)S(1)} %slice_convert_fusion), channel_id=1, source_target_pairs={{0,1},{1,0},{2,3},{3,2},{4,5},{5,4},{6,7},{7,6},{8,9},{9,8},{10,11... | collective-permute-start | bytes 1376264 | tf_op jit(solution)/shard_map/ppermute | solution.py:107
  9.3 19.6 %collective-permute-start.3 = (f16[224,1024]{1,0:T(8,128)(2,1)S(1)}, f16[224,1024]{1,0:T(8,128)(2,1)S(1)}, u32[]{:S(2)}, u32[]{:S(2)}) collective-permute-start(f16[224,1024]{1,0:T(8,128)(2,1)S(1)} %fusion.23), channel_id=1, source_target_pairs={{0,1},{1,0},{2,3},{3,2},{4,5},{5,4},{6,7},{7,6},{8,9},{9,8},{10,11... | collective-permute-start | bytes 1376264 | tf_op jit(solution)/shard_map/ppermute | solution.py:107
  20.4 13.2 %collective-permute-start.1 = (bf16[224,1024]{1,0:T(8,128)(2,1)S(1)}, bf16[224,1024]{1,0:T(8,128)(2,1)}, u32[]{:S(2)}, u32[]{:S(2)}) collective-permute-start(bf16[224,1024]{1,0:T(8,128)(2,1)S(1)} %get-tuple-element.140), channel_id=1, source_target_pairs={{0,16},{2,18},{4,20},{6,22},{8,24},{10,26},{12,28},{14,30},{1,17},... | collective-permute-start | bytes 1376264 | tf_op jit(solution)/shard_map/ppermute | solution.py:254
  30.9 13.5 %collective-permute-start.4 = (bf16[224,1024]{1,0:T(8,128)(2,1)S(1)}, bf16[224,1024]{1,0:T(8,128)(2,1)S(1)}, u32[]{:S(2)}, u32[]{:S(2)}) collective-permute-start(bf16[224,1024]{1,0:T(8,128)(2,1)S(1)} %get-tuple-element.71), channel_id=1, source_target_pairs={{0,1},{1,0},{2,3},{3,2},{4,5},{5,4},{6,7},{7,6},{8,9},{9,8},{10,11... | collective-permute-start | bytes 1376264 | tf_op jit(solution)/shard_map/ppermute | solution.py:107
  32.4 19.9 %collective-permute-start.5 = (bf16[224,1024]{1,0:T(8,128)(2,1)S(1)}, bf16[224,1024]{1,0:T(8,128)(2,1)}, u32[]{:S(2)}, u32[]{:S(2)}) collective-permute-start(bf16[224,1024]{1,0:T(8,128)(2,1)S(1)} %get-tuple-element.140), channel_id=1, source_target_pairs={{0,1},{1,0},{2,3},{3,2},{4,5},{5,4},{6,7},{7,6},{8,9},{9,8},{10,11... | collective-permute-start | bytes 1376264 | tf_op jit(solution)/shard_map/ppermute | solution.py:107
  53.5 12.7 %collective-permute-start.2 = (bf16[224,1024]{1,0:T(8,128)(2,1)}, bf16[224,1024]{1,0:T(8,128)(2,1)S(1)}, u32[]{:S(2)}, u32[]{:S(2)}) collective-permute-start(bf16[224,1024]{1,0:T(8,128)(2,1)} %collective-permute-done.1), channel_id=1, source_target_pairs={{16,17},{17,16},{18,19},{19,18},{20,21},{21,20},{22,23},{23,22},{2... | collective-permute-start | bytes 1376264 | tf_op jit(solution)/shard_map/ppermute | solution.py:255
  66.3 2.5 %copy-start.1 = (bf16[1024,1792]{1,0:T(8,128)(2,1)S(1)}, bf16[1024,1792]{1,0:T(8,128)(2,1)}, u32[]{:S(2)}) copy-start(bf16[1024,1792]{1,0:T(8,128)(2,1)} %refs_2_.4) | copy-start | bytes 11010052
  66.5 4.6 %collective-permute-start.6 = (bf16[224,1792]{1,0:T(8,128)(2,1)S(1)}, bf16[224,1792]{1,0:T(8,128)(2,1)S(1)}, u32[]{:S(2)}, u32[]{:S(2)}) collective-permute-start(bf16[224,1792]{1,0:T(8,128)(2,1)S(1)} %select_convert_fusion.1), channel_id=1, source_target_pairs={{0,2},{2,0},{4,6},{6,4},{8,10},{10,8},{12,14},{14,12},{1,3},{3,1},... | collective-permute-start | bytes 2408456 | tf_op jit(solution)/shard_map/ppermute | solution.py:112
  70.8 2.4 %collective-permute-start.8 = (bf16[224,1792]{1,0:T(8,128)(2,1)S(1)}, bf16[224,1792]{1,0:T(8,128)(2,1)S(1)}, u32[]{:S(2)}, u32[]{:S(2)}) collective-permute-start(bf16[224,1792]{1,0:T(8,128)(2,1)S(1)} %select_convert_fusion), channel_id=1, source_target_pairs={{0,2},{2,0},{4,6},{6,4},{8,10},{10,8},{12,14},{14,12},{16,18},{18,... | collective-permute-start | bytes 2408456 | tf_op jit(solution)/shard_map/ppermute | solution.py:112
  71.3 2.8 %collective-permute-start.7 = (bf16[112,1792]{1,0:T(8,128)(2,1)S(1)}, bf16[112,1792]{1,0:T(8,128)(2,1)S(1)}, u32[]{:S(2)}, u32[]{:S(2)}) collective-permute-start(bf16[112,1792]{1,0:T(8,128)(2,1)S(1)} %select_convert_fusion.5), channel_id=1, source_target_pairs={{0,4},{2,6},{4,0},{6,2},{8,12},{10,14},{12,8},{14,10},{1,5},{3,7},... | collective-permute-start | bytes 1204232 | tf_op jit(solution)/shard_map/ppermute | solution.py:112
  73.4 11.4 %collective-permute-start.10 = (bf16[112,1792]{1,0:T(8,128)(2,1)S(1)}, bf16[112,1792]{1,0:T(8,128)(2,1)S(1)}, u32[]{:S(2)}, u32[]{:S(2)}) collective-permute-start(bf16[112,1792]{1,0:T(8,128)(2,1)S(1)} %select_convert_fusion.4), channel_id=1, source_target_pairs={{0,4},{2,6},{4,0},{6,2},{8,12},{10,14},{12,8},{14,10},{16,20},{18,... | collective-permute-start | bytes 1204232 | tf_op jit(solution)/shard_map/ppermute | solution.py:112
  74.2 12.2 %collective-permute-start.9 = (bf16[112,1792]{1,0:T(8,128)(2,1)S(1)}, bf16[112,1792]{1,0:T(8,128)(2,1)S(1)}, u32[]{:S(2)}, u32[]{:S(2)}) collective-permute-start(bf16[112,1792]{1,0:T(8,128)(2,1)S(1)} %get-tuple-element.136), channel_id=1, source_target_pairs={{0,8},{2,10},{4,12},{6,14},{8,0},{10,2},{12,4},{14,6},{1,9},{3,11}... | collective-permute-start | bytes 1204232 | tf_op jit(solution)/shard_map/ppermute | solution.py:112
  84.9 6.3 %collective-permute-start.12 = (bf16[112,896]{1,0:T(8,128)(2,1)S(1)}, bf16[112,896]{1,0:T(8,128)(2,1)S(1)}, u32[]{:S(2)}, u32[]{:S(2)}) collective-permute-start(bf16[112,896]{1,0:T(8,128)(2,1)S(1)} %select_convert_fusion.6), channel_id=1, source_target_pairs={{0,8},{2,10},{4,12},{6,14},{8,0},{10,2},{12,4},{14,6},{16,24},{18,... | collective-permute-start | bytes 602120 | tf_op jit(solution)/shard_map/ppermute | solution.py:112
  87.6 11.4 %collective-permute-start.11 = (bf16[112,1792]{1,0:T(8,128)(2,1)S(1)}, bf16[112,1792]{1,0:T(8,128)(2,1)S(1)}, u32[]{:S(2)}, u32[]{:S(2)}) collective-permute-start(bf16[112,1792]{1,0:T(8,128)(2,1)S(1)} %fusion.30), channel_id=1, source_target_pairs={{0,4},{2,6},{4,0},{6,2},{8,12},{10,14},{12,8},{14,10},{1,5},{3,7},... | collective-permute-start | bytes 1204232 | tf_op jit(solution)/shard_map/ppermute | solution.py:112
  91.3 13.7 %collective-permute-start.14 = (bf16[112,896]{1,0:T(8,128)(2,1)S(1)}, bf16[112,896]{1,0:T(8,128)(2,1)S(1)}, u32[]{:S(2)}, u32[]{:S(2)}) collective-permute-start(bf16[112,896]{1,0:T(8,128)(2,1)S(1)} %get-tuple-element.134), channel_id=1, source_target_pairs={{0,16},{2,18},{4,20},{6,22},{8,24},{10,26},{12,28},{14,30},{16,0},... | collective-permute-start | bytes 602120 | tf_op jit(solution)/shard_map/ppermute | solution.py:112
  106.0 6.3 %collective-permute-start.15 = (bf16[112,896]{1,0:T(8,128)(2,1)S(1)}, bf16[112,896]{1,0:T(8,128)(2,1)S(1)}, u32[]{:S(2)}, u32[]{:S(2)}) collective-permute-start(bf16[112,896]{1,0:T(8,128)(2,1)S(1)} %fusion.37), channel_id=1, source_target_pairs={{0,8},{2,10},{4,12},{6,14},{8,0},{10,2},{12,4},{14,6},{16,24},{18,... | collective-permute-start | bytes 602120 | tf_op jit(solution)/shard_map/ppermute | solution.py:112
  112.4 9.4 %collective-permute-start.16 = (bf16[112,1792]{1,0:T(8,128)(2,1)S(1)}, bf16[112,1792]{1,0:T(8,128)(2,1)S(1)}, u32[]{:S(2)}, u32[]{:S(2)}) collective-permute-start(bf16[112,1792]{1,0:T(8,128)(2,1)S(1)} %pad_maximum_fusion.7), channel_id=1, source_target_pairs={{0,4},{2,6},{4,0},{6,2},{8,12},{10,14},{12,8},{14,10},{16,20},{18,... | collective-permute-start | bytes 1204232 | tf_op jit(solution)/shard_map/ppermute | solution.py:112
  112.8 9.2 %collective-permute-start.13 = (bf16[224,1792]{1,0:T(8,128)(2,1)S(1)}, bf16[224,1792]{1,0:T(8,128)(2,1)S(1)}, u32[]{:S(2)}, u32[]{:S(2)}) collective-permute-start(bf16[224,1792]{1,0:T(8,128)(2,1)S(1)} %pad_maximum_fusion.5), channel_id=1, source_target_pairs={{0,2},{2,0},{4,6},{6,4},{8,10},{10,8},{12,14},{14,12},{1,3},{3,1},... | collective-permute-start | bytes 2408456 | tf_op jit(solution)/shard_map/ppermute | solution.py:112
  121.9 2.4 %collective-permute-start.17 = (bf16[224,1792]{1,0:T(8,128)(2,1)S(1)}, bf16[224,1792]{1,0:T(8,128)(2,1)S(1)}, u32[]{:S(2)}, u32[]{:S(2)}) collective-permute-start(bf16[224,1792]{1,0:T(8,128)(2,1)S(1)} %pad_maximum_fusion.6), channel_id=1, source_target_pairs={{0,2},{2,0},{4,6},{6,4},{8,10},{10,8},{12,14},{14,12},{16,18},{18,... | collective-permute-start | bytes 2408456 | tf_op jit(solution)/shard_map/ppermute | solution.py:112
  124.3 2.2 %slice-start.8 = ((s8[7340032]{0:T(1024)(128)(4,1)}), s8[4194304]{0:T(1024)(128)(4,1)S(1)}, s32[]{:S(2)}) async-start(s8[7340032]{0:T(1024)(128)(4,1)} %bitcast.27), calls=%async_computation.8 | async-start | bytes 8388608
  124.4 3.1 %slice-start.9 = ((s8[7340032]{0:T(1024)(128)(4,1)}), s8[3145728]{0:T(1024)(128)(4,1)S(1)}, s32[]{:S(2)}) async-start(s8[7340032]{0:T(1024)(128)(4,1)} %bitcast.27), calls=%async_computation.9 | async-start | bytes 6291456
  131.6 15.2 %collective-permute-start.19 = (bf16[224,1024]{1,0:T(8,128)(2,1)S(1)}, bf16[224,1024]{1,0:T(8,128)(2,1)S(1)}, u32[]{:S(2)}, u32[]{:S(2)}) collective-permute-start(bf16[224,1024]{1,0:T(8,128)(2,1)S(1)} %get-tuple-element.161), channel_id=1, source_target_pairs={{16,17},{17,16},{18,19},{19,18},{20,21},{21,20},{22,23},{23,22},{2... | collective-permute-start | bytes 1376264 | tf_op jit(solution)/shard_map/ppermute | solution.py:294
  134.9 25.7 %collective-permute-start.21 = (bf16[224,1024]{1,0:T(8,128)(2,1)}, bf16[224,1024]{1,0:T(8,128)(2,1)S(1)}, u32[]{:S(2)}, u32[]{:S(2)}) collective-permute-start(bf16[224,1024]{1,0:T(8,128)(2,1)} %fusion.20), channel_id=1, source_target_pairs={{0,1},{1,0},{2,3},{3,2},{4,5},{5,4},{6,7},{7,6},{8,9},{9,8},{10,11... | collective-permute-start | bytes 1376264 | tf_op jit(solution)/shard_map/ppermute | solution.py:107
  135.6 46.9 %collective-permute-start.18 = (bf16[224,1024]{1,0:T(8,128)(2,1)}, bf16[224,1024]{1,0:T(8,128)(2,1)S(1)}, u32[]{:S(2)}, u32[]{:S(2)}) collective-permute-start(bf16[224,1024]{1,0:T(8,128)(2,1)} %fusion.26), channel_id=1, source_target_pairs={{0,1},{1,0},{2,3},{3,2},{4,5},{5,4},{6,7},{7,6},{8,9},{9,8},{10,11... | collective-permute-start | bytes 1376264 | tf_op jit(solution)/shard_map/ppermute | solution.py:107
  139.5 9.8 %copy-start.2 = (bf16[1024,1792]{1,0:T(8,128)(2,1)S(1)}, bf16[1024,1792]{1,0:T(8,128)(2,1)}, u32[]{:S(2)}) copy-start(bf16[1024,1792]{1,0:T(8,128)(2,1)} %refs_3_.4) | copy-start | bytes 11010052
  139.5 23.0 %slice-start.12 = ((s8[7340032]{0:T(1024)(128)(4,1)}), s8[4194304]{0:T(1024)(128)(4,1)S(1)}, s32[]{:S(2)}) async-start(s8[7340032]{0:T(1024)(128)(4,1)} %bitcast.31), calls=%async_computation.12 | async-start | bytes 8388608
  146.8 15.7 %slice-start.10 = ((s8[7340032]{0:T(1024)(128)(4,1)}), s8[4194304]{0:T(1024)(128)(4,1)S(1)}, s32[]{:S(2)}) async-start(s8[7340032]{0:T(1024)(128)(4,1)} %bitcast.29), calls=%async_computation.10 | async-start | bytes 8388608
  147.7 14.8 %slice-start.11 = ((s8[7340032]{0:T(1024)(128)(4,1)}), s8[3145728]{0:T(1024)(128)(4,1)S(1)}, s32[]{:S(2)}) async-start(s8[7340032]{0:T(1024)(128)(4,1)} %bitcast.29), calls=%async_computation.11 | async-start | bytes 6291456
  147.7 14.8 %slice-start.13 = ((s8[7340032]{0:T(1024)(128)(4,1)}), s8[3145728]{0:T(1024)(128)(4,1)S(1)}, s32[]{:S(2)}) async-start(s8[7340032]{0:T(1024)(128)(4,1)} %bitcast.31), calls=%async_computation.13 | async-start | bytes 6291456
  147.7 34.8 %collective-permute-start.20 = (bf16[224,1024]{1,0:T(8,128)(2,1)}, bf16[224,1024]{1,0:T(8,128)(2,1)S(1)}, u32[]{:S(2)}, u32[]{:S(2)}) collective-permute-start(bf16[224,1024]{1,0:T(8,128)(2,1)} %add_convert_fusion), channel_id=1, source_target_pairs={{16,0},{18,2},{20,4},{22,6},{24,8},{26,10},{28,12},{30,14},{17,1},... | collective-permute-start | bytes 1376264 | tf_op jit(solution)/shard_map/ppermute | solution.py:302
  149.3 2.8 %copy-start.3 = (bf16[1024,1792]{1,0:T(8,128)(2,1)S(1)}, bf16[1024,1792]{1,0:T(8,128)(2,1)}, u32[]{:S(2)}) copy-start(bf16[1024,1792]{1,0:T(8,128)(2,1)} %refs_4_.4) | copy-start | bytes 11010052
  152.1 8.5 %copy-start.7 = (f32[224,1024]{1,0:T(8,128)S(1)}, f32[224,1024]{1,0:T(8,128)}, u32[]{:S(2)}) copy-start(f32[224,1024]{1,0:T(8,128)} %get-tuple-element.108) | copy-start | bytes 2752516
  160.6 25.6 %slice-start.2 = ((s8[7340032]{0:T(1024)(128)(4,1)}), s8[4194304]{0:T(1024)(128)(4,1)S(1)}, s32[]{:S(2)}) async-start(s8[7340032]{0:T(1024)(128)(4,1)} %bitcast.21), calls=%async_computation.2 | async-start | bytes 8388608
  160.6 25.6 %slice-start.4 = ((s8[7340032]{0:T(1024)(128)(4,1)}), s8[4194304]{0:T(1024)(128)(4,1)S(1)}, s32[]{:S(2)}) async-start(s8[7340032]{0:T(1024)(128)(4,1)} %bitcast.23), calls=%async_computation.4 | async-start | bytes 8388608
  160.6 25.6 %slice-start.6 = ((s8[7340032]{0:T(1024)(128)(4,1)}), s8[4194304]{0:T(1024)(128)(4,1)S(1)}, s32[]{:S(2)}) async-start(s8[7340032]{0:T(1024)(128)(4,1)} %bitcast.25), calls=%async_computation.6 | async-start | bytes 8388608
  160.9 25.3 %slice-start.3 = ((s8[7340032]{0:T(1024)(128)(4,1)}), s8[3145728]{0:T(1024)(128)(4,1)S(1)}, s32[]{:S(2)}) async-start(s8[7340032]{0:T(1024)(128)(4,1)} %bitcast.21), calls=%async_computation.3 | async-start | bytes 6291456
  160.9 25.3 %slice-start.5 = ((s8[7340032]{0:T(1024)(128)(4,1)}), s8[3145728]{0:T(1024)(128)(4,1)S(1)}, s32[]{:S(2)}) async-start(s8[7340032]{0:T(1024)(128)(4,1)} %bitcast.23), calls=%async_computation.5 | async-start | bytes 6291456
  160.9 25.3 %slice-start.7 = ((s8[7340032]{0:T(1024)(128)(4,1)}), s8[3145728]{0:T(1024)(128)(4,1)S(1)}, s32[]{:S(2)}) async-start(s8[7340032]{0:T(1024)(128)(4,1)} %bitcast.25), calls=%async_computation.7 | async-start | bytes 6291456
  160.9 24.2 %collective-permute-start.24 = (bf16[224,1024]{1,0:T(8,128)(2,1)S(1)}, bf16[224,1024]{1,0:T(8,128)(2,1)}, u32[]{:S(2)}, u32[]{:S(2)}) collective-permute-start(bf16[224,1024]{1,0:T(8,128)(2,1)S(1)} %get-tuple-element.119), channel_id=1, source_target_pairs={{0,1},{1,0},{2,3},{3,2},{4,5},{5,4},{6,7},{7,6},{8,9},{9,8},{10,11... | collective-permute-start | bytes 1376264 | tf_op jit(solution)/shard_map/ppermute | solution.py:107
  162.5 3.9 %copy-start = (bf16[2048,1792]{1,0:T(8,128)(2,1)S(1)}, bf16[2048,1792]{1,0:T(8,128)(2,1)}, u32[]{:S(2)}) copy-start(bf16[2048,1792]{1,0:T(8,128)(2,1)} %refs_3_.5) | copy-start | bytes 22020100
  166.3 16.1 %copy-start.6 = (f32[224,1024]{1,0:T(8,128)S(1)}, f32[224,1024]{1,0:T(8,128)}, u32[]{:S(2)}) copy-start(f32[224,1024]{1,0:T(8,128)} %fusion.2) | copy-start | bytes 2752516
  182.5 1.1 copy-start.5
  182.8 12.3 %collective-permute-start.22 = (bf16[224,1024]{1,0:T(8,128)(2,1)S(1)}, bf16[224,1024]{1,0:T(8,128)(2,1)S(1)}, u32[]{:S(2)}, u32[]{:S(2)}) collective-permute-start(bf16[224,1024]{1,0:T(8,128)(2,1)S(1)} %get-tuple-element.124), channel_id=1, source_target_pairs={{0,1},{1,0},{2,3},{3,2},{4,5},{5,4},{6,7},{7,6},{8,9},{9,8},{10,11... | collective-permute-start | bytes 1376264 | tf_op jit(solution)/shard_map/ppermute | solution.py:107
  183.7 11.3 %collective-permute-start.23 = (f32[2048]{0:T(1024)S(1)}, f32[2048]{0:T(1024)S(1)}, u32[]{:S(2)}, u32[]{:S(2)}) collective-permute-start(f32[2048]{0:T(1024)S(1)} %pad_maximum_fusion.8), channel_id=1, source_target_pairs={{0,1},{1,0},{2,3},{3,2},{4,5},{5,4},{6,7},{7,6},{8,9},{9,8},{10,11... | collective-permute-start | bytes 24584 | tf_op jit(solution)/shard_map/ppermute | solution.py:107
  195.1 8.8 %copy-start.9 = (bf16[2048]{0:T(1024)(128)(2,1)S(1)}, bf16[2048]{0:T(1024)(128)(2,1)}, u32[]{:S(2)}) copy-start(bf16[2048]{0:T(1024)(128)(2,1)} %param.23) | copy-start | bytes 12292
  195.1 8.8 %copy-start.10 = (bf16[2048]{0:T(1024)(128)(2,1)S(1)}, bf16[2048]{0:T(1024)(128)(2,1)}, u32[]{:S(2)}) copy-start(bf16[2048]{0:T(1024)(128)(2,1)} %param.22) | copy-start | bytes 12292

commit v3 on v2

--- a/solution.py
+++ b/solution.py
@@ -40,9 +40,10 @@
     keep = 1.0 - learn_rate * decay_rate
     rate = learn_rate * math.sqrt(second_scale) / first_scale
     shift = adam_eps * math.sqrt(second_scale)
+    left = jnp.transpose(left_ref[...])
     for start in range(0, weight_ref.shape[1], tile):
         columns = slice(start, start + tile)
-        gradient = over_rows(left_ref[...], right_ref[:, columns])
+        gradient = matmul(left, right_ref[:, columns])
         scaled = (1.0 - beta_one) * gradient
         first_new = beta_one * first_ref[:, columns].astype(jnp.float32) + scaled
         second_new = (
@@ -89,12 +90,6 @@
 
 def matmul(left, right):
     return jnp.dot(left, right, preferred_element_type=jnp.float32)
-
-
-def over_rows(left, right):
-    return lax.dot_general(
-        left, right, (((0,), (0,)), ((), ())), preferred_element_type=jnp.float32
-    )
 
 
 def over_cols(left, right):
@@ -234,7 +229,7 @@
 
     bits = feat_count.bit_length() - 1
     second_plan = plan_of(list(range(bits)))
-    first_plan = plan_of(list(range(bits - 1)))
+    first_plan = plan_of([0, 2, 1] + list(range(3, bits - 1)))
     order = Order()
 
     inputs = jnp.concatenate(
@@ -276,7 +271,7 @@
     )
     left = [len(plan) + len(plan) - 1 for plan in (first_plan, second_plan)]
     while left[1] > 0:
-        for layer in (0, 1):
+        for layer in (1, 0):
             if left[layer] > 0:
                 order.advance(layer)
                 left[layer] -= 1
@@ -297,14 +292,14 @@
     delta_own, delta_next = order.after((delta_own, delta_next))
     kept_cross, kept_a, kept_b = back_parts(slice(0, part), delta_own, delta_next)
     order.mark(kept_cross, kept_a, kept_b)
+    next_done = adamw_matmul(
+        order.after(cross_input), delta_next, next_decoder, next_first, next_second, weight_decay
+    )
+    order.mark(*next_done)
     kept_cross, cross_arriving = order.after((kept_cross, cross_arriving))
     cross_sum = add(kept_cross, cross_arriving).astype(jnp.bfloat16)
     returned = lax.ppermute(cross_sum, "feat", upward)
     order.mark(cross_sum)
-    next_done = adamw_matmul(
-        order.after(cross_input), delta_next, next_decoder, next_first, next_second, weight_decay
-    )
-    order.mark(*next_done)
     kept_a, arriving_a, pre_a = order.after((kept_a, arriving_a, pre_a))
     grad_a = jnp.where(pre_a > 0.0, add(kept_a, arriving_a), 0.0).astype(jnp.bfloat16)
     grad_other_a = across(grad_a)

time: 205 us -> 200 us (0.976); the launches traced: 205 us -> 198 us
  waiting for transfers between devices: 78.7 us -> 71.8 us
  other arithmetic: 10.9 us -> 13 us
    ppermute x1, waiting for transfers between devices: 5.11 us -> 0.01 us  [local(): cross_arriving = lax.ppermute(leaving[0], ('feat', 'width'), trailing_pairs)]
    ppermute x12, starting transfers between devices: 16.4 us -> 12 us  [flipped(): lax.ppermute(value, 'feat', [(index, index ^ step) for index in range(mem...]
    ppermute x1, starting transfers between devices: 1.57 us -> 3.99 us  [local(): returned = lax.ppermute(cross_sum, 'feat', upward)]
    ppermute x9, waiting for transfers between devices: 36.2 us -> 34.1 us  [across(): return lax.ppermute(value, 'width', [(0, 1), (1, 0)])]
    unnamed x50 -> x62, local copies, waits for them, and re-layouts: 8.62 us -> 8.5 us
  transfers between devices with their start and end apart: 25 -> 25, of which waited for: 14 -> 14; matrix products, arithmetic and copies ran while one was open for 11% -> 12% of each run, Pallas kernels for 16% -> 17%
where the time goes in v3:
time: 200 us; the launch traced here: 198 us
  waiting for transfers between devices  71.8 us (36%)
  Pallas kernels  42 us (21%)
  starting transfers between devices  33.8 us (17%)
  matrix products  25.5 us (13%)
  other arithmetic  13 us (6%)
  local copies, waits for them, and re-layouts  10.2 us (5%)
    pallas_call x4, Pallas kernels, adamw_matmul(): pl.pallas_call(functools.partial(adamw_kernel, decay_rate, tile), grid=(r...  42 us
    ppermute x9, waiting for transfers between devices, across(): return lax.ppermute(value, 'width', [(0, 1), (1, 0)])  34.1 us
    ppermute x12, waiting for transfers between devices, flipped(): lax.ppermute(value, 'feat', [(index, index ^ step) for index in range(mem...  33.7 us
    dot_general x5, matrix products, matmul(): return jnp.dot(left, right, preferred_element_type=jnp.float32)  15.6 us
    ppermute x12, starting transfers between devices, flipped(): lax.ppermute(value, 'feat', [(index, index ^ step) for index in range(mem...  12 us
    dot_general x6, matrix products, over_cols(): lax.dot_general(left, right, (((1,), (1,)), ((), ())), preferred_element_...  9.84 us
    ppermute x9, starting transfers between devices, across(): return lax.ppermute(value, 'width', [(0, 1), (1, 0)])  9.48 us
    unnamed x62, local copies, waits for them, and re-layouts  8.5 us
  transfers between devices with their start and end apart: 25, of which 14 were waited for; matrix products, arithmetic and copies ran while one was open for 12% of the time, Pallas kernels for 17%

profile of v3, /device:TPU:20, one launch (start us, length us, event | category | flops | bytes accessed | tf_op | source)
XLA Modules:
  0.0 197.5 jit_solution(17695414186806809195)
XLA Ops:
  0.7 1.6 dynamic-slice_bitcast_fusion.1
  2.4 4.2 %fusion = f32[448,1024]{1,0:T(8,128)S(1)} fusion(bf16[1792,2048]{1,0:T(8,128)(2,1)} %refs_2_.7, bf16[224,1792]{1,0:T(8,128)(2,1)S(1)} %get-tuple-element.143, bf16[224,1792]{1,0:T(8,128)(2,1)S(1)} %get-tuple-element.142), kind=kOutput, calls=%fused_computation.1 | convolution fusion | flops 1647378432 | bytes 7110656 | tf_op jit(solution)/shard_map/dot_general | solution.py:92
  6.7 1.6 collective-permute-start
  8.2 1.0 fusion.23
  9.2 0.6 collective-permute-start.3
  9.9 10.3 %collective-permute-done = f16[224,1024]{1,0:T(8,128)(2,1)S(1)} collective-permute-done((f16[224,1024]{1,0:T(8,128)(2,1)S(1)}, f16[224,1024]{1,0:T(8,128)(2,1)S(1)}, u32[]{:S(2)}, u32[]{:S(2)}) %collective-permute-start) | collective-permute-done | bytes 458784 | tf_op jit(solution)/shard_map/ppermute | solution.py:102
  20.1 1.1 maximum_convert_fusion.1
  21.3 1.3 collective-permute-start.1
  22.6 6.3 %collective-permute-done.3 = f16[224,1024]{1,0:T(8,128)(2,1)S(1)} collective-permute-done((f16[224,1024]{1,0:T(8,128)(2,1)S(1)}, f16[224,1024]{1,0:T(8,128)(2,1)S(1)}, u32[]{:S(2)}, u32[]{:S(2)}) %collective-permute-start.3) | collective-permute-done | bytes 458784 | tf_op jit(solution)/shard_map/ppermute | solution.py:102
  28.8 2.0 %maximum_convert_fusion = (bf16[224,1024]{1,0:T(8,128)(2,1)S(1)}, f32[224,1024]{1,0:T(8,128)}) fusion(f32[1024]{0:T(1024)S(1)} %get-tuple-element.159, f16[224,1024]{1,0:T(8,128)(2,1)S(1)} %collective-permute-done.3, bf16[224,1792]{1,0:T(8,128)(2,1)S(1)} %get-tuple-element.142, bf16[1792,2048]{1,0:T(8,128)(2,1)S(1)} %bitcast.20), kind=kOutput, calls=%fused_computation.42 | convolution fusion | flops 823230464 | bytes 6311936 | tf_op jit(solution)/shard_map/dot_general | solution.py:92
  30.8 1.5 collective-permute-start.4
  32.9 1.5 collective-permute-done.1
  34.4 9.9 %collective-permute-done.4 = bf16[224,1024]{1,0:T(8,128)(2,1)S(1)} collective-permute-done((bf16[224,1024]{1,0:T(8,128)(2,1)S(1)}, bf16[224,1024]{1,0:T(8,128)(2,1)S(1)}, u32[]{:S(2)}, u32[]{:S(2)}) %collective-permute-start.4) | collective-permute-done | bytes 458784 | tf_op jit(solution)/shard_map/ppermute | solution.py:102
  44.3 0.8 copy-done.10
  45.1 7.1 %collective-permute-done.5 = bf16[224,1024]{1,0:T(8,128)(2,1)} collective-permute-done((bf16[224,1024]{1,0:T(8,128)(2,1)S(1)}, bf16[224,1024]{1,0:T(8,128)(2,1)}, u32[]{:S(2)}, u32[]{:S(2)}) %collective-permute-start.5) | collective-permute-done | bytes 458784 | tf_op jit(solution)/shard_map/ppermute | solution.py:102
  52.2 1.4 maximum_maximum_fusion.refs_0_
  53.5 3.7 %collective-permute-start.2 = (bf16[224,1024]{1,0:T(8,128)(2,1)S(1)}, bf16[224,1024]{1,0:T(8,128)(2,1)S(1)}, u32[]{:S(2)}, u32[]{:S(2)}) collective-permute-start(bf16[224,1024]{1,0:T(8,128)(2,1)S(1)} %copy-done.12), channel_id=1, source_target_pairs={{16,17},{17,16},{18,19},{19,18},{20,21},{21,20},{22,23},{23,22},{2... | collective-permute-start | bytes 1376264 | tf_op jit(solution)/shard_map/ppermute | solution.py:250
  57.2 6.6 %fusion.46 = f32[448,1792]{1,0:T(8,128)S(1)} fusion(bf16[448,2048]{1,0:T(8,128)(2,1)S(1)} %maximum_maximum_fusion.refs_0_, bf16[2048,1792]{1,0:T(8,128)(2,1)} %refs_2_.5), kind=kOutput, calls=%fused_computation.90 | convolution fusion | flops 3288334336 | bytes 12386304 | tf_op jit(solution)/shard_map/dot_general | solution.py:92
  63.8 2.4 %collective-permute-done.2 = bf16[224,1024]{1,0:T(8,128)(2,1)S(1)} collective-permute-done((bf16[224,1024]{1,0:T(8,128)(2,1)S(1)}, bf16[224,1024]{1,0:T(8,128)(2,1)S(1)}, u32[]{:S(2)}, u32[]{:S(2)}) %collective-permute-start.2) | collective-permute-done | bytes 458784 | tf_op jit(solution)/shard_map/ppermute | solution.py:250
  66.5 1.8 add_select_fusion
  68.9 0.7 collective-permute-start.6
  69.8 1.2 collective-permute-done.7
  71.3 0.6 collective-permute-start.9
  72.2 0.7 collective-permute-start.8
  73.0 9.7 %collective-permute-done.9 = bf16[112,1792]{1,0:T(8,128)(2,1)S(1)} collective-permute-done((bf16[112,1792]{1,0:T(8,128)(2,1)S(1)}, bf16[112,1792]{1,0:T(8,128)(2,1)S(1)}, u32[]{:S(2)}, u32[]{:S(2)}) %collective-permute-start.9) | collective-permute-done | bytes 401440 | tf_op jit(solution)/shard_map/ppermute | solution.py:107
  82.8 1.6 collective-permute-start.11
  84.6 0.7 collective-permute-start.10
  85.3 3.8 %collective-permute-done.11 = bf16[112,896]{1,0:T(8,128)(2,1)S(1)} collective-permute-done((bf16[112,896]{1,0:T(8,128)(2,1)S(1)}, bf16[112,896]{1,0:T(8,128)(2,1)S(1)}, u32[]{:S(2)}, u32[]{:S(2)}) %collective-permute-start.11) | collective-permute-done | bytes 200736 | tf_op jit(solution)/shard_map/ppermute | solution.py:107
  89.1 0.9 fusion.41
  90.0 1.9 fusion.30
  91.9 1.4 collective-permute-start.12
  93.3 4.3 %collective-permute-done.13 = bf16[112,896]{1,0:T(8,128)(2,1)} collective-permute-done((bf16[112,896]{1,0:T(8,128)(2,1)}, bf16[112,896]{1,0:T(8,128)(2,1)}, u32[]{:S(2)}, u32[]{:S(2)}) %collective-permute-start.13) | collective-permute-done | bytes 200736 | tf_op jit(solution)/shard_map/ppermute | solution.py:107
  97.7 1.3 fusion.37
  99.0 4.6 %collective-permute-start.15 = (bf16[112,896]{1,0:T(8,128)(2,1)S(1)}, bf16[112,896]{1,0:T(8,128)(2,1)S(1)}, u32[]{:S(2)}, u32[]{:S(2)}) collective-permute-start(bf16[112,896]{1,0:T(8,128)(2,1)S(1)} %fusion.37), channel_id=1, source_target_pairs={{0,8},{2,10},{4,12},{6,14},{8,0},{10,2},{12,4},{14,6},{16,24},{18,... | collective-permute-start | bytes 602120 | tf_op jit(solution)/shard_map/ppermute | solution.py:107
  103.6 1.2 broadcast_select_fusion.8
  104.8 3.5 %collective-permute-done.15 = bf16[112,896]{1,0:T(8,128)(2,1)S(1)} collective-permute-done((bf16[112,896]{1,0:T(8,128)(2,1)S(1)}, bf16[112,896]{1,0:T(8,128)(2,1)S(1)}, u32[]{:S(2)}, u32[]{:S(2)}) %collective-permute-start.15) | collective-permute-done | bytes 200736 | tf_op jit(solution)/shard_map/ppermute | solution.py:107
  108.4 0.6 collective-permute-start.16
  109.0 0.9 collective-permute-start.14
  109.9 8.8 %collective-permute-done.16 = bf16[112,1792]{1,0:T(8,128)(2,1)S(1)} collective-permute-done((bf16[112,1792]{1,0:T(8,128)(2,1)S(1)}, bf16[112,1792]{1,0:T(8,128)(2,1)S(1)}, u32[]{:S(2)}, u32[]{:S(2)}) %collective-permute-start.16) | collective-permute-done | bytes 401440 | tf_op jit(solution)/shard_map/ppermute | solution.py:107
  118.9 2.3 %collective-permute-done.17 = bf16[224,1792]{1,0:T(8,128)(2,1)S(1)} collective-permute-done((bf16[224,1792]{1,0:T(8,128)(2,1)S(1)}, bf16[224,1792]{1,0:T(8,128)(2,1)S(1)}, u32[]{:S(2)}, u32[]{:S(2)}) %collective-permute-start.17) | collective-permute-done | bytes 802848 | tf_op jit(solution)/shard_map/ppermute | solution.py:107
  121.5 2.0 %fusion.45 = (bf16[224,1024]{1,0:T(8,128)(2,1)}, f32[224,1024]{1,0:T(8,128)S(1)}) fusion(bf16[224,1792]{1,0:T(8,128)(2,1)S(1)} %get-tuple-element.149, bf16[1024,1792]{1,0:T(8,128)(2,1)S(1)} %copy-done.2), kind=kOutput, calls=%fused_computation.89 | convolution fusion | flops 822312960 | bytes 5849088 | tf_op jit(solution)/shard_map/dot_general | solution.py:96
  123.5 0.5 pad_maximum_fusion.2
  124.0 0.6 slice-done.9
  124.6 2.0 %fusion.26 = bf16[224,1024]{1,0:T(8,128)(2,1)} fusion(bf16[2048,1792]{1,0:T(8,128)(2,1)S(1)} %bitcast.28, bf16[448,1792]{1,0:T(8,128)(2,1)S(1)} %get-tuple-element.100.refs_1_), kind=kOutput, calls=%fused_computation.30 | convolution fusion | flops 822312960 | bytes 4931584 | tf_op jit(solution)/shard_map/dot_general | solution.py:96
  126.6 1.2 fusion.20
  127.9 3.4 %collective-permute-start.19 = (bf16[224,1024]{1,0:T(8,128)(2,1)}, bf16[224,1024]{1,0:T(8,128)(2,1)S(1)}, u32[]{:S(2)}, u32[]{:S(2)}) collective-permute-start(bf16[224,1024]{1,0:T(8,128)(2,1)} %get-tuple-element.161), channel_id=1, source_target_pairs={{16,17},{17,16},{18,19},{19,18},{20,21},{21,20},{22,23},{23,22},{2... | collective-permute-start | bytes 1376264 | tf_op jit(solution)/shard_map/ppermute | solution.py:289
  131.3 0.6 collective-permute-start.21
  131.9 1.5 collective-permute-start.18
  133.4 1.2 fusion.31
  134.6 1.2 fusion.17
  135.9 2.2 %fusion.2 = f32[224,1024]{1,0:T(8,128)} fusion(bf16[2048,1792]{1,0:T(8,128)(2,1)S(1)} %bitcast.28, bf16[448,1792]{1,0:T(8,128)(2,1)S(1)} %get-tuple-element.100.refs_1_), kind=kOutput, calls=%fused_computation.3 | convolution fusion | flops 822083584 | bytes 5390336 | tf_op jit(solution)/shard_map/dot_general | solution.py:96
  138.1 2.6 %copy-done.4 = bf16[1024,1792]{1,0:T(8,128)(2,1)S(1)} copy-done((bf16[1024,1792]{1,0:T(8,128)(2,1)S(1)}, bf16[1024,1792]{1,0:T(8,128)(2,1)}, u32[]{:S(2)}) %copy-start.4) | copy-done | bytes 3670040
  140.6 8.6 %shard_map.229 = (bf16[1024,1792]{1,0:T(8,128)(2,1)}, bf16[1024,1792]{1,0:T(8,128)(2,1)}, bf16[1024,1792]{1,0:T(8,128)(2,1)}) custom-call(bf16[448,1024]{1,0:T(8,128)(2,1)S(1)} %slice_select_fusion.2.refs_0_, bf16[448,1792]{1,0:T(8,128)(2,1)S(1)} %get-tuple-element.101.refs_1_, bf16[1024,1792]{1,0:T(8,128)(2,1)S(1)} %copy-done.2, ...), custom_call_target="tpu_custom_call" | custom-call | flops 1644167168 | bytes 22020096 | tf_op jit(solution)/shard_map/pallas_call | solution.py:68
  149.2 0.9 add_convert_fusion
  150.2 4.0 %collective-permute-start.20 = (bf16[224,1024]{1,0:T(8,128)(2,1)}, bf16[224,1024]{1,0:T(8,128)(2,1)S(1)}, u32[]{:S(2)}, u32[]{:S(2)}) collective-permute-start(bf16[224,1024]{1,0:T(8,128)(2,1)} %add_convert_fusion), channel_id=1, source_target_pairs={{16,0},{18,2},{20,4},{22,6},{24,8},{26,10},{28,12},{30,14},{17,1},... | collective-permute-start | bytes 1376264 | tf_op jit(solution)/shard_map/ppermute | solution.py:301
  154.5 1.6 collective-permute-start.24
  156.2 3.8 %copy-done = bf16[2048,1792]{1,0:T(8,128)(2,1)S(1)} copy-done((bf16[2048,1792]{1,0:T(8,128)(2,1)S(1)}, bf16[2048,1792]{1,0:T(8,128)(2,1)}, u32[]{:S(2)}) %copy-start) | copy-done | bytes 7340056
  160.0 16.1 %shard_map.230 = (bf16[2048,1792]{1,0:T(8,128)(2,1)}, bf16[2048,1792]{1,0:T(8,128)(2,1)}, bf16[2048,1792]{1,0:T(8,128)(2,1)}) custom-call(bf16[448,2048]{1,0:T(8,128)(2,1)S(1)} %maximum_maximum_fusion.refs_0_, bf16[448,1792]{1,0:T(8,128)(2,1)S(1)} %get-tuple-element.100.refs_1_, bf16[2048,1792]{1,0:T(8,128)(2,1)S(1)} %bitcast.30, ...), custom_call_target="tpu_custom_call" | custom-call | flops 3288334336 | bytes 44040192 | tf_op jit(solution)/shard_map/pallas_call | solution.py:68
  176.7 0.5 copy-done.7
  177.4 1.4 collective-permute-start.23
  178.9 8.6 %shard_map.231 = (bf16[1792,2048]{1,0:T(8,128)(2,1)}, bf16[1792,2048]{1,0:T(8,128)(2,1)}, bf16[1792,2048]{1,0:T(8,128)(2,1)}) custom-call(bf16[448,1792]{1,0:T(8,128)(2,1)S(1)} %pad_maximum_fusion.refs_0_, bf16[448,1024]{1,0:T(8,128)(2,1)S(1)} %pad_maximum_fusion.3.refs_1_, bf16[1792,2048]{1,0:T(8,128)(2,1)S(1)} %bitcast.22, ...), custom_call_target="tpu_custom_call" | custom-call | flops 1644167168 | bytes 22020096 | tf_op jit(solution)/shard_map/pallas_call | solution.py:68
  187.6 0.6 collective-permute-done.23
  188.2 8.6 %shard_map.232 = (bf16[1792,2048]{1,0:T(8,128)(2,1)}, bf16[1792,2048]{1,0:T(8,128)(2,1)}, bf16[1792,2048]{1,0:T(8,128)(2,1)}) custom-call(bf16[448,1792]{1,0:T(8,128)(2,1)S(1)} %pad_maximum_fusion.refs_0_, bf16[448,1024]{1,0:T(8,128)(2,1)S(1)} %pad_maximum_fusion.4.refs_1_, ...), custom_call_target="tpu_custom_call", output_to_operand_aliasing={{0}: (5, {}), {1}: (6, {}), {2}: (7, {})} | custom-call | flops 1644167168 | bytes 22020096 | tf_op jit(solution)/shard_map/pallas_call | solution.py:68
  196.9 0.6 fusion.40
  (109 shorter events, 4.3 us)
Async XLA Ops:
  0.7 7.6 %slice-start = ((s8[7340032]{0:T(1024)(128)(4,1)}), s8[4194304]{0:T(1024)(128)(4,1)S(1)}, s32[]{:S(2)}) async-start(s8[7340032]{0:T(1024)(128)(4,1)} %bitcast.19), calls=%async_computation | async-start | bytes 8388608
  2.3 5.9 %copy-start.6 = (bf16[224,1792]{1,0:T(8,128)(2,1)}, bf16[224,1792]{1,0:T(8,128)(2,1)S(1)}, u32[]{:S(2)}) copy-start(bf16[224,1792]{1,0:T(8,128)(2,1)S(1)} %get-tuple-element.143) | copy-start | bytes 2408452
  2.3 5.9 %slice-start.1 = ((s8[7340032]{0:T(1024)(128)(4,1)}), s8[3145728]{0:T(1024)(128)(4,1)S(1)}, s32[]{:S(2)}) async-start(s8[7340032]{0:T(1024)(128)(4,1)} %bitcast.19), calls=%async_computation.1 | async-start | bytes 6291456
  6.7 3.2 %copy-start.13 = (bf16[2048]{0:T(1024)(128)(2,1)S(1)}, bf16[2048]{0:T(1024)(128)(2,1)}, u32[]{:S(2)}) copy-start(bf16[2048]{0:T(1024)(128)(2,1)} %param.17) | copy-start | bytes 12292
  6.7 13.5 %collective-permute-start = (f16[224,1024]{1,0:T(8,128)(2,1)S(1)}, f16[224,1024]{1,0:T(8,128)(2,1)S(1)}, u32[]{:S(2)}, u32[]{:S(2)}) collective-permute-start(f16[224,1024]{1,0:T(8,128)(2,1)S(1)} %slice_convert_fusion), channel_id=1, source_target_pairs={{0,1},{1,0},{2,3},{3,2},{4,5},{5,4},{6,7},{7,6},{8,9},{9,8},{10,11... | collective-permute-start | bytes 1376264 | tf_op jit(solution)/shard_map/ppermute | solution.py:102
  9.2 19.6 %collective-permute-start.3 = (f16[224,1024]{1,0:T(8,128)(2,1)S(1)}, f16[224,1024]{1,0:T(8,128)(2,1)S(1)}, u32[]{:S(2)}, u32[]{:S(2)}) collective-permute-start(f16[224,1024]{1,0:T(8,128)(2,1)S(1)} %fusion.23), channel_id=1, source_target_pairs={{0,1},{1,0},{2,3},{3,2},{4,5},{5,4},{6,7},{7,6},{8,9},{9,8},{10,11... | collective-permute-start | bytes 1376264 | tf_op jit(solution)/shard_map/ppermute | solution.py:102
  21.3 13.1 %collective-permute-start.1 = (bf16[224,1024]{1,0:T(8,128)(2,1)S(1)}, bf16[224,1024]{1,0:T(8,128)(2,1)S(1)}, u32[]{:S(2)}, u32[]{:S(2)}) collective-permute-start(bf16[224,1024]{1,0:T(8,128)(2,1)S(1)} %get-tuple-element.140), channel_id=1, source_target_pairs={{0,16},{2,18},{4,20},{6,22},{8,24},{10,26},{12,28},{14,30},{1,17},... | collective-permute-start | bytes 1376264 | tf_op jit(solution)/shard_map/ppermute | solution.py:249
  30.8 13.5 %collective-permute-start.4 = (bf16[224,1024]{1,0:T(8,128)(2,1)S(1)}, bf16[224,1024]{1,0:T(8,128)(2,1)S(1)}, u32[]{:S(2)}, u32[]{:S(2)}) collective-permute-start(bf16[224,1024]{1,0:T(8,128)(2,1)S(1)} %get-tuple-element.71), channel_id=1, source_target_pairs={{0,1},{1,0},{2,3},{3,2},{4,5},{5,4},{6,7},{7,6},{8,9},{9,8},{10,11... | collective-permute-start | bytes 1376264 | tf_op jit(solution)/shard_map/ppermute | solution.py:102
  32.3 19.8 %collective-permute-start.5 = (bf16[224,1024]{1,0:T(8,128)(2,1)S(1)}, bf16[224,1024]{1,0:T(8,128)(2,1)}, u32[]{:S(2)}, u32[]{:S(2)}) collective-permute-start(bf16[224,1024]{1,0:T(8,128)(2,1)S(1)} %get-tuple-element.140), channel_id=1, source_target_pairs={{0,1},{1,0},{2,3},{3,2},{4,5},{5,4},{6,7},{7,6},{8,9},{9,8},{10,11... | collective-permute-start | bytes 1376264 | tf_op jit(solution)/shard_map/ppermute | solution.py:102
  34.4 9.9 %copy-start.11 = (bf16[224,1024]{1,0:T(8,128)(2,1)}, bf16[224,1024]{1,0:T(8,128)(2,1)S(1)}, u32[]{:S(2)}) copy-start(bf16[224,1024]{1,0:T(8,128)(2,1)S(1)} %collective-permute-done.1) | copy-start | bytes 1376260
  44.3 0.8 copy-start.10
  52.2 1.4 copy-start.12
  53.5 13.0 %copy-start.1 = (bf16[1024,1792]{1,0:T(8,128)(2,1)S(1)}, bf16[1024,1792]{1,0:T(8,128)(2,1)}, u32[]{:S(2)}) copy-start(bf16[1024,1792]{1,0:T(8,128)(2,1)} %refs_2_.4) | copy-start | bytes 11010052
  53.5 12.6 %collective-permute-start.2 = (bf16[224,1024]{1,0:T(8,128)(2,1)S(1)}, bf16[224,1024]{1,0:T(8,128)(2,1)S(1)}, u32[]{:S(2)}, u32[]{:S(2)}) collective-permute-start(bf16[224,1024]{1,0:T(8,128)(2,1)S(1)} %copy-done.12), channel_id=1, source_target_pairs={{16,17},{17,16},{18,19},{19,18},{20,21},{21,20},{22,23},{23,22},{2... | collective-permute-start | bytes 1376264 | tf_op jit(solution)/shard_map/ppermute | solution.py:250
  68.7 2.4 %collective-permute-start.7 = (bf16[224,1792]{1,0:T(8,128)(2,1)S(1)}, bf16[224,1792]{1,0:T(8,128)(2,1)S(1)}, u32[]{:S(2)}, u32[]{:S(2)}) collective-permute-start(bf16[224,1792]{1,0:T(8,128)(2,1)S(1)} %select_convert_fusion), channel_id=1, source_target_pairs={{0,2},{2,0},{4,6},{6,4},{8,10},{10,8},{12,14},{14,12},{16,18},{18,... | collective-permute-start | bytes 2408456 | tf_op jit(solution)/shard_map/ppermute | solution.py:107
  68.9 3.0 %collective-permute-start.6 = (bf16[224,1792]{1,0:T(8,128)(2,1)S(1)}, bf16[224,1792]{1,0:T(8,128)(2,1)S(1)}, u32[]{:S(2)}, u32[]{:S(2)}) collective-permute-start(bf16[224,1792]{1,0:T(8,128)(2,1)S(1)} %select_convert_fusion.1), channel_id=1, source_target_pairs={{0,2},{2,0},{4,6},{6,4},{8,10},{10,8},{12,14},{14,12},{1,3},{3,1},... | collective-permute-start | bytes 2408456 | tf_op jit(solution)/shard_map/ppermute | solution.py:107
  71.3 11.4 %collective-permute-start.9 = (bf16[112,1792]{1,0:T(8,128)(2,1)S(1)}, bf16[112,1792]{1,0:T(8,128)(2,1)S(1)}, u32[]{:S(2)}, u32[]{:S(2)}) collective-permute-start(bf16[112,1792]{1,0:T(8,128)(2,1)S(1)} %select_convert_fusion.5), channel_id=1, source_target_pairs={{0,4},{2,6},{4,0},{6,2},{8,12},{10,14},{12,8},{14,10},{16,20},{18,... | collective-permute-start | bytes 1204232 | tf_op jit(solution)/shard_map/ppermute | solution.py:107
  72.2 12.3 %collective-permute-start.8 = (bf16[112,1792]{1,0:T(8,128)(2,1)S(1)}, bf16[112,1792]{1,0:T(8,128)(2,1)S(1)}, u32[]{:S(2)}, u32[]{:S(2)}) collective-permute-start(bf16[112,1792]{1,0:T(8,128)(2,1)S(1)} %select_convert_fusion.4), channel_id=1, source_target_pairs={{0,8},{2,10},{4,12},{6,14},{8,0},{10,2},{12,4},{14,6},{1,9},{3,11}... | collective-permute-start | bytes 1204232 | tf_op jit(solution)/shard_map/ppermute | solution.py:107
  82.8 6.3 %collective-permute-start.11 = (bf16[112,896]{1,0:T(8,128)(2,1)S(1)}, bf16[112,896]{1,0:T(8,128)(2,1)S(1)}, u32[]{:S(2)}, u32[]{:S(2)}) collective-permute-start(bf16[112,896]{1,0:T(8,128)(2,1)S(1)} %select_convert_fusion.6), channel_id=1, source_target_pairs={{0,8},{2,10},{4,12},{6,14},{8,0},{10,2},{12,4},{14,6},{16,24},{18,... | collective-permute-start | bytes 602120 | tf_op jit(solution)/shard_map/ppermute | solution.py:107
  84.6 5.4 %collective-permute-start.10 = (bf16[112,1792]{1,0:T(8,128)(2,1)S(1)}, bf16[112,1792]{1,0:T(8,128)(2,1)S(1)}, u32[]{:S(2)}, u32[]{:S(2)}) collective-permute-start(bf16[112,1792]{1,0:T(8,128)(2,1)S(1)} %get-tuple-element.136), channel_id=1, source_target_pairs={{0,4},{2,6},{4,0},{6,2},{8,12},{10,14},{12,8},{14,10},{1,5},{3,7},... | collective-permute-start | bytes 1204232 | tf_op jit(solution)/shard_map/ppermute | solution.py:107
  90.0 7.7 %collective-permute-start.13 = (bf16[112,896]{1,0:T(8,128)(2,1)}, bf16[112,896]{1,0:T(8,128)(2,1)}, u32[]{:S(2)}, u32[]{:S(2)}) collective-permute-start(bf16[112,896]{1,0:T(8,128)(2,1)} %get-tuple-element.134), channel_id=1, source_target_pairs={{0,16},{2,18},{4,20},{6,22},{8,24},{10,26},{12,28},{14,30},{16,0},... | collective-permute-start | bytes 602120 | tf_op jit(solution)/shard_map/ppermute | solution.py:107
  91.9 11.7 %collective-permute-start.12 = (bf16[112,1792]{1,0:T(8,128)(2,1)}, bf16[112,1792]{1,0:T(8,128)(2,1)}, u32[]{:S(2)}, u32[]{:S(2)}) collective-permute-start(bf16[112,1792]{1,0:T(8,128)(2,1)} %fusion.30), channel_id=1, source_target_pairs={{0,8},{2,10},{4,12},{6,14},{8,0},{10,2},{12,4},{14,6},{1,9},{3,11}... | collective-permute-start | bytes 1204232 | tf_op jit(solution)/shard_map/ppermute | solution.py:107
  99.0 9.4 %collective-permute-start.15 = (bf16[112,896]{1,0:T(8,128)(2,1)S(1)}, bf16[112,896]{1,0:T(8,128)(2,1)S(1)}, u32[]{:S(2)}, u32[]{:S(2)}) collective-permute-start(bf16[112,896]{1,0:T(8,128)(2,1)S(1)} %fusion.37), channel_id=1, source_target_pairs={{0,8},{2,10},{4,12},{6,14},{8,0},{10,2},{12,4},{14,6},{16,24},{18,... | collective-permute-start | bytes 602120 | tf_op jit(solution)/shard_map/ppermute | solution.py:107
  108.4 10.3 %collective-permute-start.16 = (bf16[112,1792]{1,0:T(8,128)(2,1)S(1)}, bf16[112,1792]{1,0:T(8,128)(2,1)S(1)}, u32[]{:S(2)}, u32[]{:S(2)}) collective-permute-start(bf16[112,1792]{1,0:T(8,128)(2,1)S(1)} %pad_maximum_fusion.7), channel_id=1, source_target_pairs={{0,4},{2,6},{4,0},{6,2},{8,12},{10,14},{12,8},{14,10},{16,20},{18,... | collective-permute-start | bytes 1204232 | tf_op jit(solution)/shard_map/ppermute | solution.py:107
  109.0 9.9 %collective-permute-start.14 = (bf16[224,1792]{1,0:T(8,128)(2,1)S(1)}, bf16[224,1792]{1,0:T(8,128)(2,1)S(1)}, u32[]{:S(2)}, u32[]{:S(2)}) collective-permute-start(bf16[224,1792]{1,0:T(8,128)(2,1)S(1)} %pad_maximum_fusion.5), channel_id=1, source_target_pairs={{0,2},{2,0},{4,6},{6,4},{8,10},{10,8},{12,14},{14,12},{1,3},{3,1},... | collective-permute-start | bytes 2408456 | tf_op jit(solution)/shard_map/ppermute | solution.py:107
  118.8 2.6 %copy-start.2 = (bf16[1024,1792]{1,0:T(8,128)(2,1)S(1)}, bf16[1024,1792]{1,0:T(8,128)(2,1)}, u32[]{:S(2)}) copy-start(bf16[1024,1792]{1,0:T(8,128)(2,1)} %refs_2_.4) | copy-start | bytes 11010052
  118.9 2.4 %collective-permute-start.17 = (bf16[224,1792]{1,0:T(8,128)(2,1)S(1)}, bf16[224,1792]{1,0:T(8,128)(2,1)S(1)}, u32[]{:S(2)}, u32[]{:S(2)}) collective-permute-start(bf16[224,1792]{1,0:T(8,128)(2,1)S(1)} %pad_maximum_fusion.6), channel_id=1, source_target_pairs={{0,2},{2,0},{4,6},{6,4},{8,10},{10,8},{12,14},{14,12},{16,18},{18,... | collective-permute-start | bytes 2408456 | tf_op jit(solution)/shard_map/ppermute | solution.py:107
  121.2 2.8 %slice-start.8 = ((s8[7340032]{0:T(1024)(128)(4,1)}), s8[4194304]{0:T(1024)(128)(4,1)S(1)}, s32[]{:S(2)}) async-start(s8[7340032]{0:T(1024)(128)(4,1)} %bitcast.27), calls=%async_computation.8 | async-start | bytes 8388608
  121.5 3.2 %slice-start.9 = ((s8[7340032]{0:T(1024)(128)(4,1)}), s8[3145728]{0:T(1024)(128)(4,1)S(1)}, s32[]{:S(2)}) async-start(s8[7340032]{0:T(1024)(128)(4,1)} %bitcast.27), calls=%async_computation.9 | async-start | bytes 6291456
  127.9 21.4 %collective-permute-start.19 = (bf16[224,1024]{1,0:T(8,128)(2,1)}, bf16[224,1024]{1,0:T(8,128)(2,1)S(1)}, u32[]{:S(2)}, u32[]{:S(2)}) collective-permute-start(bf16[224,1024]{1,0:T(8,128)(2,1)} %get-tuple-element.161), channel_id=1, source_target_pairs={{16,17},{17,16},{18,19},{19,18},{20,21},{21,20},{22,23},{23,22},{2... | collective-permute-start | bytes 1376264 | tf_op jit(solution)/shard_map/ppermute | solution.py:289
  131.3 22.9 %collective-permute-start.21 = (bf16[224,1024]{1,0:T(8,128)(2,1)S(1)}, bf16[224,1024]{1,0:T(8,128)(2,1)S(1)}, u32[]{:S(2)}, u32[]{:S(2)}) collective-permute-start(bf16[224,1024]{1,0:T(8,128)(2,1)S(1)} %fusion.20), channel_id=1, source_target_pairs={{0,1},{1,0},{2,3},{3,2},{4,5},{5,4},{6,7},{7,6},{8,9},{9,8},{10,11... | collective-permute-start | bytes 1376264 | tf_op jit(solution)/shard_map/ppermute | solution.py:102
  131.9 44.3 %collective-permute-start.18 = (bf16[224,1024]{1,0:T(8,128)(2,1)}, bf16[224,1024]{1,0:T(8,128)(2,1)S(1)}, u32[]{:S(2)}, u32[]{:S(2)}) collective-permute-start(bf16[224,1024]{1,0:T(8,128)(2,1)} %fusion.26), channel_id=1, source_target_pairs={{0,1},{1,0},{2,3},{3,2},{4,5},{5,4},{6,7},{7,6},{8,9},{9,8},{10,11... | collective-permute-start | bytes 1376264 | tf_op jit(solution)/shard_map/ppermute | solution.py:102
  134.6 3.4 %copy-start.3 = (bf16[1024,1792]{1,0:T(8,128)(2,1)S(1)}, bf16[1024,1792]{1,0:T(8,128)(2,1)}, u32[]{:S(2)}) copy-start(bf16[1024,1792]{1,0:T(8,128)(2,1)} %refs_3_.4) | copy-start | bytes 11010052
  135.9 20.3 %slice-start.10 = ((s8[7340032]{0:T(1024)(128)(4,1)}), s8[4194304]{0:T(1024)(128)(4,1)S(1)}, s32[]{:S(2)}) async-start(s8[7340032]{0:T(1024)(128)(4,1)} %bitcast.29), calls=%async_computation.10 | async-start | bytes 8388608
  135.9 20.2 %slice-start.12 = ((s8[7340032]{0:T(1024)(128)(4,1)}), s8[4194304]{0:T(1024)(128)(4,1)S(1)}, s32[]{:S(2)}) async-start(s8[7340032]{0:T(1024)(128)(4,1)} %bitcast.31), calls=%async_computation.12 | async-start | bytes 8388608
  138.1 2.6 %copy-start.4 = (bf16[1024,1792]{1,0:T(8,128)(2,1)S(1)}, bf16[1024,1792]{1,0:T(8,128)(2,1)}, u32[]{:S(2)}) copy-start(bf16[1024,1792]{1,0:T(8,128)(2,1)} %refs_4_.4) | copy-start | bytes 11010052
  140.6 13.5 %copy-start.9 = (f32[224,1024]{1,0:T(8,128)S(1)}, f32[224,1024]{1,0:T(8,128)}, u32[]{:S(2)}) copy-start(f32[224,1024]{1,0:T(8,128)} %get-tuple-element.108) | copy-start | bytes 2752516
  140.6 15.5 %slice-start.11 = ((s8[7340032]{0:T(1024)(128)(4,1)}), s8[3145728]{0:T(1024)(128)(4,1)S(1)}, s32[]{:S(2)}) async-start(s8[7340032]{0:T(1024)(128)(4,1)} %bitcast.29), calls=%async_computation.11 | async-start | bytes 6291456
  140.6 15.5 %slice-start.13 = ((s8[7340032]{0:T(1024)(128)(4,1)}), s8[3145728]{0:T(1024)(128)(4,1)S(1)}, s32[]{:S(2)}) async-start(s8[7340032]{0:T(1024)(128)(4,1)} %bitcast.31), calls=%async_computation.13 | async-start | bytes 6291456
  150.2 26.0 %collective-permute-start.20 = (bf16[224,1024]{1,0:T(8,128)(2,1)}, bf16[224,1024]{1,0:T(8,128)(2,1)S(1)}, u32[]{:S(2)}, u32[]{:S(2)}) collective-permute-start(bf16[224,1024]{1,0:T(8,128)(2,1)} %add_convert_fusion), channel_id=1, source_target_pairs={{16,0},{18,2},{20,4},{22,6},{24,8},{26,10},{28,12},{30,14},{17,1},... | collective-permute-start | bytes 1376264 | tf_op jit(solution)/shard_map/ppermute | solution.py:301
  154.2 24.7 %slice-start.2 = ((s8[7340032]{0:T(1024)(128)(4,1)}), s8[4194304]{0:T(1024)(128)(4,1)S(1)}, s32[]{:S(2)}) async-start(s8[7340032]{0:T(1024)(128)(4,1)} %bitcast.21), calls=%async_computation.2 | async-start | bytes 8388608
  154.2 24.7 %slice-start.4 = ((s8[7340032]{0:T(1024)(128)(4,1)}), s8[4194304]{0:T(1024)(128)(4,1)S(1)}, s32[]{:S(2)}) async-start(s8[7340032]{0:T(1024)(128)(4,1)} %bitcast.23), calls=%async_computation.4 | async-start | bytes 8388608
  154.2 24.6 %slice-start.6 = ((s8[7340032]{0:T(1024)(128)(4,1)}), s8[4194304]{0:T(1024)(128)(4,1)S(1)}, s32[]{:S(2)}) async-start(s8[7340032]{0:T(1024)(128)(4,1)} %bitcast.25), calls=%async_computation.6 | async-start | bytes 8388608
  154.5 24.4 %slice-start.3 = ((s8[7340032]{0:T(1024)(128)(4,1)}), s8[3145728]{0:T(1024)(128)(4,1)S(1)}, s32[]{:S(2)}) async-start(s8[7340032]{0:T(1024)(128)(4,1)} %bitcast.21), calls=%async_computation.3 | async-start | bytes 6291456
  154.5 24.4 %slice-start.5 = ((s8[7340032]{0:T(1024)(128)(4,1)}), s8[3145728]{0:T(1024)(128)(4,1)S(1)}, s32[]{:S(2)}) async-start(s8[7340032]{0:T(1024)(128)(4,1)} %bitcast.23), calls=%async_computation.5 | async-start | bytes 6291456
  154.5 24.4 %slice-start.7 = ((s8[7340032]{0:T(1024)(128)(4,1)}), s8[3145728]{0:T(1024)(128)(4,1)S(1)}, s32[]{:S(2)}) async-start(s8[7340032]{0:T(1024)(128)(4,1)} %bitcast.25), calls=%async_computation.7 | async-start | bytes 6291456
  154.5 24.2 %collective-permute-start.24 = (bf16[224,1024]{1,0:T(8,128)(2,1)S(1)}, bf16[224,1024]{1,0:T(8,128)(2,1)S(1)}, u32[]{:S(2)}, u32[]{:S(2)}) collective-permute-start(bf16[224,1024]{1,0:T(8,128)(2,1)S(1)} %get-tuple-element.119), channel_id=1, source_target_pairs={{0,1},{1,0},{2,3},{3,2},{4,5},{5,4},{6,7},{7,6},{8,9},{9,8},{10,11... | collective-permute-start | bytes 1376264 | tf_op jit(solution)/shard_map/ppermute | solution.py:102
  156.1 3.9 %copy-start = (bf16[2048,1792]{1,0:T(8,128)(2,1)S(1)}, bf16[2048,1792]{1,0:T(8,128)(2,1)}, u32[]{:S(2)}) copy-start(bf16[2048,1792]{1,0:T(8,128)(2,1)} %refs_3_.5) | copy-start | bytes 22020100
  160.0 16.2 %copy-start.5 = (f32[224,1024]{1,0:T(8,128)S(1)}, f32[224,1024]{1,0:T(8,128)}, u32[]{:S(2)}) copy-start(f32[224,1024]{1,0:T(8,128)} %get-tuple-element.115) | copy-start | bytes 2752516
  160.0 16.2 %copy-start.8 = (f32[224,1024]{1,0:T(8,128)S(1)}, f32[224,1024]{1,0:T(8,128)}, u32[]{:S(2)}) copy-start(f32[224,1024]{1,0:T(8,128)} %fusion.2) | copy-start | bytes 2752516
  176.1 1.1 copy-start.7
  176.5 11.6 %collective-permute-start.22 = (bf16[224,1024]{1,0:T(8,128)(2,1)S(1)}, bf16[224,1024]{1,0:T(8,128)(2,1)S(1)}, u32[]{:S(2)}, u32[]{:S(2)}) collective-permute-start(bf16[224,1024]{1,0:T(8,128)(2,1)S(1)} %get-tuple-element.124), channel_id=1, source_target_pairs={{0,1},{1,0},{2,3},{3,2},{4,5},{5,4},{6,7},{7,6},{8,9},{9,8},{10,11... | collective-permute-start | bytes 1376264 | tf_op jit(solution)/shard_map/ppermute | solution.py:102
  177.4 10.7 %collective-permute-start.23 = (f32[2048]{0:T(1024)S(1)}, f32[2048]{0:T(1024)S(1)}, u32[]{:S(2)}, u32[]{:S(2)}) collective-permute-start(f32[2048]{0:T(1024)S(1)} %pad_maximum_fusion.8), channel_id=1, source_target_pairs={{0,1},{1,0},{2,3},{3,2},{4,5},{5,4},{6,7},{7,6},{8,9},{9,8},{10,11... | collective-permute-start | bytes 24584 | tf_op jit(solution)/shard_map/ppermute | solution.py:102
  188.2 8.7 %copy-start.14 = (bf16[2048]{0:T(1024)(128)(2,1)S(1)}, bf16[2048]{0:T(1024)(128)(2,1)}, u32[]{:S(2)}) copy-start(bf16[2048]{0:T(1024)(128)(2,1)} %param.17) | copy-start | bytes 12292
  188.2 8.7 %copy-start.15 = (bf16[2048]{0:T(1024)(128)(2,1)S(1)}, bf16[2048]{0:T(1024)(128)(2,1)}, u32[]{:S(2)}) copy-start(bf16[2048]{0:T(1024)(128)(2,1)} %param.23) | copy-start | bytes 12292
  188.2 8.7 %copy-start.16 = (bf16[2048]{0:T(1024)(128)(2,1)S(1)}, bf16[2048]{0:T(1024)(128)(2,1)}, u32[]{:S(2)}) copy-start(bf16[2048]{0:T(1024)(128)(2,1)} %param.22) | copy-start | bytes 12292

commit v4 on v3

--- a/solution.py
+++ b/solution.py
@@ -62,7 +62,7 @@
     tokens = left.shape[0]
     rows, width = weight.shape
     span = width // share[1]
-    block = math.gcd(rows, 256 if span <= 1024 else 128)
+    block = math.gcd(rows, 256)
     tile = math.gcd(span, 256)
     strip = pl.BlockSpec((block, span), lambda place: (place, share[0]))
     return pl.pallas_call(
@@ -79,7 +79,7 @@
         out_specs=[strip] * 3,
         out_shape=[jax.ShapeDtypeStruct((rows, width), jnp.bfloat16)] * 3,
         input_output_aliases={5 + at: at for at in range(len(partly_done))},
-        compiler_params=pltpu.CompilerParams(vmem_limit_bytes=14 * 2**20),
+        compiler_params=pltpu.CompilerParams(vmem_limit_bytes=18 * 2**20),
         cost_estimate=pl.CostEstimate(
             flops=2 * tokens * rows * span,
             bytes_accessed=12 * rows * span,
@@ -269,12 +269,9 @@
     order.start(
         1, summed_steps(second_part, second_plan, feat_count, wanted_block(1, second_plan))
     )
-    left = [len(plan) + len(plan) - 1 for plan in (first_plan, second_plan)]
-    while left[1] > 0:
-        for layer in (1, 0):
-            if left[layer] > 0:
-                order.advance(layer)
-                left[layer] -= 1
+    turns = [1, 0] * len(first_plan) + [1] + [1, 0] * (len(first_plan) - 1) + [1]
+    for layer in turns:
+        order.advance(layer)
     delta_first, delta_next = order.result(0), order.result(1)
     delta_own = jnp.where(leading, delta_first, delta_next)
 

time: 200 us -> 199 us (level); the launches traced: 198 us -> 199 us
  waiting for transfers between devices: 71.8 us -> 78.4 us
  Pallas kernels: 42 us -> 38 us
  local copies, waits for them, and re-layouts: 10.2 us -> 13.5 us
    pallas_call x4, Pallas kernels: 42 us -> 38 us  [adamw_matmul(): pl.pallas_call(functools.partial(adamw_kernel, decay_rate, tile), grid=(r...]
    ppermute x9, waiting for transfers between devices: 34.1 us -> 37.8 us  [across(): return lax.ppermute(value, 'width', [(0, 1), (1, 0)])]
    unnamed x62 -> x56, local copies, waits for them, and re-layouts: 8.5 us -> 11.8 us
    ppermute x12, waiting for transfers between devices: 33.7 us -> 35.9 us  [flipped(): lax.ppermute(value, 'feat', [(index, index ^ step) for index in range(mem...]
  transfers between devices with their start and end apart: 25 -> 25, of which waited for: 14 -> 14; matrix products, arithmetic and copies ran while one was open for 12% -> 11% of each run, Pallas kernels for 17% -> 15%
where the time goes in v4:
time: 199 us
  waiting for transfers between devices  78.4 us (39%)
  Pallas kernels  38 us (19%)
  starting transfers between devices  31.9 us (16%)
  matrix products  24.1 us (12%)
  local copies, waits for them, and re-layouts  13.5 us (7%)
  other arithmetic  11.6 us (6%)
    pallas_call x4, Pallas kernels, adamw_matmul(): pl.pallas_call(functools.partial(adamw_kernel, decay_rate, tile), grid=(r...  38 us
    ppermute x9, waiting for transfers between devices, across(): return lax.ppermute(value, 'width', [(0, 1), (1, 0)])  37.8 us
    ppermute x12, waiting for transfers between devices, flipped(): lax.ppermute(value, 'feat', [(index, index ^ step) for index in range(mem...  35.9 us
    dot_general x5, matrix products, matmul(): return jnp.dot(left, right, preferred_element_type=jnp.float32)  15 us
    unnamed x56, local copies, waits for them, and re-layouts  11.8 us
    ppermute x12, starting transfers between devices, flipped(): lax.ppermute(value, 'feat', [(index, index ^ step) for index in range(mem...  11.3 us
    ppermute x9, starting transfers between devices, across(): return lax.ppermute(value, 'width', [(0, 1), (1, 0)])  10.1 us
    dot_general x6, matrix products, over_cols(): lax.dot_general(left, right, (((1,), (1,)), ((), ())), preferred_element_...  9.08 us
  transfers between devices with their start and end apart: 25, of which 14 were waited for; matrix products, arithmetic and copies ran while one was open for 11% of the time, Pallas kernels for 15%

profile of v4, /device:TPU:20, one launch (start us, length us, event | category | flops | bytes accessed | tf_op | source)
XLA Modules:
  0.0 198.8 jit_solution(14581761102004394755)
XLA Ops:
  0.7 1.6 dynamic-slice_bitcast_fusion.1
  2.4 4.5 %fusion = f32[448,1024]{1,0:T(8,128)S(1)} fusion(bf16[1792,2048]{1,0:T(8,128)(2,1)} %refs_2_.7, bf16[224,1792]{1,0:T(8,128)(2,1)S(1)} %get-tuple-element.143, bf16[224,1792]{1,0:T(8,128)(2,1)S(1)} %get-tuple-element.142), kind=kOutput, calls=%fused_computation.1 | convolution fusion | flops 1647378432 | bytes 7110656 | tf_op jit(solution)/shard_map/dot_general | solution.py:92
  7.0 1.6 collective-permute-start
  8.5 1.0 fusion.23
  9.5 0.6 collective-permute-start.3
  10.2 10.3 %collective-permute-done = f16[224,1024]{1,0:T(8,128)(2,1)S(1)} collective-permute-done((f16[224,1024]{1,0:T(8,128)(2,1)S(1)}, f16[224,1024]{1,0:T(8,128)(2,1)S(1)}, u32[]{:S(2)}, u32[]{:S(2)}) %collective-permute-start) | collective-permute-done | bytes 458784 | tf_op jit(solution)/shard_map/ppermute | solution.py:102
  20.5 1.1 maximum_convert_fusion.1
  21.6 1.3 collective-permute-start.1
  22.9 6.3 %collective-permute-done.3 = f16[224,1024]{1,0:T(8,128)(2,1)S(1)} collective-permute-done((f16[224,1024]{1,0:T(8,128)(2,1)S(1)}, f16[224,1024]{1,0:T(8,128)(2,1)S(1)}, u32[]{:S(2)}, u32[]{:S(2)}) %collective-permute-start.3) | collective-permute-done | bytes 458784 | tf_op jit(solution)/shard_map/ppermute | solution.py:102
  29.1 1.0 maximum_convert_fusion
  30.2 1.6 collective-permute-start.4
  31.7 0.5 collective-permute-start.5
  32.3 2.4 %collective-permute-done.1 = bf16[224,1024]{1,0:T(8,128)(2,1)S(1)} collective-permute-done((bf16[224,1024]{1,0:T(8,128)(2,1)S(1)}, bf16[224,1024]{1,0:T(8,128)(2,1)S(1)}, u32[]{:S(2)}, u32[]{:S(2)}) %collective-permute-start.1) | collective-permute-done | bytes 458784 | tf_op jit(solution)/shard_map/ppermute | solution.py:249
  34.7 9.0 %collective-permute-done.4 = bf16[224,1024]{1,0:T(8,128)(2,1)S(1)} collective-permute-done((bf16[224,1024]{1,0:T(8,128)(2,1)S(1)}, bf16[224,1024]{1,0:T(8,128)(2,1)S(1)}, u32[]{:S(2)}, u32[]{:S(2)}) %collective-permute-start.4) | collective-permute-done | bytes 458784 | tf_op jit(solution)/shard_map/ppermute | solution.py:102
  43.7 7.8 %collective-permute-done.5 = bf16[224,1024]{1,0:T(8,128)(2,1)S(1)} collective-permute-done((bf16[224,1024]{1,0:T(8,128)(2,1)S(1)}, bf16[224,1024]{1,0:T(8,128)(2,1)S(1)}, u32[]{:S(2)}, u32[]{:S(2)}) %collective-permute-start.5) | collective-permute-done | bytes 458784 | tf_op jit(solution)/shard_map/ppermute | solution.py:102
  51.6 3.7 %collective-permute-start.2 = (bf16[224,1024]{1,0:T(8,128)(2,1)S(1)}, bf16[224,1024]{1,0:T(8,128)(2,1)S(1)}, u32[]{:S(2)}, u32[]{:S(2)}) collective-permute-start(bf16[224,1024]{1,0:T(8,128)(2,1)S(1)} %collective-permute-done.1), channel_id=1, source_target_pairs={{16,17},{17,16},{18,19},{19,18},{20,21},{21,20},{22,23},{23,22},{2... | collective-permute-start | bytes 1376264 | tf_op jit(solution)/shard_map/ppermute | solution.py:250
  55.3 6.6 %fusion.46 = f32[448,1792]{1,0:T(8,128)S(1)} fusion(bf16[448,2048]{1,0:T(8,128)(2,1)S(1)} %maximum_maximum_fusion.refs_0_, bf16[2048,1792]{1,0:T(8,128)(2,1)} %refs_2_.5), kind=kOutput, calls=%fused_computation.90 | convolution fusion | flops 3288334336 | bytes 12386304 | tf_op jit(solution)/shard_map/dot_general | solution.py:92
  61.9 2.3 %collective-permute-done.2 = bf16[224,1024]{1,0:T(8,128)(2,1)S(1)} collective-permute-done((bf16[224,1024]{1,0:T(8,128)(2,1)S(1)}, bf16[224,1024]{1,0:T(8,128)(2,1)S(1)}, u32[]{:S(2)}, u32[]{:S(2)}) %collective-permute-start.2) | collective-permute-done | bytes 458784 | tf_op jit(solution)/shard_map/ppermute | solution.py:250
  64.3 0.3 slice_select_fusion.2.refs_0_
  64.6 1.9 add_select_fusion
  67.0 0.7 collective-permute-start.6
  67.9 1.2 collective-permute-done.7
  69.4 0.6 collective-permute-start.9
  70.3 0.7 collective-permute-start.8
  71.1 9.7 %collective-permute-done.9 = bf16[112,1792]{1,0:T(8,128)(2,1)S(1)} collective-permute-done((bf16[112,1792]{1,0:T(8,128)(2,1)S(1)}, bf16[112,1792]{1,0:T(8,128)(2,1)S(1)}, u32[]{:S(2)}, u32[]{:S(2)}) %collective-permute-start.9) | collective-permute-done | bytes 401440 | tf_op jit(solution)/shard_map/ppermute | solution.py:107
  80.9 1.7 collective-permute-start.11
  82.7 0.7 collective-permute-start.10
  83.4 3.8 %collective-permute-done.11 = bf16[112,896]{1,0:T(8,128)(2,1)S(1)} collective-permute-done((bf16[112,896]{1,0:T(8,128)(2,1)S(1)}, bf16[112,896]{1,0:T(8,128)(2,1)S(1)}, u32[]{:S(2)}, u32[]{:S(2)}) %collective-permute-start.11) | collective-permute-done | bytes 200736 | tf_op jit(solution)/shard_map/ppermute | solution.py:107
  87.4 1.2 fusion.30
  88.6 6.2 %collective-permute-done.13 = bf16[112,896]{1,0:T(8,128)(2,1)S(1)} collective-permute-done((bf16[112,896]{1,0:T(8,128)(2,1)S(1)}, bf16[112,896]{1,0:T(8,128)(2,1)S(1)}, u32[]{:S(2)}, u32[]{:S(2)}) %collective-permute-start.13) | collective-permute-done | bytes 200736 | tf_op jit(solution)/shard_map/ppermute | solution.py:107
  94.7 1.1 fusion.37
  95.8 4.6 %collective-permute-start.14 = (bf16[112,896]{1,0:T(8,128)(2,1)S(1)}, bf16[112,896]{1,0:T(8,128)(2,1)S(1)}, u32[]{:S(2)}, u32[]{:S(2)}) collective-permute-start(bf16[112,896]{1,0:T(8,128)(2,1)S(1)} %fusion.37), channel_id=1, source_target_pairs={{0,8},{2,10},{4,12},{6,14},{8,0},{10,2},{12,4},{14,6},{16,24},{18,... | collective-permute-start | bytes 602120 | tf_op jit(solution)/shard_map/ppermute | solution.py:107
  100.4 0.7 collective-permute-start.12
  101.1 4.1 %collective-permute-done.14 = bf16[112,896]{1,0:T(8,128)(2,1)S(1)} collective-permute-done((bf16[112,896]{1,0:T(8,128)(2,1)S(1)}, bf16[112,896]{1,0:T(8,128)(2,1)S(1)}, u32[]{:S(2)}, u32[]{:S(2)}) %collective-permute-start.14) | collective-permute-done | bytes 200736 | tf_op jit(solution)/shard_map/ppermute | solution.py:107
  105.3 0.6 collective-permute-start.16
  106.0 0.9 collective-permute-start.15
  106.9 8.7 %collective-permute-done.16 = bf16[112,1792]{1,0:T(8,128)(2,1)S(1)} collective-permute-done((bf16[112,1792]{1,0:T(8,128)(2,1)S(1)}, bf16[112,1792]{1,0:T(8,128)(2,1)S(1)}, u32[]{:S(2)}, u32[]{:S(2)}) %collective-permute-start.16) | collective-permute-done | bytes 401440 | tf_op jit(solution)/shard_map/ppermute | solution.py:107
  115.8 2.3 %collective-permute-done.17 = bf16[224,1792]{1,0:T(8,128)(2,1)S(1)} collective-permute-done((bf16[224,1792]{1,0:T(8,128)(2,1)S(1)}, bf16[224,1792]{1,0:T(8,128)(2,1)S(1)}, u32[]{:S(2)}, u32[]{:S(2)}) %collective-permute-start.17) | collective-permute-done | bytes 802848 | tf_op jit(solution)/shard_map/ppermute | solution.py:107
  118.3 1.2 fusion.45
  119.5 0.5 pad_maximum_fusion.2
  120.2 1.5 slice-done.9
  121.7 2.0 %fusion.26 = bf16[224,1024]{1,0:T(8,128)(2,1)} fusion(bf16[2048,1792]{1,0:T(8,128)(2,1)S(1)} %bitcast.28, bf16[448,1792]{1,0:T(8,128)(2,1)S(1)} %get-tuple-element.100.refs_1_), kind=kOutput, calls=%fused_computation.30 | convolution fusion | flops 822312960 | bytes 4931584 | tf_op jit(solution)/shard_map/dot_general | solution.py:96
  123.7 1.2 fusion.20
  125.0 3.4 %collective-permute-start.19 = (bf16[224,1024]{1,0:T(8,128)(2,1)S(1)}, bf16[224,1024]{1,0:T(8,128)(2,1)S(1)}, u32[]{:S(2)}, u32[]{:S(2)}) collective-permute-start(bf16[224,1024]{1,0:T(8,128)(2,1)S(1)} %get-tuple-element.161), channel_id=1, source_target_pairs={{16,17},{17,16},{18,19},{19,18},{20,21},{21,20},{22,23},{23,22},{2... | collective-permute-start | bytes 1376264 | tf_op jit(solution)/shard_map/ppermute | solution.py:286
  128.4 0.6 collective-permute-start.21
  129.0 1.5 collective-permute-start.18
  130.5 1.2 fusion.31
  131.7 1.2 fusion.17
  133.0 2.2 %fusion.2 = f32[224,1024]{1,0:T(8,128)} fusion(bf16[2048,1792]{1,0:T(8,128)(2,1)S(1)} %bitcast.28, bf16[448,1792]{1,0:T(8,128)(2,1)S(1)} %get-tuple-element.100.refs_1_), kind=kOutput, calls=%fused_computation.3 | convolution fusion | flops 822083584 | bytes 5390336 | tf_op jit(solution)/shard_map/dot_general | solution.py:96
  135.2 7.4 %shard_map.229 = (bf16[1024,1792]{1,0:T(8,128)(2,1)}, bf16[1024,1792]{1,0:T(8,128)(2,1)}, bf16[1024,1792]{1,0:T(8,128)(2,1)}) custom-call(bf16[448,1024]{1,0:T(8,128)(2,1)S(1)} %slice_select_fusion.2.refs_0_, bf16[448,1792]{1,0:T(8,128)(2,1)S(1)} %get-tuple-element.101.refs_1_, bf16[1024,1792]{1,0:T(8,128)(2,1)S(1)} %copy-done.6, ...), custom_call_target="tpu_custom_call" | custom-call | flops 1644167168 | bytes 22020096 | tf_op jit(solution)/shard_map/pallas_call | solution.py:68
  142.7 0.9 add_convert_fusion
  143.6 2.1 %collective-permute-start.20 = (bf16[224,1024]{1,0:T(8,128)(2,1)}, bf16[224,1024]{1,0:T(8,128)(2,1)}, u32[]{:S(2)}, u32[]{:S(2)}) collective-permute-start(bf16[224,1024]{1,0:T(8,128)(2,1)} %add_convert_fusion), channel_id=1, source_target_pairs={{16,0},{18,2},{20,4},{22,6},{24,8},{26,10},{28,12},{30,14},{17,1},... | collective-permute-start | bytes 1376264 | tf_op jit(solution)/shard_map/ppermute | solution.py:298
  145.6 4.4 %collective-permute-done.21 = bf16[224,1024]{1,0:T(8,128)(2,1)S(1)} collective-permute-done((bf16[224,1024]{1,0:T(8,128)(2,1)S(1)}, bf16[224,1024]{1,0:T(8,128)(2,1)S(1)}, u32[]{:S(2)}, u32[]{:S(2)}) %collective-permute-start.21) | collective-permute-done | bytes 458784 | tf_op jit(solution)/shard_map/ppermute | solution.py:102
  150.3 1.6 collective-permute-start.24
  152.0 3.8 %copy-done.2 = bf16[2048,1792]{1,0:T(8,128)(2,1)S(1)} copy-done((bf16[2048,1792]{1,0:T(8,128)(2,1)S(1)}, bf16[2048,1792]{1,0:T(8,128)(2,1)}, u32[]{:S(2)}) %copy-start.2) | copy-done | bytes 7340056
  155.8 3.9 %copy-done.3 = bf16[2048,1792]{1,0:T(8,128)(2,1)S(1)} copy-done((bf16[2048,1792]{1,0:T(8,128)(2,1)S(1)}, bf16[2048,1792]{1,0:T(8,128)(2,1)}, u32[]{:S(2)}) %copy-start.3) | copy-done | bytes 7340056
  159.7 2.2 %copy-done.5 = bf16[448,1792]{1,0:T(8,128)(2,1)S(1)} copy-done((bf16[448,1792]{1,0:T(8,128)(2,1)S(1)}, bf16[448,1792]{1,0:T(8,128)(2,1)}, u32[]{:S(2)}) %copy-start.5) | copy-done | bytes 1605656
  161.9 13.4 %shard_map.230 = (bf16[2048,1792]{1,0:T(8,128)(2,1)}, bf16[2048,1792]{1,0:T(8,128)(2,1)}, bf16[2048,1792]{1,0:T(8,128)(2,1)}) custom-call(bf16[448,2048]{1,0:T(8,128)(2,1)S(1)} %copy-done.1, bf16[448,1792]{1,0:T(8,128)(2,1)S(1)} %copy-done.5, bf16[2048,1792]{1,0:T(8,128)(2,1)S(1)} %copy-done.2, bf16[2048,1792]{1,0:T(8,128)(2,1)S(1)} %copy-done.3, ...), custom_call_target="tpu_custom_call" | custom-call | flops 3288334336 | bytes 44040192 | tf_op jit(solution)/shard_map/pallas_call | solution.py:68
  175.3 2.1 %convert_reduce_fusion = (f32[1024]{0:T(1024)S(1)}, bf16[224,1024]{1,0:T(8,128)(2,1)S(1)}) fusion(bf16[224,1024]{1,0:T(8,128)(2,1)} %collective-permute-done.20, f32[224,1024]{1,0:T(8,128)} %fusion.2, bf16[224,1024]{1,0:T(8,128)(2,1)} %collective-permute-done.18, f32[224,1024]{1,0:T(8,128)} %get-tuple-element.115), kind=kLoop, calls=%fused_computation.37 | loop fusion | flops 2063360 | bytes 3215360 | tf_op jit(solution)/shard_map/reduce_sum | solution.py:313
  177.8 1.9 collective-permute-start.23
  179.7 1.1 pad_maximum_fusion.3.refs_1_
  180.9 8.6 %shard_map.231 = (bf16[1792,2048]{1,0:T(8,128)(2,1)}, bf16[1792,2048]{1,0:T(8,128)(2,1)}, bf16[1792,2048]{1,0:T(8,128)(2,1)}) custom-call(bf16[448,1792]{1,0:T(8,128)(2,1)S(1)} %pad_maximum_fusion.refs_0_, bf16[448,1024]{1,0:T(8,128)(2,1)S(1)} %pad_maximum_fusion.3.refs_1_, bf16[1792,2048]{1,0:T(8,128)(2,1)S(1)} %bitcast.22, ...), custom_call_target="tpu_custom_call" | custom-call | flops 1644167168 | bytes 22020096 | tf_op jit(solution)/shard_map/pallas_call | solution.py:68
  189.6 8.6 %shard_map.232 = (bf16[1792,2048]{1,0:T(8,128)(2,1)}, bf16[1792,2048]{1,0:T(8,128)(2,1)}, bf16[1792,2048]{1,0:T(8,128)(2,1)}) custom-call(bf16[448,1792]{1,0:T(8,128)(2,1)S(1)} %pad_maximum_fusion.refs_0_, bf16[448,1024]{1,0:T(8,128)(2,1)S(1)} %pad_maximum_fusion.4.refs_1_, ...), custom_call_target="tpu_custom_call", output_to_operand_aliasing={{0}: (5, {}), {1}: (6, {}), {2}: (7, {})} | custom-call | flops 1644167168 | bytes 22020096 | tf_op jit(solution)/shard_map/pallas_call | solution.py:68
  198.2 0.6 fusion.40
  (102 shorter events, 3.6 us)
Async XLA Ops:
  0.7 7.9 %slice-start = ((s8[7340032]{0:T(1024)(128)(4,1)}), s8[4194304]{0:T(1024)(128)(4,1)S(1)}, s32[]{:S(2)}) async-start(s8[7340032]{0:T(1024)(128)(4,1)} %bitcast.19), calls=%async_computation | async-start | bytes 8388608
  2.3 6.2 %copy-start.11 = (bf16[224,1792]{1,0:T(8,128)(2,1)}, bf16[224,1792]{1,0:T(8,128)(2,1)S(1)}, u32[]{:S(2)}) copy-start(bf16[224,1792]{1,0:T(8,128)(2,1)S(1)} %get-tuple-element.143) | copy-start | bytes 2408452
  2.3 26.8 %copy-start.9 = (bf16[224,1792]{1,0:T(8,128)(2,1)}, bf16[224,1792]{1,0:T(8,128)(2,1)S(1)}, u32[]{:S(2)}) copy-start(bf16[224,1792]{1,0:T(8,128)(2,1)S(1)} %get-tuple-element.142) | copy-start | bytes 2408452
  2.3 6.2 %slice-start.1 = ((s8[7340032]{0:T(1024)(128)(4,1)}), s8[3145728]{0:T(1024)(128)(4,1)S(1)}, s32[]{:S(2)}) async-start(s8[7340032]{0:T(1024)(128)(4,1)} %bitcast.19), calls=%async_computation.1 | async-start | bytes 6291456
  7.0 3.2 %copy-start.13 = (bf16[2048]{0:T(1024)(128)(2,1)S(1)}, bf16[2048]{0:T(1024)(128)(2,1)}, u32[]{:S(2)}) copy-start(bf16[2048]{0:T(1024)(128)(2,1)} %param.17) | copy-start | bytes 12292
  7.0 13.5 %collective-permute-start = (f16[224,1024]{1,0:T(8,128)(2,1)S(1)}, f16[224,1024]{1,0:T(8,128)(2,1)S(1)}, u32[]{:S(2)}, u32[]{:S(2)}) collective-permute-start(f16[224,1024]{1,0:T(8,128)(2,1)S(1)} %slice_convert_fusion), channel_id=1, source_target_pairs={{0,1},{1,0},{2,3},{3,2},{4,5},{5,4},{6,7},{7,6},{8,9},{9,8},{10,11... | collective-permute-start | bytes 1376264 | tf_op jit(solution)/shard_map/ppermute | solution.py:102
  9.5 19.6 %collective-permute-start.3 = (f16[224,1024]{1,0:T(8,128)(2,1)S(1)}, f16[224,1024]{1,0:T(8,128)(2,1)S(1)}, u32[]{:S(2)}, u32[]{:S(2)}) collective-permute-start(f16[224,1024]{1,0:T(8,128)(2,1)S(1)} %fusion.23), channel_id=1, source_target_pairs={{0,1},{1,0},{2,3},{3,2},{4,5},{5,4},{6,7},{7,6},{8,9},{9,8},{10,11... | collective-permute-start | bytes 1376264 | tf_op jit(solution)/shard_map/ppermute | solution.py:102
  21.6 13.1 %collective-permute-start.1 = (bf16[224,1024]{1,0:T(8,128)(2,1)S(1)}, bf16[224,1024]{1,0:T(8,128)(2,1)S(1)}, u32[]{:S(2)}, u32[]{:S(2)}) collective-permute-start(bf16[224,1024]{1,0:T(8,128)(2,1)S(1)} %get-tuple-element.140), channel_id=1, source_target_pairs={{0,16},{2,18},{4,20},{6,22},{8,24},{10,26},{12,28},{14,30},{1,17},... | collective-permute-start | bytes 1376264 | tf_op jit(solution)/shard_map/ppermute | solution.py:249
  30.2 13.5 %collective-permute-start.4 = (bf16[224,1024]{1,0:T(8,128)(2,1)S(1)}, bf16[224,1024]{1,0:T(8,128)(2,1)S(1)}, u32[]{:S(2)}, u32[]{:S(2)}) collective-permute-start(bf16[224,1024]{1,0:T(8,128)(2,1)S(1)} %get-tuple-element.71), channel_id=1, source_target_pairs={{0,1},{1,0},{2,3},{3,2},{4,5},{5,4},{6,7},{7,6},{8,9},{9,8},{10,11... | collective-permute-start | bytes 1376264 | tf_op jit(solution)/shard_map/ppermute | solution.py:102
  31.7 19.7 %collective-permute-start.5 = (bf16[224,1024]{1,0:T(8,128)(2,1)S(1)}, bf16[224,1024]{1,0:T(8,128)(2,1)S(1)}, u32[]{:S(2)}, u32[]{:S(2)}) collective-permute-start(bf16[224,1024]{1,0:T(8,128)(2,1)S(1)} %get-tuple-element.140), channel_id=1, source_target_pairs={{0,1},{1,0},{2,3},{3,2},{4,5},{5,4},{6,7},{7,6},{8,9},{9,8},{10,11... | collective-permute-start | bytes 1376264 | tf_op jit(solution)/shard_map/ppermute | solution.py:102
  51.6 12.6 %copy-start = (bf16[448,2048]{1,0:T(8,128)(2,1)}, bf16[448,2048]{1,0:T(8,128)(2,1)S(1)}, u32[]{:S(2)}) copy-start(bf16[448,2048]{1,0:T(8,128)(2,1)S(1)} %maximum_maximum_fusion.refs_0_) | copy-start | bytes 5505028
  51.6 13.0 %copy-start.6 = (bf16[1024,1792]{1,0:T(8,128)(2,1)S(1)}, bf16[1024,1792]{1,0:T(8,128)(2,1)}, u32[]{:S(2)}) copy-start(bf16[1024,1792]{1,0:T(8,128)(2,1)} %refs_2_.4) | copy-start | bytes 11010052
  51.6 12.6 %collective-permute-start.2 = (bf16[224,1024]{1,0:T(8,128)(2,1)S(1)}, bf16[224,1024]{1,0:T(8,128)(2,1)S(1)}, u32[]{:S(2)}, u32[]{:S(2)}) collective-permute-start(bf16[224,1024]{1,0:T(8,128)(2,1)S(1)} %collective-permute-done.1), channel_id=1, source_target_pairs={{16,17},{17,16},{18,19},{19,18},{20,21},{21,20},{22,23},{23,22},{2... | collective-permute-start | bytes 1376264 | tf_op jit(solution)/shard_map/ppermute | solution.py:250
  66.8 2.4 %collective-permute-start.7 = (bf16[224,1792]{1,0:T(8,128)(2,1)S(1)}, bf16[224,1792]{1,0:T(8,128)(2,1)S(1)}, u32[]{:S(2)}, u32[]{:S(2)}) collective-permute-start(bf16[224,1792]{1,0:T(8,128)(2,1)S(1)} %select_convert_fusion), channel_id=1, source_target_pairs={{0,2},{2,0},{4,6},{6,4},{8,10},{10,8},{12,14},{14,12},{16,18},{18,... | collective-permute-start | bytes 2408456 | tf_op jit(solution)/shard_map/ppermute | solution.py:107
  67.0 3.1 %collective-permute-start.6 = (bf16[224,1792]{1,0:T(8,128)(2,1)S(1)}, bf16[224,1792]{1,0:T(8,128)(2,1)S(1)}, u32[]{:S(2)}, u32[]{:S(2)}) collective-permute-start(bf16[224,1792]{1,0:T(8,128)(2,1)S(1)} %select_convert_fusion.1), channel_id=1, source_target_pairs={{0,2},{2,0},{4,6},{6,4},{8,10},{10,8},{12,14},{14,12},{1,3},{3,1},... | collective-permute-start | bytes 2408456 | tf_op jit(solution)/shard_map/ppermute | solution.py:107
  69.4 11.4 %collective-permute-start.9 = (bf16[112,1792]{1,0:T(8,128)(2,1)S(1)}, bf16[112,1792]{1,0:T(8,128)(2,1)S(1)}, u32[]{:S(2)}, u32[]{:S(2)}) collective-permute-start(bf16[112,1792]{1,0:T(8,128)(2,1)S(1)} %select_convert_fusion.5), channel_id=1, source_target_pairs={{0,4},{2,6},{4,0},{6,2},{8,12},{10,14},{12,8},{14,10},{16,20},{18,... | collective-permute-start | bytes 1204232 | tf_op jit(solution)/shard_map/ppermute | solution.py:107
  70.3 12.3 %collective-permute-start.8 = (bf16[112,1792]{1,0:T(8,128)(2,1)S(1)}, bf16[112,1792]{1,0:T(8,128)(2,1)S(1)}, u32[]{:S(2)}, u32[]{:S(2)}) collective-permute-start(bf16[112,1792]{1,0:T(8,128)(2,1)S(1)} %select_convert_fusion.4), channel_id=1, source_target_pairs={{0,8},{2,10},{4,12},{6,14},{8,0},{10,2},{12,4},{14,6},{1,9},{3,11}... | collective-permute-start | bytes 1204232 | tf_op jit(solution)/shard_map/ppermute | solution.py:107
  80.9 6.3 %collective-permute-start.11 = (bf16[112,896]{1,0:T(8,128)(2,1)S(1)}, bf16[112,896]{1,0:T(8,128)(2,1)S(1)}, u32[]{:S(2)}, u32[]{:S(2)}) collective-permute-start(bf16[112,896]{1,0:T(8,128)(2,1)S(1)} %select_convert_fusion.6), channel_id=1, source_target_pairs={{0,8},{2,10},{4,12},{6,14},{8,0},{10,2},{12,4},{14,6},{16,24},{18,... | collective-permute-start | bytes 602120 | tf_op jit(solution)/shard_map/ppermute | solution.py:107
  82.7 4.7 %collective-permute-start.10 = (bf16[112,1792]{1,0:T(8,128)(2,1)S(1)}, bf16[112,1792]{1,0:T(8,128)(2,1)S(1)}, u32[]{:S(2)}, u32[]{:S(2)}) collective-permute-start(bf16[112,1792]{1,0:T(8,128)(2,1)S(1)} %get-tuple-element.136), channel_id=1, source_target_pairs={{0,4},{2,6},{4,0},{6,2},{8,12},{10,14},{12,8},{14,10},{1,5},{3,7},... | collective-permute-start | bytes 1204232 | tf_op jit(solution)/shard_map/ppermute | solution.py:107
  87.3 7.5 %collective-permute-start.13 = (bf16[112,896]{1,0:T(8,128)(2,1)S(1)}, bf16[112,896]{1,0:T(8,128)(2,1)S(1)}, u32[]{:S(2)}, u32[]{:S(2)}) collective-permute-start(bf16[112,896]{1,0:T(8,128)(2,1)S(1)} %get-tuple-element.134), channel_id=1, source_target_pairs={{0,16},{2,18},{4,20},{6,22},{8,24},{10,26},{12,28},{14,30},{16,0},... | collective-permute-start | bytes 602120 | tf_op jit(solution)/shard_map/ppermute | solution.py:107
  95.8 9.4 %collective-permute-start.14 = (bf16[112,896]{1,0:T(8,128)(2,1)S(1)}, bf16[112,896]{1,0:T(8,128)(2,1)S(1)}, u32[]{:S(2)}, u32[]{:S(2)}) collective-permute-start(bf16[112,896]{1,0:T(8,128)(2,1)S(1)} %fusion.37), channel_id=1, source_target_pairs={{0,8},{2,10},{4,12},{6,14},{8,0},{10,2},{12,4},{14,6},{16,24},{18,... | collective-permute-start | bytes 602120 | tf_op jit(solution)/shard_map/ppermute | solution.py:107
  100.4 5.5 %collective-permute-start.12 = (bf16[112,1792]{1,0:T(8,128)(2,1)S(1)}, bf16[112,1792]{1,0:T(8,128)(2,1)S(1)}, u32[]{:S(2)}, u32[]{:S(2)}) collective-permute-start(bf16[112,1792]{1,0:T(8,128)(2,1)S(1)} %fusion.30), channel_id=1, source_target_pairs={{0,8},{2,10},{4,12},{6,14},{8,0},{10,2},{12,4},{14,6},{1,9},{3,11}... | collective-permute-start | bytes 1204232 | tf_op jit(solution)/shard_map/ppermute | solution.py:107
  105.3 10.3 %collective-permute-start.16 = (bf16[112,1792]{1,0:T(8,128)(2,1)S(1)}, bf16[112,1792]{1,0:T(8,128)(2,1)S(1)}, u32[]{:S(2)}, u32[]{:S(2)}) collective-permute-start(bf16[112,1792]{1,0:T(8,128)(2,1)S(1)} %pad_maximum_fusion.7), channel_id=1, source_target_pairs={{0,4},{2,6},{4,0},{6,2},{8,12},{10,14},{12,8},{14,10},{16,20},{18,... | collective-permute-start | bytes 1204232 | tf_op jit(solution)/shard_map/ppermute | solution.py:107
  106.0 9.8 %collective-permute-start.15 = (bf16[224,1792]{1,0:T(8,128)(2,1)S(1)}, bf16[224,1792]{1,0:T(8,128)(2,1)S(1)}, u32[]{:S(2)}, u32[]{:S(2)}) collective-permute-start(bf16[224,1792]{1,0:T(8,128)(2,1)S(1)} %pad_maximum_fusion.5), channel_id=1, source_target_pairs={{0,2},{2,0},{4,6},{6,4},{8,10},{10,8},{12,14},{14,12},{1,3},{3,1},... | collective-permute-start | bytes 2408456 | tf_op jit(solution)/shard_map/ppermute | solution.py:107
  115.7 2.4 %collective-permute-start.17 = (bf16[224,1792]{1,0:T(8,128)(2,1)S(1)}, bf16[224,1792]{1,0:T(8,128)(2,1)S(1)}, u32[]{:S(2)}, u32[]{:S(2)}) collective-permute-start(bf16[224,1792]{1,0:T(8,128)(2,1)S(1)} %pad_maximum_fusion.6), channel_id=1, source_target_pairs={{0,2},{2,0},{4,6},{6,4},{8,10},{10,8},{12,14},{14,12},{16,18},{18,... | collective-permute-start | bytes 2408456 | tf_op jit(solution)/shard_map/ppermute | solution.py:107
  118.1 2.2 %slice-start.8 = ((s8[7340032]{0:T(1024)(128)(4,1)}), s8[4194304]{0:T(1024)(128)(4,1)S(1)}, s32[]{:S(2)}) async-start(s8[7340032]{0:T(1024)(128)(4,1)} %bitcast.27), calls=%async_computation.8 | async-start | bytes 8388608
  118.3 3.5 %slice-start.9 = ((s8[7340032]{0:T(1024)(128)(4,1)}), s8[3145728]{0:T(1024)(128)(4,1)S(1)}, s32[]{:S(2)}) async-start(s8[7340032]{0:T(1024)(128)(4,1)} %bitcast.27), calls=%async_computation.9 | async-start | bytes 6291456
  120.0 13.0 %copy-start.4 = (bf16[448,1792]{1,0:T(8,128)(2,1)}, bf16[448,1792]{1,0:T(8,128)(2,1)S(1)}, u32[]{:S(2)}) copy-start(bf16[448,1792]{1,0:T(8,128)(2,1)S(1)} %get-tuple-element.100.refs_1_) | copy-start | bytes 4816900
  125.0 17.7 %collective-permute-start.19 = (bf16[224,1024]{1,0:T(8,128)(2,1)S(1)}, bf16[224,1024]{1,0:T(8,128)(2,1)S(1)}, u32[]{:S(2)}, u32[]{:S(2)}) collective-permute-start(bf16[224,1024]{1,0:T(8,128)(2,1)S(1)} %get-tuple-element.161), channel_id=1, source_target_pairs={{16,17},{17,16},{18,19},{19,18},{20,21},{21,20},{22,23},{23,22},{2... | collective-permute-start | bytes 1376264 | tf_op jit(solution)/shard_map/ppermute | solution.py:286
  128.4 21.6 %collective-permute-start.21 = (bf16[224,1024]{1,0:T(8,128)(2,1)S(1)}, bf16[224,1024]{1,0:T(8,128)(2,1)S(1)}, u32[]{:S(2)}, u32[]{:S(2)}) collective-permute-start(bf16[224,1024]{1,0:T(8,128)(2,1)S(1)} %fusion.20), channel_id=1, source_target_pairs={{0,1},{1,0},{2,3},{3,2},{4,5},{5,4},{6,7},{7,6},{8,9},{9,8},{10,11... | collective-permute-start | bytes 1376264 | tf_op jit(solution)/shard_map/ppermute | solution.py:102
  129.0 46.3 %collective-permute-start.18 = (bf16[224,1024]{1,0:T(8,128)(2,1)}, bf16[224,1024]{1,0:T(8,128)(2,1)}, u32[]{:S(2)}, u32[]{:S(2)}) collective-permute-start(bf16[224,1024]{1,0:T(8,128)(2,1)} %fusion.26), channel_id=1, source_target_pairs={{0,1},{1,0},{2,3},{3,2},{4,5},{5,4},{6,7},{7,6},{8,9},{9,8},{10,11... | collective-permute-start | bytes 1376264 | tf_op jit(solution)/shard_map/ppermute | solution.py:102
  131.7 3.5 %copy-start.8 = (bf16[1024,1792]{1,0:T(8,128)(2,1)S(1)}, bf16[1024,1792]{1,0:T(8,128)(2,1)}, u32[]{:S(2)}) copy-start(bf16[1024,1792]{1,0:T(8,128)(2,1)} %refs_4_.4) | copy-start | bytes 11010052
  133.0 2.2 %copy-start.7 = (bf16[1024,1792]{1,0:T(8,128)(2,1)S(1)}, bf16[1024,1792]{1,0:T(8,128)(2,1)}, u32[]{:S(2)}) copy-start(bf16[1024,1792]{1,0:T(8,128)(2,1)} %refs_3_.4) | copy-start | bytes 11010052
  133.0 18.9 %slice-start.10 = ((s8[7340032]{0:T(1024)(128)(4,1)}), s8[3145728]{0:T(1024)(128)(4,1)S(1)}, s32[]{:S(2)}) async-start(s8[7340032]{0:T(1024)(128)(4,1)} %bitcast.29), calls=%async_computation.10 | async-start | bytes 6291456
  135.2 16.7 %slice-start.11 = ((s8[7340032]{0:T(1024)(128)(4,1)}), s8[4194304]{0:T(1024)(128)(4,1)S(1)}, s32[]{:S(2)}) async-start(s8[7340032]{0:T(1024)(128)(4,1)} %bitcast.29), calls=%async_computation.11 | async-start | bytes 8388608
  142.7 9.3 %copy-start.1 = (bf16[448,2048]{1,0:T(8,128)(2,1)S(1)}, bf16[448,2048]{1,0:T(8,128)(2,1)}, u32[]{:S(2)}) copy-start(bf16[448,2048]{1,0:T(8,128)(2,1)} %copy-done) | copy-start | bytes 5505028
  143.6 31.7 %collective-permute-start.20 = (bf16[224,1024]{1,0:T(8,128)(2,1)}, bf16[224,1024]{1,0:T(8,128)(2,1)}, u32[]{:S(2)}, u32[]{:S(2)}) collective-permute-start(bf16[224,1024]{1,0:T(8,128)(2,1)} %add_convert_fusion), channel_id=1, source_target_pairs={{16,0},{18,2},{20,4},{22,6},{24,8},{26,10},{28,12},{30,14},{17,1},... | collective-permute-start | bytes 1376264 | tf_op jit(solution)/shard_map/ppermute | solution.py:298
  150.1 30.7 %slice-start.2 = ((s8[7340032]{0:T(1024)(128)(4,1)}), s8[4194304]{0:T(1024)(128)(4,1)S(1)}, s32[]{:S(2)}) async-start(s8[7340032]{0:T(1024)(128)(4,1)} %bitcast.21), calls=%async_computation.2 | async-start | bytes 8388608
  150.1 30.7 %slice-start.4 = ((s8[7340032]{0:T(1024)(128)(4,1)}), s8[4194304]{0:T(1024)(128)(4,1)S(1)}, s32[]{:S(2)}) async-start(s8[7340032]{0:T(1024)(128)(4,1)} %bitcast.23), calls=%async_computation.4 | async-start | bytes 8388608
  150.1 30.7 %slice-start.6 = ((s8[7340032]{0:T(1024)(128)(4,1)}), s8[4194304]{0:T(1024)(128)(4,1)S(1)}, s32[]{:S(2)}) async-start(s8[7340032]{0:T(1024)(128)(4,1)} %bitcast.25), calls=%async_computation.6 | async-start | bytes 8388608
  150.3 30.5 %slice-start.3 = ((s8[7340032]{0:T(1024)(128)(4,1)}), s8[3145728]{0:T(1024)(128)(4,1)S(1)}, s32[]{:S(2)}) async-start(s8[7340032]{0:T(1024)(128)(4,1)} %bitcast.21), calls=%async_computation.3 | async-start | bytes 6291456
  150.3 30.5 %slice-start.5 = ((s8[7340032]{0:T(1024)(128)(4,1)}), s8[3145728]{0:T(1024)(128)(4,1)S(1)}, s32[]{:S(2)}) async-start(s8[7340032]{0:T(1024)(128)(4,1)} %bitcast.23), calls=%async_computation.5 | async-start | bytes 6291456
  150.3 30.5 %slice-start.7 = ((s8[7340032]{0:T(1024)(128)(4,1)}), s8[3145728]{0:T(1024)(128)(4,1)S(1)}, s32[]{:S(2)}) async-start(s8[7340032]{0:T(1024)(128)(4,1)} %bitcast.25), calls=%async_computation.7 | async-start | bytes 6291456
  150.3 29.4 %collective-permute-start.24 = (bf16[224,1024]{1,0:T(8,128)(2,1)S(1)}, bf16[224,1024]{1,0:T(8,128)(2,1)}, u32[]{:S(2)}, u32[]{:S(2)}) collective-permute-start(bf16[224,1024]{1,0:T(8,128)(2,1)S(1)} %get-tuple-element.119), channel_id=1, source_target_pairs={{0,1},{1,0},{2,3},{3,2},{4,5},{5,4},{6,7},{7,6},{8,9},{9,8},{10,11... | collective-permute-start | bytes 1376264 | tf_op jit(solution)/shard_map/ppermute | solution.py:102
  151.9 3.9 %copy-start.2 = (bf16[2048,1792]{1,0:T(8,128)(2,1)S(1)}, bf16[2048,1792]{1,0:T(8,128)(2,1)}, u32[]{:S(2)}) copy-start(bf16[2048,1792]{1,0:T(8,128)(2,1)} %refs_2_.5) | copy-start | bytes 22020100
  155.8 3.9 %copy-start.3 = (bf16[2048,1792]{1,0:T(8,128)(2,1)S(1)}, bf16[2048,1792]{1,0:T(8,128)(2,1)}, u32[]{:S(2)}) copy-start(bf16[2048,1792]{1,0:T(8,128)(2,1)} %refs_3_.5) | copy-start | bytes 22020100
  159.7 2.2 %copy-start.5 = (bf16[448,1792]{1,0:T(8,128)(2,1)S(1)}, bf16[448,1792]{1,0:T(8,128)(2,1)}, u32[]{:S(2)}) copy-start(bf16[448,1792]{1,0:T(8,128)(2,1)} %copy-done.4) | copy-start | bytes 4816900
  175.3 2.4 %copy-start.10 = (bf16[224,1792]{1,0:T(8,128)(2,1)S(1)}, bf16[224,1792]{1,0:T(8,128)(2,1)}, u32[]{:S(2)}) copy-start(bf16[224,1792]{1,0:T(8,128)(2,1)} %copy-done.9) | copy-start | bytes 2408452
  175.3 2.4 %copy-start.12 = (bf16[224,1792]{1,0:T(8,128)(2,1)S(1)}, bf16[224,1792]{1,0:T(8,128)(2,1)}, u32[]{:S(2)}) copy-start(bf16[224,1792]{1,0:T(8,128)(2,1)} %copy-done.11) | copy-start | bytes 2408452
  177.4 12.1 %collective-permute-start.22 = (bf16[224,1024]{1,0:T(8,128)(2,1)S(1)}, bf16[224,1024]{1,0:T(8,128)(2,1)S(1)}, u32[]{:S(2)}, u32[]{:S(2)}) collective-permute-start(bf16[224,1024]{1,0:T(8,128)(2,1)S(1)} %get-tuple-element.124), channel_id=1, source_target_pairs={{0,1},{1,0},{2,3},{3,2},{4,5},{5,4},{6,7},{7,6},{8,9},{9,8},{10,11... | collective-permute-start | bytes 1376264 | tf_op jit(solution)/shard_map/ppermute | solution.py:102
  177.8 11.6 %collective-permute-start.23 = (f32[2048]{0:T(1024)S(1)}, f32[2048]{0:T(1024)S(1)}, u32[]{:S(2)}, u32[]{:S(2)}) collective-permute-start(f32[2048]{0:T(1024)S(1)} %pad_maximum_fusion.8), channel_id=1, source_target_pairs={{0,1},{1,0},{2,3},{3,2},{4,5},{5,4},{6,7},{7,6},{8,9},{9,8},{10,11... | collective-permute-start | bytes 24584 | tf_op jit(solution)/shard_map/ppermute | solution.py:102
  189.6 8.6 %copy-start.14 = (bf16[2048]{0:T(1024)(128)(2,1)S(1)}, bf16[2048]{0:T(1024)(128)(2,1)}, u32[]{:S(2)}) copy-start(bf16[2048]{0:T(1024)(128)(2,1)} %param.23) | copy-start | bytes 12292
  189.6 8.6 %copy-start.15 = (bf16[2048]{0:T(1024)(128)(2,1)S(1)}, bf16[2048]{0:T(1024)(128)(2,1)}, u32[]{:S(2)}) copy-start(bf16[2048]{0:T(1024)(128)(2,1)} %param.22) | copy-start | bytes 12292
